TPU v7x, 32 devices: a whole 2x2x4 slice. The times are simulated.
32 devices in a mesh: row: 2 (over core), col: 16 (over z, y, x).
Axes of the slice: x: 2, y: 2, z: 4, core: 2. Of those that a mesh axis runs over, the one named last changes fastest.
Arguments:
- tokens: bfloat16 [256, 6144], P('row', 'col'), may hold values from -6 to 6
- gate_weight: bfloat16 [6144, 24576], P('row', 'col'), may hold values from -0.15625 to 0.15625
- up_weight: bfloat16 [6144, 24576], P('row', 'col'), may hold values from -0.15625 to 0.15625
- block_mask: int32 [48, 192], P(None, 'col'), may hold values from 0 to 1, as said below
- cotangent: bfloat16 [256, 24576], P('row', 'col'), may hold values from -6 to 6
Outputs:
- hidden: bfloat16 [256, 24576], P('row', 'col')
- input_grad: bfloat16 [256, 6144], P('row', 'col')
- gate_grad: float32 [6144, 24576], P('row', 'col')
- up_grad: float32 [6144, 24576], P('row', 'col')
Inputs may be any that keep to these rules, and one draw needn't show every extreme that they name: `block_mask`: in every block column, each run of 24 block rows that starts at a multiple of 24 holds exactly 12 ones, the others zero.
All inputs are finite; a program needn't handle non-finite values.
Results may differ from a plain program's by a relative error of at most 0.0085.
Values may be sent and summed in bfloat16 or wider, within the bound.
No kernel may reach another device: no remote copies, remote signals or barrier semaphores. Data moves between devices by JAX's collectives and lax.ppermute only.
A program may use at most 192 MiB of HBM per device.

v0:
```python
import jax
import jax.numpy as jnp
from jax import lax
from jax.sharding import PartitionSpec as P

BLOCK = 128


def expand_mask(small_mask):
    return jnp.repeat(jnp.repeat(small_mask, BLOCK, axis=0), BLOCK, axis=1)


def body(tokens, gate_weight, up_weight, block_mask, cotangent):
    row_groups = lax.axis_size("row")
    row_index = lax.axis_index("row")
    seg_rows = gate_weight.shape[0]
    seg_blocks = seg_rows // BLOCK
    out_columns = gate_weight.shape[1]
    column_blocks = out_columns // BLOCK
    gathered = lax.all_gather(tokens, "col", axis=1, tiled=True)
    mask_groups = block_mask.reshape(row_groups, seg_blocks, column_blocks)
    own_mask = lax.dynamic_index_in_dim(mask_groups, row_index, 0, keepdims=False)
    own_expanded = expand_mask(own_mask).astype(jnp.bfloat16)
    gate_panel, up_panel = (
        lax.all_gather(gate_weight * own_expanded, "row", axis=0, tiled=True),
        lax.all_gather(up_weight * own_expanded, "row", axis=0, tiled=True),
    )
    gate = jnp.dot(gathered, gate_panel, preferred_element_type=jnp.float32)
    up_values = jnp.dot(gathered, up_panel, preferred_element_type=jnp.float32)
    sigmoid_gate = jax.nn.sigmoid(gate)
    silu_gate = gate * sigmoid_gate
    hidden = (silu_gate * up_values).astype(jnp.bfloat16)
    cot_float = cotangent.astype(jnp.float32)
    grad_gate = (cot_float * up_values * sigmoid_gate * (1.0 + gate * (1.0 - sigmoid_gate))).astype(
        jnp.bfloat16
    )
    grad_up = (cot_float * silu_gate).astype(jnp.bfloat16)
    contract = (((1,), (1,)), ((), ()))
    transposed = lax.psum_scatter(
        lax.dot_general(gate_panel, grad_gate, contract, preferred_element_type=jnp.float32)
        + lax.dot_general(up_panel, grad_up, contract, preferred_element_type=jnp.float32),
        "col",
        scatter_dimension=0,
        tiled=True,
    )
    input_grad = transposed.T.astype(jnp.bfloat16)
    token_contract = (((0,), (0,)), ((), ()))
    gate_partial = lax.dot_general(
        gathered, grad_gate, token_contract, preferred_element_type=jnp.float32
    )
    up_partial = lax.dot_general(
        gathered, grad_up, token_contract, preferred_element_type=jnp.float32
    )
    gate_sums, up_sums = (
        lax.psum_scatter(
            gate_partial.astype(jnp.bfloat16), "row", scatter_dimension=0, tiled=True
        ).astype(jnp.float32),
        lax.psum_scatter(
            up_partial.astype(jnp.bfloat16), "row", scatter_dimension=0, tiled=True
        ).astype(jnp.float32),
    )
    mask_float = expand_mask(own_mask).astype(jnp.float32)
    gate_grad = gate_sums * mask_float
    up_grad = up_sums * mask_float
    return (hidden, input_grad, gate_grad, up_grad)


def solution(mesh):
    placed = (P("row", "col"), P("row", "col"), P("row", "col"), P(None, "col"), P("row", "col"))
    return jax.shard_map(
        body,
        mesh=mesh,
        in_specs=placed,
        out_specs=(P("row", "col"), P("row", "col"), P("row", "col"), P("row", "col")),
        check_vma=False,
    )
```

profile of v0, /device:TPU:0, one launch (start us, length us, event | category | flops | bytes accessed | tf_op | source)
XLA Modules:
  0.0 423.9 jit_solution(6684463173865597436)
XLA Ops:
  7.2 0.0 all-gather.6.cloned.1.call-start
  7.2 0.7 all-gather.6.cloned.1.call-update
  7.9 0.0 all-gather.4.cloned.1.call-start
  7.9 0.8 reshape.21
  8.8 0.1 broadcast_bitcast_fusion.1
  8.9 12.6 %copy.22 = bf16[3072,1536]{0,1:T(8,128)(2,1)} copy(bf16[3072,1536]{1,0:T(8,128)(2,1)} %param.6) | data formatting | bytes 18874368 | tf_op args[1]
  21.5 12.6 %copy.23 = bf16[3072,1536]{0,1:T(8,128)(2,1)} copy(bf16[3072,1536]{1,0:T(8,128)(2,1)} %param.7) | data formatting | bytes 18874368 | tf_op args[2]
  34.1 14.5 %bitcast_multiply_fusion.3 = (bf16[3072,1536]{0,1:T(8,128)(2,1)}, bf16[3072,1536]{0,1:T(8,128)(2,1)}) fusion(bf16[3072,1536]{0,1:T(8,128)(2,1)} %copy.22, bf16[3072,12]{0,1:T(8,128)(2,1)S(1)} %bitcast.51, bf16[3072,1536]{0,1:T(8,128)(2,1)} %copy.23), kind=kLoop, calls=%fused_computation.7 | loop fusion | flops 9437184 | bytes 37822464 | tf_op jit(solution)/shard_map/mul | solution.py:25
  48.6 0.0 copy-start.1
  48.6 0.0 all-gather.4.cloned.1.call-update
  48.6 0.0 all-gather.8.cloned.1.call-start
  48.7 0.7 all-gather.8.cloned.1.call-update
  49.4 0.0 reduce-scatter.4.cloned.1.call-start
  49.4 0.2 copy-done.1
  49.6 0.2 copy.24
  49.8 19.4 %all-gather.6.cloned.1.call-done = bf16[128,6144]{1,0:T(8,128)(2,1)} async-done(((bf16[128,384]{1,0:T(8,128)(2,1)}), bf16[128,6144]{1,0:T(8,128)(2,1)}) %all-gather.6.cloned.1.call-update) | async-done | bytes 1572880 | tf_op jit(solution)/shard_map/all_gather | solution.py:20
  69.2 0.0 copy-start
  69.2 34.8 %all-gather.4.cloned.1.call-done = bf16[6144,1536]{0,1:T(8,128)(2,1)} async-done(((bf16[3072,1536]{0,1:T(8,128)(2,1)}), bf16[6144,1536]{0,1:T(8,128)(2,1)}) %all-gather.4.cloned.1.call-update) | async-done | bytes 18874384 | tf_op jit(solution)/shard_map/all_gather | solution.py:25
  104.1 9.4 %convolution_bitcast_fusion.1 = f32[128,1536]{0,1:T(8,128)S(1)} fusion(bf16[6144,1536]{0,1:T(8,128)(2,1)} %all-gather.4.cloned.1.call-done, bf16[128,6144]{1,0:T(8,128)(2,1)} %all-gather.6.cloned.1.call-done), kind=kOutput, calls=%fused_computation.10 | convolution fusion | flops 2415919104 | bytes 21233664 | tf_op jit(solution)/shard_map/dot_general | solution.py:28
  113.5 27.7 %all-gather.8.cloned.1.call-done = bf16[6144,1536]{0,1:T(8,128)(2,1)} async-done(((bf16[3072,1536]{0,1:T(8,128)(2,1)}), bf16[6144,1536]{0,1:T(8,128)(2,1)}) %all-gather.8.cloned.1.call-update) | async-done | bytes 18874384 | tf_op jit(solution)/shard_map/all_gather | solution.py:26
  141.2 0.0 copy-done
  141.2 9.6 %fusion.4 = (bf16[128,1536]{0,1:T(8,128)(2,1)S(1)}, bf16[128,1536]{0,1:T(8,128)(2,1)S(1)}) fusion(bf16[128,1536]{0,1:T(8,128)(2,1)S(1)} %copy.24, f32[128,1536]{0,1:T(8,128)S(1)} %convolution_bitcast_fusion.1, bf16[6144,1536]{0,1:T(8,128)(2,1)} %all-gather.8.cloned.1.call-done, bf16[128,6144]{1,0:T(8,128)(2,1)S(1)} %copy-done), kind=kOutput, calls=%fused_computation.15 | convolution fusion | flops 2418671616 | bytes 22413312 | tf_op jit(solution)/shard_map/dot_general | solution.py:29
  150.8 0.0 slice-start.3
  150.8 0.0 slice-start.4
  150.8 9.4 %fusion.9 = f32[6144,128]{1,0:T(8,128)S(1)} fusion(bf16[6144,1536]{0,1:T(8,128)(2,1)} %all-gather.4.cloned.1.call-done, bf16[128,1536]{0,1:T(8,128)(2,1)S(1)} %get-tuple-element.16), kind=kOutput, calls=%fused_computation.27 | convolution fusion | flops 2415919104 | bytes 22413312 | tf_op jit(solution)/shard_map/dot_general | solution.py:40
  160.2 0.0 slice-done
  160.2 0.0 slice-done.1
  160.2 0.0 slice-done.2
  160.2 0.0 slice-done.3
  160.3 0.0 slice-done.4
  160.3 6.8 %convolution_add_fusion = f32[6144,128]{1,0:T(8,128)} fusion(f32[6144,128]{1,0:T(8,128)S(1)} %fusion.9, bf16[6144,1536]{0,1:T(8,128)(2,1)S(1)} %bitcast.47, bf16[128,1536]{0,1:T(8,128)(2,1)S(1)} %copy.24, f32[128,1536]{0,1:T(8,128)S(1)} %convolution_bitcast_fusion.1), kind=kOutput, calls=%fused_computation.8 | convolution fusion | flops 2418081792 | bytes 26345472 | tf_op jit(solution)/shard_map/dot_general | solution.py:41
  167.1 0.0 reduce-scatter.4.cloned.1.call-update
  167.1 0.0 reduce-scatter.8.cloned.1.call-start
  167.1 9.5 %fusion.1 = bf16[6144,1536]{0,1:T(8,128)(2,1)} fusion(bf16[128,6144]{1,0:T(8,128)(2,1)S(1)} %copy-done, bf16[128,1536]{0,1:T(8,128)(2,1)S(1)} %copy.24, f32[128,1536]{0,1:T(8,128)S(1)} %convolution_bitcast_fusion.1), kind=kOutput, calls=%fused_computation.5 | convolution fusion | flops 2426732544 | bytes 21626880 | tf_op jit(solution)/shard_map/dot_general | solution.py:51
  176.6 0.0 reduce-scatter.8.cloned.1.call-update
  176.7 0.0 reduce-scatter.6.cloned.1.call-start
  176.7 9.7 %fusion = bf16[6144,1536]{0,1:T(8,128)(2,1)} fusion(bf16[128,1536]{0,1:T(8,128)(2,1)S(1)} %get-tuple-element.16, bf16[128,6144]{1,0:T(8,128)(2,1)S(1)} %copy-done), kind=kOutput, calls=%fused_computation.4 | convolution fusion | flops 2425356288 | bytes 20840448 | tf_op jit(solution)/shard_map/dot_general | solution.py:48
  186.4 0.0 reduce-scatter.6.cloned.1.call-update
  186.4 0.1 broadcast_bitcast_fusion
  186.6 0.9 copy.25
  187.5 111.3 %reduce-scatter.4.cloned.1.call-done = f32[384,128]{1,0:T(8,128)} async-done(((f32[6144,128]{1,0:T(8,128)}), f32[384,128]{1,0:T(8,128)}) %reduce-scatter.4.cloned.1.call-update) | async-done | bytes 196624 | tf_op jit(solution)/shard_map/reduce_scatter | solution.py:39
  298.9 0.9 convert_bitcast_fusion
  299.8 0.8 copy.26
  300.6 28.6 %reduce-scatter.8.cloned.1.call-done = bf16[3072,1536]{0,1:T(8,128)(2,1)} async-done(((bf16[6144,1536]{0,1:T(8,128)(2,1)}), bf16[3072,1536]{0,1:T(8,128)(2,1)}) %reduce-scatter.8.cloned.1.call-update) | async-done | bytes 9437200 | tf_op jit(solution)/shard_map/reduce_scatter | solution.py:58
  329.1 32.3 %reduce-scatter.6.cloned.1.call-done = bf16[3072,1536]{0,1:T(8,128)(2,1)} async-done(((bf16[6144,1536]{0,1:T(8,128)(2,1)}), bf16[3072,1536]{0,1:T(8,128)(2,1)}) %reduce-scatter.6.cloned.1.call-update) | async-done | bytes 9437200 | tf_op jit(solution)/shard_map/reduce_scatter | solution.py:55
  361.4 18.3 %bitcast_multiply_fusion = (f32[3072,1536]{0,1:T(8,128)}, f32[3072,1536]{0,1:T(8,128)}) fusion(bf16[3072,1536]{0,1:T(8,128)(2,1)} %reduce-scatter.8.cloned.1.call-done, f32[3072,12]{0,1:T(8,128)S(1)} %bitcast.49, bf16[3072,1536]{0,1:T(8,128)(2,1)} %reduce-scatter.6.cloned.1.call-done), kind=kLoop, calls=%fused_computation | loop fusion | flops 18874368 | bytes 56770560 | tf_op jit(solution)/shard_map/mul | solution.py:64
  379.7 18.6 %copy.28 = f32[3072,1536]{1,0:T(8,128)} copy(f32[3072,1536]{0,1:T(8,128)} %get-tuple-element.18) | data formatting | bytes 37748736
  398.4 18.6 %copy.27 = f32[3072,1536]{1,0:T(8,128)} copy(f32[3072,1536]{0,1:T(8,128)} %get-tuple-element.19) | data formatting | bytes 37748736
  (11 shorter events, 0.1 us)
Async XLA Ops:
  7.2 62.1 %all-gather.6.cloned.1.call-start = ((), (), s32[]{:S(2)}) async-start(), calls=%async_computation.4 | async-start | bytes 1671168 | tf_op jit(solution)/shard_map/all_gather | solution.py:20
  7.9 96.2 %all-gather.4.cloned.1.call-start = ((), (), s32[]{:S(2)}) async-start(), calls=%async_computation.3 | async-start | bytes 28311552 | tf_op jit(solution)/shard_map/all_gather | solution.py:25
  48.6 1.0 copy-start.1
  48.6 92.6 %all-gather.8.cloned.1.call-start = ((), (), s32[]{:S(2)}) async-start(), calls=%async_computation.5 | async-start | bytes 28311552 | tf_op jit(solution)/shard_map/all_gather | solution.py:26
  49.4 249.5 %reduce-scatter.4.cloned.1.call-start = ((), (), s32[]{:S(2)}) async-start(), calls=%async_computation.6 | async-start | bytes 3342336 | tf_op jit(solution)/shard_map/reduce_scatter | solution.py:39
  69.2 72.0 %copy-start = (bf16[128,6144]{1,0:T(8,128)(2,1)S(1)}, bf16[128,6144]{1,0:T(8,128)(2,1)}, u32[]{:S(2)}) copy-start(bf16[128,6144]{1,0:T(8,128)(2,1)} %all-gather.6.cloned.1.call-done) | copy-start | bytes 4718596
  141.2 19.0 %slice-start = ((s8[18874368]{0:T(1024)(128)(4,1)}), s8[4194304]{0:T(1024)(128)(4,1)S(1)}, s32[]{:S(2)}) async-start(s8[18874368]{0:T(1024)(128)(4,1)} %bitcast.46), calls=%async_computation.9 | async-start | bytes 8388608
  141.2 19.0 %slice-start.1 = ((s8[18874368]{0:T(1024)(128)(4,1)}), s8[4194304]{0:T(1024)(128)(4,1)S(1)}, s32[]{:S(2)}) async-start(s8[18874368]{0:T(1024)(128)(4,1)} %bitcast.46), calls=%async_computation.10 | async-start | bytes 8388608
  141.2 19.0 %slice-start.2 = ((s8[18874368]{0:T(1024)(128)(4,1)}), s8[4194304]{0:T(1024)(128)(4,1)S(1)}, s32[]{:S(2)}) async-start(s8[18874368]{0:T(1024)(128)(4,1)} %bitcast.46), calls=%async_computation.11 | async-start | bytes 8388608
  150.8 9.4 %slice-start.3 = ((s8[18874368]{0:T(1024)(128)(4,1)}), s8[4194304]{0:T(1024)(128)(4,1)S(1)}, s32[]{:S(2)}) async-start(s8[18874368]{0:T(1024)(128)(4,1)} %bitcast.46), calls=%async_computation.12 | async-start | bytes 8388608
  150.8 9.4 %slice-start.4 = ((s8[18874368]{0:T(1024)(128)(4,1)}), s8[2097152]{0:T(1024)(128)(4,1)S(1)}, s32[]{:S(2)}) async-start(s8[18874368]{0:T(1024)(128)(4,1)} %bitcast.46), calls=%async_computation.13 | async-start | bytes 4194304
  167.1 162.0 %reduce-scatter.8.cloned.1.call-start = ((), (), s32[]{:S(2)}) async-start(), calls=%async_computation.8 | async-start | bytes 28311552 | tf_op jit(solution)/shard_map/reduce_scatter | solution.py:58
  176.7 184.8 %reduce-scatter.6.cloned.1.call-start = ((), (), s32[]{:S(2)}) async-start(), calls=%async_computation.7 | async-start | bytes 28311552 | tf_op jit(solution)/shard_map/reduce_scatter | solution.py:55
Sparse Core Ops, SparseCore 0:
  10.7 58.4 all-gather.5
  71.4 32.6 all-gather.3
  106.2 34.9 all-gather.7
  167.2 131.5 reduce-scatter.3
  301.6 27.4 reduce-scatter.7
  331.8 29.5 reduce-scatter.5
where the time goes:
time: 425 us; the launch traced here: 424 us
  waiting for transfers between devices  256 us (60%)
  local copies, waits for them, and re-layouts  65.7 us (15%)
  matrix products  54.4 us (13%)
  other arithmetic  33.7 us (8%)
  between operations  14.3 us (3%)
    reduce_scatter x1, waiting for transfers between devices, body(): lax.psum_scatter(lax.dot_general(gate_panel, grad_gate, contract, preferr...  111 us
    unnamed x29, local copies, waits for them, and re-layouts  64.9 us
    all_gather x1, waiting for transfers between devices, body(): lax.all_gather(gate_weight * own_expanded, 'row', axis=0, tiled=True)  34.8 us
    reduce_scatter x1, waiting for transfers between devices, body(): lax.psum_scatter(gate_partial.astype(jnp.bfloat16), 'row', scatter_dimens...  32.3 us
    reduce_scatter x1, waiting for transfers between devices, body(): lax.psum_scatter(up_partial.astype(jnp.bfloat16), 'row', scatter_dimensio...  28.6 us
    all_gather x1, waiting for transfers between devices, body(): lax.all_gather(up_weight * own_expanded, 'row', axis=0, tiled=True)  27.7 us
    all_gather x1, waiting for transfers between devices, body(): gathered = lax.all_gather(tokens, 'col', axis=1, tiled=True)  19.4 us
    mul x1, other arithmetic, body(): up_grad = up_sums * mask_float  18.3 us
  transfers between devices with their start and end apart: 6, of which 6 were waited for; matrix products, arithmetic and copies ran while one was open for 17% of the time, Pallas kernels for 0%

commit v1 on v0

--- a/solution.py
+++ b/solution.py
@@ -1,16 +1,25 @@
+import functools
+
 import jax
 import jax.numpy as jnp
 from jax import lax
+from jax.experimental import pallas as pl
+from jax.experimental.pallas import tpu as pltpu
 from jax.sharding import PartitionSpec as P
 
 BLOCK = 128
+MIB = 1 << 20
+AXES = ("row", "col")
+ROWS, COLS = 2, 16
+F32, BF16 = jnp.float32, jnp.bfloat16
+VMEM, SMEM = pltpu.VMEM, pltpu.SMEM
 
 
 def expand_mask(small_mask):
     return jnp.repeat(jnp.repeat(small_mask, BLOCK, axis=0), BLOCK, axis=1)
 
 
-def body(tokens, gate_weight, up_weight, block_mask, cotangent):
+def general_body(tokens, gate_weight, up_weight, block_mask, cotangent):
     row_groups = lax.axis_size("row")
     row_index = lax.axis_index("row")
     seg_rows = gate_weight.shape[0]
@@ -65,10 +74,366 @@
     return (hidden, input_grad, gate_grad, up_grad)
 
 
+def place(row, z, y, x):
+    return row * COLS + z * 4 + y * 2 + x
+
+
+def z_pairs(k1, k0):
+    return [
+        (place(k1 ^ (z >> 1), 2 * half + (k0 ^ (z & 1)), y, x), place(half, z, y, x))
+        for half in range(2)
+        for z in range(4)
+        for y in range(2)
+        for x in range(2)
+    ]
+
+
+def lane_pairs(first, second):
+    return [(r * COLS + c, r * COLS + (c ^ (first, second)[r])) for r in range(2) for c in range(COLS)]
+
+
+X, Y = 1, 2
+NEAR, FAR = lane_pairs(X, Y), lane_pairs(Y, X)
+SLACK = 4
+SMALL = pl.CostEstimate(flops=1, bytes_accessed=1, transcendentals=0)
+
+
+def coords():
+    row, col = lax.axis_index("row"), lax.axis_index("col")
+    return row, col // 4, (col // 2) % 2, col % 2
+
+
+def flip(bit, with_bit):
+    return bit + with_bit - 2 * bit * with_bit
+
+
+def block_of(q, dnear, dfar, k1, k0):
+    row, z, y, x = q
+    dy = dnear * row + dfar * (1 - row)
+    dx = dnear * (1 - row) + dfar * row
+    return flip(k0, z % 2) * 4 + flip(dy, y) * 2 + flip(dx, x), flip(k1, z // 2)
+
+
+def in_vmem(array):
+    return pltpu.with_memory_space_constraint(array, VMEM)
+
+
+def in_hbm(array):
+    return pltpu.with_memory_space_constraint(array, pltpu.HBM)
+
+
+def spec(space):
+    return pl.BlockSpec(memory_space=space)
+
+
+def spanning(index):
+    return pl.ds(pl.multiple_of(index * BLOCK, BLOCK), BLOCK)
+
+
+def kept_of(listed):
+    return listed.shape[1] // 2 - SLACK
+
+
+def list_kernel(mask, listed):
+    columns, half = listed.shape[0], listed.shape[1] // 2
+    segs = mask.shape[1] // ROWS
+    low = lax.axis_index("row") == 0
+    own = jnp.where(low, mask[:, :segs], mask[:, segs:])
+    before = lax.broadcasted_iota(jnp.int32, (segs, segs), 0) <= lax.broadcasted_iota(jnp.int32, (segs, segs), 1)
+    kept = jnp.dot(own.astype(F32), before.astype(F32), preferred_element_type=F32).astype(jnp.int32)
+    dropped = lax.broadcasted_iota(jnp.int32, (columns, segs), 1) + 1 - kept
+    lane = lax.broadcasted_iota(jnp.int32, (columns, 2 * half), 1)
+    out = jnp.zeros((columns, 2 * half), jnp.int32)
+    for counts, first in ((kept, 0), (dropped, half)):
+        for k in range(segs // 2):
+            place = jnp.sum((counts <= k).astype(jnp.int32), axis=1, keepdims=True)
+            out = jnp.where(lane == first + k, place, out)
+    listed[...] = out
+
+
+def places(mask_t, segs):
+    return pl.pallas_call(
+        list_kernel,
+        out_shape=VMEM((mask_t.shape[0], segs + 2 * SLACK), jnp.int32),
+        in_specs=[spec(VMEM)],
+        out_specs=spec(VMEM),
+        compiler_params=pltpu.CompilerParams(vmem_limit_bytes=4 * MIB),
+        cost_estimate=SMALL,
+        name="places",
+    )(mask_t)
+
+
+def pack_kernel(first, turning, listed, gate_w, up_w, *refs):
+    if turning:
+        earlier, _, packed, turned, sem = refs
+    else:
+        _, packed, sem = refs
+    columns, kept = packed.shape[0], kept_of(listed)
+
+    def column(j, _):
+        cols = spanning(first + j)
+        for k in range(kept):
+            rows = spanning(listed[first + j, k])
+            to = packed.at[j, k * BLOCK : (k + 1) * BLOCK]
+            pltpu.make_async_copy(gate_w.at[rows, cols], to.at[:, :BLOCK], sem).start()
+            pltpu.make_async_copy(up_w.at[rows, cols], to.at[:, BLOCK:], sem).start()
+        return 0
+
+    lax.fori_loop(0, columns, column, 0)
+    if turning:
+
+        def turn(j, _):
+            turned[j] = earlier[j].T
+            return 0
+
+        lax.fori_loop(0, earlier.shape[0], turn, 0)
+    pltpu.make_async_copy(packed, packed, sem).wait()
+
+
+def pack(first, columns, listed, gate_w, up_w, later_than, earlier=None):
+    turning = earlier is not None
+    outs = [VMEM((columns, kept_of(listed) * BLOCK, 2 * BLOCK), BF16)]
+    if turning:
+        outs.append(VMEM((earlier.shape[0], earlier.shape[2], earlier.shape[1]), BF16))
+    return pl.pallas_call(
+        functools.partial(pack_kernel, first, turning),
+        out_shape=outs,
+        in_specs=[spec(SMEM), spec(pltpu.HBM), spec(pltpu.HBM)] + [spec(VMEM)] * turning + [spec(pl.ANY)],
+        out_specs=[spec(VMEM)] * len(outs),
+        scratch_shapes=[pltpu.SemaphoreType.DMA],
+        compiler_params=pltpu.CompilerParams(vmem_limit_bytes=4 * MIB),
+        cost_estimate=SMALL,
+        name="pack",
+    )(listed, in_hbm(gate_w), in_hbm(up_w), *([in_vmem(earlier)] if turning else []), later_than)
+
+
+def forward_kernel(turn, listed, packed_a, packed_b, own, near, far, both, part, turned, tokens):
+    q = coords()
+    width = own.shape[1] // BLOCK
+    for ref, dnear, dfar in ((own, 0, 0), (near, 1, 0), (far, 0, 1), (both, 1, 1)):
+        for k0 in range(2):
+            chip, _ = block_of(q, dnear, dfar, turn, k0)
+            for s in range(width):
+                tokens[chip * width + s] = ref[k0 * BLOCK : (k0 + 1) * BLOCK, s * BLOCK : (s + 1) * BLOCK]
+    cut = packed_a.shape[0]
+    for j in range(part.shape[0]):
+        picked = jnp.concatenate([tokens[listed[j, k]] for k in range(kept_of(listed))], axis=1)
+        weights = packed_a[j] if j < cut else packed_b[j - cut]
+        part[j] = jnp.dot(picked, weights, preferred_element_type=F32)
+    for i in range(tokens.shape[0]):
+        turned[i] = tokens[i].T
+
+
+def forward(turn, listed, packed, parts):
+    columns = packed[0].shape[0] + packed[1].shape[0]
+    seg = parts[0].shape[1] // BLOCK * 8
+    return pl.pallas_call(
+        functools.partial(forward_kernel, turn),
+        out_shape=[VMEM((columns, BLOCK, 2 * BLOCK), F32), VMEM((seg, BLOCK, BLOCK), BF16)],
+        in_specs=[spec(SMEM)] + [spec(VMEM)] * 6,
+        out_specs=[spec(VMEM)] * 2,
+        scratch_shapes=[VMEM((seg, BLOCK, BLOCK), BF16)],
+        compiler_params=pltpu.CompilerParams(vmem_limit_bytes=8 * MIB),
+        cost_estimate=SMALL,
+        name="forward",
+    )(listed, *map(in_vmem, packed), *parts)
+
+
+def backward_kernel(
+    turn, listed, turned_a, packed_b, part, other, cot, other_cot, *rest
+):
+    if turn:
+        before, gate_in, up_in, hidden, grads, s00, s01, s10, s11, gate_out, up_out, acc, zeros, sem = rest
+    else:
+        hidden, grads, s00, s01, s10, s11, gate_out, up_out, acc, zeros, sem = rest
+    q = coords()
+    columns, kept = part.shape[0], kept_of(listed)
+    mine = flip(turn, q[1] // 2) == q[0]
+    acc[...] = jnp.zeros_like(acc)
+    zeros[...] = jnp.zeros_like(zeros)
+    cut = turned_a.shape[0]
+
+    def column(j, packed, at):
+        cols = spanning(j)
+        total = part[j] + other[j]
+        gate, up = total[:, :BLOCK], total[:, BLOCK:]
+        sig = 1.0 / (1.0 + jnp.exp(-gate))
+        silu = gate * sig
+        cotf = jnp.where(mine, cot[:, cols], other_cot[:, cols]).astype(F32)
+        shown = (silu * up).astype(BF16)
+        hidden[:, cols] = jnp.where(mine, shown, before[:, cols]) if turn else shown
+        grads[j, :, :BLOCK] = (cotf * up * sig * (1.0 + gate * (1.0 - sig))).astype(BF16)
+        grads[j, :, BLOCK:] = (cotf * silu).astype(BF16)
+        facing = (((1,), (0 if packed is turned_a else 1,)), ((), ()))
+        spread = lax.dot_general(grads[j], packed[at], facing, preferred_element_type=F32)
+        for k in range(kept):
+            acc[listed[j, k]] += spread[:, k * BLOCK : (k + 1) * BLOCK]
+
+    def clear(j):
+        for k in range(kept):
+            rows = spanning(listed[j, kept + SLACK + k])
+            pltpu.make_async_copy(zeros, gate_out.at[rows, spanning(j)], sem).start()
+            pltpu.make_async_copy(zeros, up_out.at[rows, spanning(j)], sem).start()
+
+    cleared = columns // 2
+    lax.fori_loop(0, cleared, lambda j, _: (clear(turn * cleared + j), 0)[1], 0)
+    step = 3
+    for packed, first, number in ((turned_a, 0, cut), (packed_b, cut, columns - cut)):
+
+        def steps(g, _, packed=packed, first=first):
+            for u in range(step):
+                column(first + g * step + u, packed, g * step + u)
+            return 0
+
+        lax.fori_loop(0, number // step, steps, 0)
+    width = s00.shape[1] // BLOCK
+    for ref, dnear, dfar in ((s11, 1, 1), (s01, 0, 1), (s10, 1, 0), (s00, 0, 0)):
+        for k0 in range(2):
+            chip, _ = block_of(q, dnear, dfar, turn, k0)
+            for s in range(width):
+                ref[k0 * BLOCK : (k0 + 1) * BLOCK, s * BLOCK : (s + 1) * BLOCK] = acc[chip * width + s].astype(BF16)
+    part_written = gate_out.at[:, pl.ds(0, cleared * BLOCK)]
+    pltpu.make_async_copy(part_written, part_written, sem).wait()
+
+
+def backward(turn, listed, packed, part, other, cot, other_cot, width, grad_shape, before=None):
+    columns = part.shape[0]
+    extra = [] if before is None else [before[0], in_hbm(before[1]), in_hbm(before[2])]
+    return pl.pallas_call(
+        functools.partial(backward_kernel, turn),
+        out_shape=[VMEM(cot.shape, BF16), VMEM((columns, BLOCK, 2 * BLOCK), BF16)]
+        + [VMEM((2 * BLOCK, width), BF16)] * 4
+        + [pltpu.HBM(grad_shape, F32)] * 2,
+        in_specs=[spec(SMEM)] + [spec(VMEM)] * 6 + ([spec(VMEM)] + [spec(pltpu.HBM)] * 2 if extra else []),
+        out_specs=[spec(VMEM)] * 6 + [spec(pltpu.HBM)] * 2,
+        scratch_shapes=[
+            VMEM((8 * width // BLOCK, BLOCK, BLOCK), F32),
+            VMEM((BLOCK, BLOCK), F32),
+            pltpu.SemaphoreType.DMA,
+        ],
+        input_output_aliases={8: 6, 9: 7} if extra else {},
+        compiler_params=pltpu.CompilerParams(vmem_limit_bytes=8 * MIB),
+        cost_estimate=SMALL,
+        name="backward",
+    )(listed, *map(in_vmem, packed), in_vmem(part), in_vmem(other), cot, other_cot, *extra)
+
+
+def weight_kernel(first, listed, toks0, toks1, grads0, grads1, gate_in, up_in, _, gate_out, up_out, token, stage, sem):
+    kept = kept_of(listed)
+    for slot in range(stage.shape[0]):
+        j = first + slot
+        picked = jnp.concatenate(
+            [jnp.concatenate([toks0[listed[j, k]], toks1[listed[j, k]]], axis=1) for k in range(kept)], axis=0
+        )
+        grads = jnp.concatenate([grads0[j], grads1[j]], axis=0)
+        stage[slot] = jnp.dot(picked, grads, preferred_element_type=F32)
+        for k in range(kept):
+            rows = spanning(listed[j, k])
+            here = stage.at[slot, k * BLOCK : (k + 1) * BLOCK]
+            pltpu.make_async_copy(here.at[:, :BLOCK], gate_out.at[rows, spanning(j)], sem).start()
+            pltpu.make_async_copy(here.at[:, BLOCK:], up_out.at[rows, spanning(j)], sem).start()
+    token[...] = jnp.zeros_like(token)
+    pltpu.make_async_copy(stage, stage, sem).wait()
+
+
+def weight_grads(first, count, listed, tokens, grads, written, later_than):
+    kept = kept_of(listed)
+    grad = pltpu.HBM(written[0].shape, F32)
+    return pl.pallas_call(
+        functools.partial(weight_kernel, first),
+        out_shape=[grad, grad, VMEM((8, BLOCK), F32)],
+        in_specs=[spec(SMEM)] + [spec(VMEM)] * 4 + [spec(pltpu.HBM)] * 2 + [spec(pl.ANY)],
+        out_specs=[spec(pltpu.HBM)] * 2 + [spec(VMEM)],
+        scratch_shapes=[VMEM((count, kept * BLOCK, 2 * BLOCK), F32), pltpu.SemaphoreType.DMA],
+        input_output_aliases={5: 0, 6: 1},
+        compiler_params=pltpu.CompilerParams(vmem_limit_bytes=12 * MIB),
+        cost_estimate=SMALL,
+        name="weight_grads",
+    )(listed, *map(in_vmem, tokens), *map(in_vmem, grads), in_hbm(written[0]), in_hbm(written[1]), later_than)
+
+
+def add_kernel(*refs):
+    out = refs[-1]
+    total = refs[0][...].astype(F32)
+    for ref in refs[1:-2]:
+        total += ref[...].astype(F32)
+    out[...] = total.astype(BF16)
+
+
+def add(*terms, later_than):
+    return pl.pallas_call(
+        add_kernel,
+        out_shape=VMEM(terms[0].shape, BF16),
+        in_specs=[spec(VMEM)] * len(terms) + [spec(pl.ANY)],
+        out_specs=spec(VMEM),
+        compiler_params=pltpu.CompilerParams(vmem_limit_bytes=4 * MIB),
+        cost_estimate=SMALL,
+        name="add",
+    )(*terms, later_than)
+
+
+def chip_body(tokens, gate_weight, up_weight, block_mask, cotangent):
+    swap = [(0, 1), (1, 0)]
+    width = tokens.shape[1]
+    columns, segs = gate_weight.shape[1] // BLOCK, gate_weight.shape[0] // BLOCK
+    cut = columns // 2
+    other_cot = lax.ppermute(cotangent, "row", swap)
+    listed = places(block_mask.T, segs)
+
+    def gathered(turn):
+        return jnp.concatenate([lax.ppermute(tokens, AXES, z_pairs(turn, k0)) for k0 in range(2)], axis=0)
+
+    owns = [gathered(0), gathered(1)]
+    nears = [lax.ppermute(own, AXES, NEAR) for own in owns]
+    fars = [lax.ppermute(own, AXES, FAR) for own in owns]
+    (pack_a,) = pack(0, cut, listed, gate_weight, up_weight, owns[1])
+    pack_b, turned_a = pack(cut, columns - cut, listed, gate_weight, up_weight, nears[1], pack_a)
+    boths = [lax.ppermute(near, AXES, FAR) for near in nears]
+    held = list(zip(owns, nears, fars, boths))
+
+    parts, toks = zip(*[forward(turn, listed, (pack_a, pack_b), held[turn]) for turn in range(2)])
+    others = [lax.ppermute(part, "row", swap) for part in parts]
+    done = []
+    for turn in range(2):
+        before = (done[0][0], done[0][6], done[0][7]) if turn else None
+        weights = (turned_a, pack_b)
+        done.append(
+            backward(
+                turn, listed, weights, parts[turn], others[turn], cotangent, other_cot, width, gate_weight.shape, before
+            )
+        )
+    grads = [out[1] for out in done]
+    hidden = done[1][0]
+
+    (a00, a01, a10, a11), (b00, b01, b10, b11) = done[0][2:6], done[1][2:6]
+    first_a, direct_a = lax.ppermute(a11, AXES, FAR), lax.ppermute(a01, AXES, FAR)
+    first_b, direct_b = lax.ppermute(b11, AXES, FAR), lax.ppermute(b01, AXES, FAR)
+    sum_a = add(a10, first_a, later_than=b10)
+    carried_a = lax.ppermute(sum_a, AXES, NEAR)
+    lead, middle = columns // 3, columns // 4
+    written = done[1][6:8]
+    *written, token = weight_grads(0, lead, listed, toks, grads, written, sum_a)
+    sum_b = add(b10, first_b, later_than=token)
+    carried_b = lax.ppermute(sum_b, AXES, NEAR)
+    here_a = add(a00, direct_a, carried_a, later_than=sum_b)
+    *written, token = weight_grads(lead, middle, listed, toks, grads, written, here_a)
+    here_b = add(b00, direct_b, carried_b, later_than=token)
+    total = jnp.zeros(tokens.shape, F32)
+    for turn, here in enumerate((here_a, here_b)):
+        for k0 in range(2):
+            back = [(b, a) for a, b in z_pairs(turn, k0)]
+            total += lax.ppermute(here[k0 * BLOCK : (k0 + 1) * BLOCK], AXES, back).astype(F32)
+    input_grad = total.astype(BF16)
+    last = lead + middle
+    *written, token = weight_grads(last, columns - last, listed, toks, grads, written, here_b)
+    return hidden, input_grad, *written
+
+
 def solution(mesh):
+    fits = mesh.shape["row"] == ROWS and mesh.shape["col"] == COLS
     placed = (P("row", "col"), P("row", "col"), P("row", "col"), P(None, "col"), P("row", "col"))
     return jax.shard_map(
-        body,
+        chip_body if fits else general_body,
         mesh=mesh,
         in_specs=placed,
         out_specs=(P("row", "col"), P("row", "col"), P("row", "col"), P("row", "col")),

time: 425 us -> 83.9 us (0.20)
  waiting for transfers between devices: 256 us -> 16.8 us
  local copies, waits for them, and re-layouts: 65.7 us -> 1.55 us
  matrix products: 54.4 us -> 0 us
  other arithmetic: 33.7 us -> 0.69 us
  Pallas kernels: 0 us -> 32.3 us
  starting transfers between devices: 0.24 us -> 31.4 us
  between operations: 14.3 us -> 0.84 us
    reduce_scatter x3 -> x0, waiting for transfers between devices: 172 us -> none  [the longest x1 111 us: body(): lax.psum_scatter(lax.dot_general(gate_panel, grad_gate, contract, preferr...]
    all_gather x3 -> x0, waiting for transfers between devices: 81.9 us -> none  [the longest x1 34.8 us: body(): lax.all_gather(gate_weight * own_expanded, 'row', axis=0, tiled=True)]
    unnamed x29 -> x7, local copies, waits for them, and re-layouts: 64.9 us -> 1.47 us
    dot_general x6 -> x0, matrix products: 54.4 us -> none  [the longest x1 9.69 us: body(): lax.dot_general(gathered, grad_gate, token_contract, preferred_element_ty...]
    mul x2 -> x0, other arithmetic: 32.8 us -> none  [the longest x1 18.3 us: body(): up_grad = up_sums * mask_float]
    pallas_call x0 -> x14, Pallas kernels: none -> 32.3 us  [the longest x3 11.7 us: weight_grads(): pl.pallas_call(functools.partial(weight_kernel, first), out_shape=[grad,...]
    ppermute x0 -> x23, starting transfers between devices: none -> 31.4 us  [the longest x4 8.05 us: chip_body(): lax.ppermute(here[k0 * BLOCK:(k0 + 1) * BLOCK], AXES, back).astype(F32)]
    ppermute x0 -> x23, waiting for transfers between devices: none -> 16.8 us  [the longest x4 5.47 us: gathered(): lax.ppermute(tokens, AXES, z_pairs(turn, k0))]
  transfers between devices with their start and end apart: 6 -> 23, of which waited for: 6 -> 8; matrix products, arithmetic and copies ran while one was open for 17% -> 1% of each run, Pallas kernels for 0% -> 39%
where the time goes in v1:
time: 83.9 us; the launch traced here: 83.6 us
  Pallas kernels  32.3 us (38%)
  starting transfers between devices  31.4 us (37%)
  waiting for transfers between devices  16.8 us (20%)
  local copies, waits for them, and re-layouts  1.55 us (2%)
  between operations  0.84 us (1%)
    pallas_call x3, Pallas kernels, weight_grads(): pl.pallas_call(functools.partial(weight_kernel, first), out_shape=[grad,...  11.7 us
    pallas_call x2, Pallas kernels, backward(): pl.pallas_call(functools.partial(backward_kernel, turn), out_shape=[VMEM(...  8.81 us
    ppermute x4, starting transfers between devices, chip_body(): lax.ppermute(here[k0 * BLOCK:(k0 + 1) * BLOCK], AXES, back).astype(F32)  8.05 us
    ppermute x4, starting transfers between devices, gathered(): lax.ppermute(tokens, AXES, z_pairs(turn, k0))  7.68 us
    pallas_call x2, Pallas kernels, pack(): pl.pallas_call(functools.partial(pack_kernel, first, turning), out_shape=...  6.23 us
    ppermute x4, waiting for transfers between devices, gathered(): lax.ppermute(tokens, AXES, z_pairs(turn, k0))  5.47 us
    pallas_call x2, Pallas kernels, forward(): pl.pallas_call(functools.partial(forward_kernel, turn), out_shape=[VMEM((...  4.93 us
    ppermute x2, starting transfers between devices, chip_body(): boths = [lax.ppermute(near, AXES, FAR) for near in nears]  3.91 us
  transfers between devices with their start and end apart: 23, of which 8 were waited for; matrix products, arithmetic and copies ran while one was open for 1% of the time, Pallas kernels for 39%

profile of v1, /device:TPU:0, one launch (start us, length us, event | category | flops | bytes accessed | tf_op | source)
XLA Modules:
  0.0 83.6 jit_solution(5861009294555849436)
XLA Ops:
  0.6 1.6 %collective-permute-start.7 = (bf16[128,384]{1,0:T(8,128)(2,1)}, bf16[128,384]{1,0:T(8,128)(2,1)S(1)}, u32[]{:S(2)}, u32[]{:S(2)}) collective-permute-start(bf16[128,384]{1,0:T(8,128)(2,1)} %param.5), channel_id=1, source_target_pairs={{0,0},{1,1},{2,2},{3,3},{4,4},{5,5},{6,6},{7,7},{16,8},{17,9},{18,... | collective-permute-start | bytes 294920 | tf_op jit(solution)/shard_map/ppermute | solution.py:384
  2.2 5.5 %collective-permute-start.1 = (bf16[128,384]{1,0:T(8,128)(2,1)}, bf16[128,384]{1,0:T(8,128)(2,1)S(1)}, u32[]{:S(2)}, u32[]{:S(2)}) collective-permute-start(bf16[128,384]{1,0:T(8,128)(2,1)} %param.5), channel_id=1, source_target_pairs={{20,0},{21,1},{22,2},{23,3},{16,4},{17,5},{18,6},{19,7},{4,8},{5,9... | collective-permute-start | bytes 294920 | tf_op jit(solution)/shard_map/ppermute | solution.py:384
  7.7 0.6 collective-permute-start.8
  8.3 5.5 %collective-permute-done.8 = bf16[128,384]{1,0:T(8,128)(2,1)S(1)} collective-permute-done((bf16[128,384]{1,0:T(8,128)(2,1)}, bf16[128,384]{1,0:T(8,128)(2,1)S(1)}, u32[]{:S(2)}, u32[]{:S(2)}) %collective-permute-start.8) | collective-permute-done | bytes 98336 | tf_op jit(solution)/shard_map/ppermute | solution.py:384
  13.8 1.6 %collective-permute-start.9 = (bf16[256,384]{1,0:T(8,128)(2,1)S(1)}, bf16[256,384]{1,0:T(8,128)(2,1)S(1)}, u32[]{:S(2)}, u32[]{:S(2)}) collective-permute-start(bf16[256,384]{1,0:T(8,128)(2,1)S(1)} %constant_dynamic-update-slice_fusion.2.own), channel_id=1, source_target_pairs={{0,1},{1,0},{2,3},{3,2},{4,5},{5,4},{6,7},{7,6},{8,9},{9,8},{10,11... | collective-permute-start | bytes 589832 | tf_op jit(solution)/shard_map/ppermute | solution.py:387
  15.4 0.6 collective-permute-start.2
  16.0 1.5 %collective-permute-start.10 = (bf16[256,384]{1,0:T(8,128)(2,1)S(1)}, bf16[256,384]{1,0:T(8,128)(2,1)S(1)}, u32[]{:S(2)}, u32[]{:S(2)}) collective-permute-start(bf16[256,384]{1,0:T(8,128)(2,1)S(1)} %constant_dynamic-update-slice_fusion.2.own), channel_id=1, source_target_pairs={{0,2},{1,3},{2,0},{3,1},{4,6},{5,7},{6,4},{7,5},{8,10},{9,11},{10,... | collective-permute-start | bytes 589832 | tf_op jit(solution)/shard_map/ppermute | solution.py:388
  17.5 2.0 %collective-permute-done.9.near = bf16[256,384]{1,0:T(8,128)(2,1)S(1)} collective-permute-done((bf16[256,384]{1,0:T(8,128)(2,1)S(1)}, bf16[256,384]{1,0:T(8,128)(2,1)S(1)}, u32[]{:S(2)}, u32[]{:S(2)}) %collective-permute-start.9) | collective-permute-done | bytes 196640 | tf_op jit(solution)/shard_map/ppermute | solution.py:387
  19.5 1.5 %collective-permute-start.11 = (bf16[256,384]{1,0:T(8,128)(2,1)S(1)}, bf16[256,384]{1,0:T(8,128)(2,1)S(1)}, u32[]{:S(2)}, u32[]{:S(2)}) collective-permute-start(bf16[256,384]{1,0:T(8,128)(2,1)S(1)} %collective-permute-done.9.near), channel_id=1, source_target_pairs={{0,2},{1,3},{2,0},{3,1},{4,6},{5,7},{6,4},{7,5},{8,10},{9,11},{10,... | collective-permute-start | bytes 589832 | tf_op jit(solution)/shard_map/ppermute | solution.py:391
  21.1 0.7 copy-done.1
  21.8 0.4 places.1.listed
  22.1 0.6 collective-permute-start.3
  22.7 2.4 %collective-permute-start.4 = (bf16[256,384]{1,0:T(8,128)(2,1)S(1)}, bf16[256,384]{1,0:T(8,128)(2,1)S(1)}, u32[]{:S(2)}, u32[]{:S(2)}) collective-permute-start(bf16[256,384]{1,0:T(8,128)(2,1)S(1)} %collective-permute-done.2.refs_1_.near), channel_id=1, source_target_pairs={{0,2},{1,3},{2,0},{3,1},{4,6},{5,7},{6,4},{7,5},{8,10},{9,11},{10,... | collective-permute-start | bytes 589832 | tf_op jit(solution)/shard_map/ppermute | solution.py:391
  25.1 3.1 %pack.2.refs_0_.packed_a = bf16[6,1536,256]{2,1,0:T(8,128)(2,1)S(1)} custom-call(s32[12,32]{1,0:T(8,128)S(1)} %places.1.listed, bf16[3072,1536]{1,0:T(8,128)(2,1)} %gate_w.3, bf16[3072,1536]{1,0:T(8,128)(2,1)} %up_w.3, bf16[256,384]{1,0:T(8,128)(2,1)S(1)} %constant_dynamic-update-slice_fusion.refs_0_.own), custom_call_target="tpu_custom_call" | custom-call | flops 1 | bytes 1 | tf_op jit(solution)/shard_map/pack/pallas_call | solution.py:198
  28.2 0.0 copy-start
  28.2 3.1 %pack.3 = (bf16[6,1536,256]{2,1,0:T(8,128)(2,1)S(1)}, bf16[6,256,1536]{2,1,0:T(8,128)(2,1)S(1)}) custom-call(s32[12,32]{1,0:T(8,128)S(1)} %places.1.listed, bf16[3072,1536]{1,0:T(8,128)(2,1)} %gate_w.3, bf16[3072,1536]{1,0:T(8,128)(2,1)} %up_w.3, bf16[6,1536,256]{2,1,0:T(8,128)(2,1)S(1)} %pack.2.refs_0_.packed_a, ...), custom_call_target="tpu_custom_call" | custom-call | flops 1 | bytes 1 | tf_op jit(solution)/shard_map/pack/pallas_call | solution.py:198
  31.4 2.5 %forward.3 = (f32[12,128,256]{2,1,0:T(8,128)S(1)}, bf16[24,128,128]{2,1,0:T(8,128)(2,1)S(1)}) custom-call(s32[12,32]{1,0:T(8,128)S(1)} %places.1.listed, bf16[6,1536,256]{2,1,0:T(8,128)(2,1)S(1)} %pack.2.refs_0_.packed_a, bf16[6,1536,256]{2,1,0:T(8,128)(2,1)S(1)} %get-tuple-element.35.packed_b, bf16[256,384]{1,0:T(8,128)(2,1)S(1)} %constant_dynamic-update-slice_fusion.2.own, ...), custom_call_target="tpu_custom_call" | custom-call | flops 1 | bytes 1 | tf_op jit(solution)/shard_map/forward/pallas_call | solution.py:230
  33.9 1.1 %collective-permute-start.12 = (f32[12,128,256]{2,1,0:T(8,128)S(1)}, f32[12,128,256]{2,1,0:T(8,128)S(1)}, u32[]{:S(2)}, u32[]{:S(2)}) collective-permute-start(f32[12,128,256]{2,1,0:T(8,128)S(1)} %get-tuple-element.37.part), channel_id=1, source_target_pairs={{0,16},{16,0},{1,17},{17,1},{2,18},{18,2},{3,19},{19,3},{4,20},{20... | collective-permute-start | bytes 4718600 | tf_op jit(solution)/shard_map/ppermute | solution.py:395
  35.0 2.5 %forward.2 = (f32[12,128,256]{2,1,0:T(8,128)S(1)}, bf16[24,128,128]{2,1,0:T(8,128)(2,1)S(1)}) custom-call(s32[12,32]{1,0:T(8,128)S(1)} %places.1.listed, bf16[6,1536,256]{2,1,0:T(8,128)(2,1)S(1)} %pack.2.refs_0_.packed_a, bf16[6,1536,256]{2,1,0:T(8,128)(2,1)S(1)} %get-tuple-element.35.packed_b, ...), custom_call_target="tpu_custom_call" | custom-call | flops 1 | bytes 1 | tf_op jit(solution)/shard_map/forward/pallas_call | solution.py:230
  37.4 0.1 collective-permute-start.5
  37.5 0.5 collective-permute-start.6
  38.0 3.5 %collective-permute-done.6.other_cot = bf16[128,1536]{1,0:T(8,128)(2,1)S(1)} collective-permute-done((bf16[128,1536]{1,0:T(8,128)(2,1)S(1)}, bf16[128,1536]{1,0:T(8,128)(2,1)S(1)}, u32[]{:S(2)}, u32[]{:S(2)}) %collective-permute-start.6) | collective-permute-done | bytes 393248 | tf_op jit(solution)/shard_map/ppermute | solution.py:380
  41.5 4.4 %backward.2 = (bf16[128,1536]{1,0:T(8,128)(2,1)S(1)}, bf16[12,128,256]{2,1,0:T(8,128)(2,1)S(1)}, bf16[256,384]{1,0:T(8,128)(2,1)S(1)}, bf16[256,384]{1,0:T(8,128...) custom-call(s32[12,32]{1,0:T(8,128)S(1)} %places.1.listed, ...), custom_call_target="tpu_custom_call" | custom-call | flops 1 | bytes 1 | tf_op jit(solution)/shard_map/backward/pallas_call | solution.py:302
  45.8 1.6 %collective-permute-start.14 = (bf16[256,384]{1,0:T(8,128)(2,1)S(1)}, bf16[256,384]{1,0:T(8,128)(2,1)S(1)}, u32[]{:S(2)}, u32[]{:S(2)}) collective-permute-start(bf16[256,384]{1,0:T(8,128)(2,1)S(1)} %get-tuple-element.45), channel_id=1, source_target_pairs={{0,2},{1,3},{2,0},{3,1},{4,6},{5,7},{6,4},{7,5},{8,10},{9,11},{10,... | collective-permute-start | bytes 589832 | tf_op jit(solution)/shard_map/ppermute | solution.py:409
  47.4 4.4 %backward.3 = (bf16[128,1536]{1,0:T(8,128)(2,1)S(1)}, bf16[12,128,256]{2,1,0:T(8,128)(2,1)S(1)}, bf16[256,384]{1,0:T(8,128)(2,1)S(1)}, bf16[256,384]{1,0:T(8,128...) custom-call(s32[12,32]{1,0:T(8,128)S(1)} %places.1.listed, ...), custom_call_target="tpu_custom_call", output_to_operand_aliasing={{6}: (8, {}), {7}: (9, {})} | custom-call | flops 1 | bytes 1 | tf_op jit(solution)/shard_map/backward/pallas_call | solution.py:302
  51.9 0.6 collective-permute-start.16
  52.5 1.5 %collective-permute-start.13 = (bf16[256,384]{1,0:T(8,128)(2,1)S(1)}, bf16[256,384]{1,0:T(8,128)(2,1)S(1)}, u32[]{:S(2)}, u32[]{:S(2)}) collective-permute-start(bf16[256,384]{1,0:T(8,128)(2,1)S(1)} %get-tuple-element.43), channel_id=1, source_target_pairs={{0,2},{1,3},{2,0},{3,1},{4,6},{5,7},{6,4},{7,5},{8,10},{9,11},{10,... | collective-permute-start | bytes 589832 | tf_op jit(solution)/shard_map/ppermute | solution.py:409
  54.0 0.1 add.19._
  54.0 0.6 collective-permute-start.15
  54.6 0.6 collective-permute-start.19
  55.2 3.8 %weight_grads.3 = (f32[3072,1536]{1,0:T(8,128)}, f32[3072,1536]{1,0:T(8,128)}, f32[8,128]{1,0:T(8,128)S(1)}) custom-call(s32[12,32]{1,0:T(8,128)S(1)} %places.1.listed, bf16[24,128,128]{2,1,0:T(8,128)(2,1)S(1)} %get-tuple-element.48.toks0, bf16[24,128,128]{2,1,0:T(8,128)(2,1)S(1)} %get-tuple-element.49.toks1, ...), custom_call_target="tpu_custom_call", output_to_operand_aliasing={{0}: (5, {}), {1}: (6, {})} | custom-call | flops 1 | bytes 1 | tf_op jit(solution)/shard_map/weight_grads/pallas_call | solution.py:342
  59.0 0.5 collective-permute-done.16.refs_1_
  59.5 0.1 add.20.refs_3_
  59.5 1.1 %collective-permute-start.20 = (bf16[256,384]{1,0:T(8,128)(2,1)S(1)}, bf16[256,384]{1,0:T(8,128)(2,1)S(1)}, u32[]{:S(2)}, u32[]{:S(2)}) collective-permute-start(bf16[256,384]{1,0:T(8,128)(2,1)S(1)} %add.20.refs_3_), channel_id=1, source_target_pairs={{0,1},{1,0},{2,3},{3,2},{4,5},{5,4},{6,7},{7,6},{8,9},{9,8},{10,11... | collective-permute-start | bytes 589832 | tf_op jit(solution)/shard_map/ppermute | solution.py:417
  60.6 1.1 %collective-permute-done.13.refs_1_ = bf16[256,384]{1,0:T(8,128)(2,1)S(1)} collective-permute-done((bf16[256,384]{1,0:T(8,128)(2,1)S(1)}, bf16[256,384]{1,0:T(8,128)(2,1)S(1)}, u32[]{:S(2)}, u32[]{:S(2)}) %collective-permute-start.13) | collective-permute-done | bytes 196640 | tf_op jit(solution)/shard_map/ppermute | solution.py:409
  61.7 0.2 collective-permute-done.15.refs_2_
  61.9 0.1 add.21._
  62.0 3.2 %weight_grads.4 = (f32[3072,1536]{1,0:T(8,128)}, f32[3072,1536]{1,0:T(8,128)}, f32[8,128]{1,0:T(8,128)S(1)}) custom-call(s32[12,32]{1,0:T(8,128)S(1)} %places.1.listed, bf16[24,128,128]{2,1,0:T(8,128)(2,1)S(1)} %get-tuple-element.48.toks0, bf16[24,128,128]{2,1,0:T(8,128)(2,1)S(1)} %get-tuple-element.49.toks1, ...), custom_call_target="tpu_custom_call", output_to_operand_aliasing={{0}: (5, {}), {1}: (6, {})} | custom-call | flops 1 | bytes 1 | tf_op jit(solution)/shard_map/weight_grads/pallas_call | solution.py:342
  65.2 0.6 collective-permute-done.19.refs_1_
  65.8 0.1 add.22._
  65.9 0.7 collective-permute-start.17
  66.6 2.1 %collective-permute-start.18 = (bf16[128,384]{1,0:T(8,128)(2,1)S(1)}, bf16[128,384]{1,0:T(8,128)(2,1)S(1)}, u32[]{:S(2)}, u32[]{:S(2)}) collective-permute-start(bf16[128,384]{1,0:T(8,128)(2,1)S(1)} %get-tuple-element.65), channel_id=1, source_target_pairs={{0,4},{1,5},{2,6},{3,7},{4,0},{5,1},{6,2},{7,3},{8,20},{9,21},{10,... | collective-permute-start | bytes 294920 | tf_op jit(solution)/shard_map/ppermute | solution.py:425
  68.7 5.2 %collective-permute-start.21 = (bf16[128,384]{1,0:T(8,128)(2,1)S(1)}, bf16[128,384]{1,0:T(8,128)(2,1)S(1)}, u32[]{:S(2)}, u32[]{:S(2)}) collective-permute-start(bf16[128,384]{1,0:T(8,128)(2,1)S(1)} %get-tuple-element.66), channel_id=1, source_target_pairs={{0,16},{1,17},{2,18},{3,19},{4,20},{5,21},{6,22},{7,23},{8,0},{9,1... | collective-permute-start | bytes 294920 | tf_op jit(solution)/shard_map/ppermute | solution.py:425
  73.9 0.1 collective-permute-start.22
  74.0 0.7 copy.27
  74.7 4.7 %weight_grads.5 = (f32[3072,1536]{1,0:T(8,128)}, f32[3072,1536]{1,0:T(8,128)}, f32[8,128]{1,0:T(8,128)}) custom-call(s32[12,32]{1,0:T(8,128)S(1)} %places.1.listed, bf16[24,128,128]{2,1,0:T(8,128)(2,1)S(1)} %get-tuple-element.48.toks0, bf16[24,128,128]{2,1,0:T(8,128)(2,1)S(1)} %get-tuple-element.49.toks1, ...), custom_call_target="tpu_custom_call", output_to_operand_aliasing={{0}: (5, {}), {1}: (6, {})} | custom-call | flops 1 | bytes 1 | tf_op jit(solution)/shard_map/weight_grads/pallas_call | solution.py:342
  79.5 3.4 %collective-permute-done.22 = bf16[128,384]{1,0:T(8,128)(2,1)S(1)} collective-permute-done((bf16[128,384]{1,0:T(8,128)(2,1)S(1)}, bf16[128,384]{1,0:T(8,128)(2,1)S(1)}, u32[]{:S(2)}, u32[]{:S(2)}) %collective-permute-start.22) | collective-permute-done | bytes 98336 | tf_op jit(solution)/shard_map/ppermute | solution.py:425
  82.9 0.7 add_convert_fusion
  (24 shorter events, 0.1 us)
Async XLA Ops:
  0.6 7.7 %collective-permute-start.7 = (bf16[128,384]{1,0:T(8,128)(2,1)}, bf16[128,384]{1,0:T(8,128)(2,1)S(1)}, u32[]{:S(2)}, u32[]{:S(2)}) collective-permute-start(bf16[128,384]{1,0:T(8,128)(2,1)} %param.5), channel_id=1, source_target_pairs={{0,0},{1,1},{2,2},{3,3},{4,4},{5,5},{6,6},{7,7},{16,8},{17,9},{18,... | collective-permute-start | bytes 294920 | tf_op jit(solution)/shard_map/ppermute | solution.py:384
  2.2 13.2 %collective-permute-start.1 = (bf16[128,384]{1,0:T(8,128)(2,1)}, bf16[128,384]{1,0:T(8,128)(2,1)S(1)}, u32[]{:S(2)}, u32[]{:S(2)}) collective-permute-start(bf16[128,384]{1,0:T(8,128)(2,1)} %param.5), channel_id=1, source_target_pairs={{20,0},{21,1},{22,2},{23,3},{16,4},{17,5},{18,6},{19,7},{4,8},{5,9... | collective-permute-start | bytes 294920 | tf_op jit(solution)/shard_map/ppermute | solution.py:384
  7.7 7.7 %collective-permute-start = (bf16[128,384]{1,0:T(8,128)(2,1)}, bf16[128,384]{1,0:T(8,128)(2,1)S(1)}, u32[]{:S(2)}, u32[]{:S(2)}) collective-permute-start(bf16[128,384]{1,0:T(8,128)(2,1)} %param.5), channel_id=1, source_target_pairs={{16,0},{17,1},{18,2},{19,3},{20,4},{21,5},{22,6},{23,7},{0,8},{1,9... | collective-permute-start | bytes 294920 | tf_op jit(solution)/shard_map/ppermute | solution.py:384
  7.7 6.1 %collective-permute-start.8 = (bf16[128,384]{1,0:T(8,128)(2,1)}, bf16[128,384]{1,0:T(8,128)(2,1)S(1)}, u32[]{:S(2)}, u32[]{:S(2)}) collective-permute-start(bf16[128,384]{1,0:T(8,128)(2,1)} %param.5), channel_id=1, source_target_pairs={{4,0},{5,1},{6,2},{7,3},{0,4},{1,5},{2,6},{3,7},{20,8},{21,9},{22,... | collective-permute-start | bytes 294920 | tf_op jit(solution)/shard_map/ppermute | solution.py:384
  13.8 5.7 %collective-permute-start.9 = (bf16[256,384]{1,0:T(8,128)(2,1)S(1)}, bf16[256,384]{1,0:T(8,128)(2,1)S(1)}, u32[]{:S(2)}, u32[]{:S(2)}) collective-permute-start(bf16[256,384]{1,0:T(8,128)(2,1)S(1)} %constant_dynamic-update-slice_fusion.2.own), channel_id=1, source_target_pairs={{0,1},{1,0},{2,3},{3,2},{4,5},{5,4},{6,7},{7,6},{8,9},{9,8},{10,11... | collective-permute-start | bytes 589832 | tf_op jit(solution)/shard_map/ppermute | solution.py:387
  15.4 7.3 %collective-permute-start.2 = (bf16[256,384]{1,0:T(8,128)(2,1)S(1)}, bf16[256,384]{1,0:T(8,128)(2,1)S(1)}, u32[]{:S(2)}, u32[]{:S(2)}) collective-permute-start(bf16[256,384]{1,0:T(8,128)(2,1)S(1)} %constant_dynamic-update-slice_fusion.refs_0_.own), channel_id=1, source_target_pairs={{0,1},{1,0},{2,3},{3,2},{4,5},{5,4},{6,7},{7,6},{8,9},{9,8},{10,11... | collective-permute-start | bytes 589832 | tf_op jit(solution)/shard_map/ppermute | solution.py:387
  16.0 15.3 %collective-permute-start.10 = (bf16[256,384]{1,0:T(8,128)(2,1)S(1)}, bf16[256,384]{1,0:T(8,128)(2,1)S(1)}, u32[]{:S(2)}, u32[]{:S(2)}) collective-permute-start(bf16[256,384]{1,0:T(8,128)(2,1)S(1)} %constant_dynamic-update-slice_fusion.2.own), channel_id=1, source_target_pairs={{0,2},{1,3},{2,0},{3,1},{4,6},{5,7},{6,4},{7,5},{8,10},{9,11},{10,... | collective-permute-start | bytes 589832 | tf_op jit(solution)/shard_map/ppermute | solution.py:388
  19.5 11.8 %collective-permute-start.11 = (bf16[256,384]{1,0:T(8,128)(2,1)S(1)}, bf16[256,384]{1,0:T(8,128)(2,1)S(1)}, u32[]{:S(2)}, u32[]{:S(2)}) collective-permute-start(bf16[256,384]{1,0:T(8,128)(2,1)S(1)} %collective-permute-done.9.near), channel_id=1, source_target_pairs={{0,2},{1,3},{2,0},{3,1},{4,6},{5,7},{6,4},{7,5},{8,10},{9,11},{10,... | collective-permute-start | bytes 589832 | tf_op jit(solution)/shard_map/ppermute | solution.py:391
  21.1 0.7 copy-start.1
  22.1 12.8 %collective-permute-start.3 = (bf16[256,384]{1,0:T(8,128)(2,1)S(1)}, bf16[256,384]{1,0:T(8,128)(2,1)S(1)}, u32[]{:S(2)}, u32[]{:S(2)}) collective-permute-start(bf16[256,384]{1,0:T(8,128)(2,1)S(1)} %constant_dynamic-update-slice_fusion.refs_0_.own), channel_id=1, source_target_pairs={{0,2},{1,3},{2,0},{3,1},{4,6},{5,7},{6,4},{7,5},{8,10},{9,11},{10,... | collective-permute-start | bytes 589832 | tf_op jit(solution)/shard_map/ppermute | solution.py:388
  22.7 12.3 %collective-permute-start.4 = (bf16[256,384]{1,0:T(8,128)(2,1)S(1)}, bf16[256,384]{1,0:T(8,128)(2,1)S(1)}, u32[]{:S(2)}, u32[]{:S(2)}) collective-permute-start(bf16[256,384]{1,0:T(8,128)(2,1)S(1)} %collective-permute-done.2.refs_1_.near), channel_id=1, source_target_pairs={{0,2},{1,3},{2,0},{3,1},{4,6},{5,7},{6,4},{7,5},{8,10},{9,11},{10,... | collective-permute-start | bytes 589832 | tf_op jit(solution)/shard_map/ppermute | solution.py:391
  28.2 9.3 %copy-start = (bf16[128,1536]{1,0:T(8,128)(2,1)S(1)}, bf16[128,1536]{1,0:T(8,128)(2,1)}, u32[]{:S(2)}) copy-start(bf16[128,1536]{1,0:T(8,128)(2,1)} %cot.3) | copy-start | bytes 1179652
  33.9 7.6 %collective-permute-start.12 = (f32[12,128,256]{2,1,0:T(8,128)S(1)}, f32[12,128,256]{2,1,0:T(8,128)S(1)}, u32[]{:S(2)}, u32[]{:S(2)}) collective-permute-start(f32[12,128,256]{2,1,0:T(8,128)S(1)} %get-tuple-element.37.part), channel_id=1, source_target_pairs={{0,16},{16,0},{1,17},{17,1},{2,18},{18,2},{3,19},{19,3},{4,20},{20... | collective-permute-start | bytes 4718600 | tf_op jit(solution)/shard_map/ppermute | solution.py:395
  37.4 10.0 %collective-permute-start.5 = (f32[12,128,256]{2,1,0:T(8,128)S(1)}, f32[12,128,256]{2,1,0:T(8,128)S(1)}, u32[]{:S(2)}, u32[]{:S(2)}) collective-permute-start(f32[12,128,256]{2,1,0:T(8,128)S(1)} %get-tuple-element.36.part), channel_id=1, source_target_pairs={{0,16},{16,0},{1,17},{17,1},{2,18},{18,2},{3,19},{19,3},{4,20},{20... | collective-permute-start | bytes 4718600 | tf_op jit(solution)/shard_map/ppermute | solution.py:395
  37.5 3.9 %collective-permute-start.6 = (bf16[128,1536]{1,0:T(8,128)(2,1)S(1)}, bf16[128,1536]{1,0:T(8,128)(2,1)S(1)}, u32[]{:S(2)}, u32[]{:S(2)}) collective-permute-start(bf16[128,1536]{1,0:T(8,128)(2,1)S(1)} %copy-done), channel_id=1, source_target_pairs={{0,16},{16,0},{1,17},{17,1},{2,18},{18,2},{3,19},{19,3},{4,20},{20... | collective-permute-start | bytes 1179656 | tf_op jit(solution)/shard_map/ppermute | solution.py:380
  45.8 8.1 %collective-permute-start.14 = (bf16[256,384]{1,0:T(8,128)(2,1)S(1)}, bf16[256,384]{1,0:T(8,128)(2,1)S(1)}, u32[]{:S(2)}, u32[]{:S(2)}) collective-permute-start(bf16[256,384]{1,0:T(8,128)(2,1)S(1)} %get-tuple-element.45), channel_id=1, source_target_pairs={{0,2},{1,3},{2,0},{3,1},{4,6},{5,7},{6,4},{7,5},{8,10},{9,11},{10,... | collective-permute-start | bytes 589832 | tf_op jit(solution)/shard_map/ppermute | solution.py:409
  51.9 7.6 %collective-permute-start.16 = (bf16[256,384]{1,0:T(8,128)(2,1)S(1)}, bf16[256,384]{1,0:T(8,128)(2,1)S(1)}, u32[]{:S(2)}, u32[]{:S(2)}) collective-permute-start(bf16[256,384]{1,0:T(8,128)(2,1)S(1)} %get-tuple-element.47), channel_id=1, source_target_pairs={{0,2},{1,3},{2,0},{3,1},{4,6},{5,7},{6,4},{7,5},{8,10},{9,11},{10,... | collective-permute-start | bytes 589832 | tf_op jit(solution)/shard_map/ppermute | solution.py:410
  52.5 9.3 %collective-permute-start.13 = (bf16[256,384]{1,0:T(8,128)(2,1)S(1)}, bf16[256,384]{1,0:T(8,128)(2,1)S(1)}, u32[]{:S(2)}, u32[]{:S(2)}) collective-permute-start(bf16[256,384]{1,0:T(8,128)(2,1)S(1)} %get-tuple-element.43), channel_id=1, source_target_pairs={{0,2},{1,3},{2,0},{3,1},{4,6},{5,7},{6,4},{7,5},{8,10},{9,11},{10,... | collective-permute-start | bytes 589832 | tf_op jit(solution)/shard_map/ppermute | solution.py:409
  54.0 7.9 %collective-permute-start.15 = (bf16[256,384]{1,0:T(8,128)(2,1)S(1)}, bf16[256,384]{1,0:T(8,128)(2,1)S(1)}, u32[]{:S(2)}, u32[]{:S(2)}) collective-permute-start(bf16[256,384]{1,0:T(8,128)(2,1)S(1)} %add.19._), channel_id=1, source_target_pairs={{0,1},{1,0},{2,3},{3,2},{4,5},{5,4},{6,7},{7,6},{8,9},{9,8},{10,11... | collective-permute-start | bytes 589832 | tf_op jit(solution)/shard_map/ppermute | solution.py:412
  54.6 11.2 %collective-permute-start.19 = (bf16[256,384]{1,0:T(8,128)(2,1)S(1)}, bf16[256,384]{1,0:T(8,128)(2,1)S(1)}, u32[]{:S(2)}, u32[]{:S(2)}) collective-permute-start(bf16[256,384]{1,0:T(8,128)(2,1)S(1)} %get-tuple-element.56), channel_id=1, source_target_pairs={{0,2},{1,3},{2,0},{3,1},{4,6},{5,7},{6,4},{7,5},{8,10},{9,11},{10,... | collective-permute-start | bytes 589832 | tf_op jit(solution)/shard_map/ppermute | solution.py:410
  59.5 6.3 %collective-permute-start.20 = (bf16[256,384]{1,0:T(8,128)(2,1)S(1)}, bf16[256,384]{1,0:T(8,128)(2,1)S(1)}, u32[]{:S(2)}, u32[]{:S(2)}) collective-permute-start(bf16[256,384]{1,0:T(8,128)(2,1)S(1)} %add.20.refs_3_), channel_id=1, source_target_pairs={{0,1},{1,0},{2,3},{3,2},{4,5},{5,4},{6,7},{7,6},{8,9},{9,8},{10,11... | collective-permute-start | bytes 589832 | tf_op jit(solution)/shard_map/ppermute | solution.py:417
  65.9 13.5 %collective-permute-start.17 = (bf16[128,384]{1,0:T(8,128)(2,1)S(1)}, bf16[128,384]{1,0:T(8,128)(2,1)S(1)}, u32[]{:S(2)}, u32[]{:S(2)}) collective-permute-start(bf16[128,384]{1,0:T(8,128)(2,1)S(1)} %get-tuple-element.64), channel_id=1, source_target_pairs={{0,0},{1,1},{2,2},{3,3},{4,4},{5,5},{6,6},{7,7},{8,16},{9,17},{10,... | collective-permute-start | bytes 294920 | tf_op jit(solution)/shard_map/ppermute | solution.py:425
  66.6 12.8 %collective-permute-start.18 = (bf16[128,384]{1,0:T(8,128)(2,1)S(1)}, bf16[128,384]{1,0:T(8,128)(2,1)S(1)}, u32[]{:S(2)}, u32[]{:S(2)}) collective-permute-start(bf16[128,384]{1,0:T(8,128)(2,1)S(1)} %get-tuple-element.65), channel_id=1, source_target_pairs={{0,4},{1,5},{2,6},{3,7},{4,0},{5,1},{6,2},{7,3},{8,20},{9,21},{10,... | collective-permute-start | bytes 294920 | tf_op jit(solution)/shard_map/ppermute | solution.py:425
  68.7 10.8 %collective-permute-start.21 = (bf16[128,384]{1,0:T(8,128)(2,1)S(1)}, bf16[128,384]{1,0:T(8,128)(2,1)S(1)}, u32[]{:S(2)}, u32[]{:S(2)}) collective-permute-start(bf16[128,384]{1,0:T(8,128)(2,1)S(1)} %get-tuple-element.66), channel_id=1, source_target_pairs={{0,16},{1,17},{2,18},{3,19},{4,20},{5,21},{6,22},{7,23},{8,0},{9,1... | collective-permute-start | bytes 294920 | tf_op jit(solution)/shard_map/ppermute | solution.py:425
  73.9 9.0 %collective-permute-start.22 = (bf16[128,384]{1,0:T(8,128)(2,1)S(1)}, bf16[128,384]{1,0:T(8,128)(2,1)S(1)}, u32[]{:S(2)}, u32[]{:S(2)}) collective-permute-start(bf16[128,384]{1,0:T(8,128)(2,1)S(1)} %get-tuple-element.67), channel_id=1, source_target_pairs={{0,20},{1,21},{2,22},{3,23},{4,16},{5,17},{6,18},{7,19},{8,4},{9,5... | collective-permute-start | bytes 294920 | tf_op jit(solution)/shard_map/ppermute | solution.py:425

commit v2 on v1

--- a/solution.py
+++ b/solution.py
@@ -80,7 +80,7 @@
 
 def z_pairs(k1, k0):
     return [
-        (place(k1 ^ (z >> 1), 2 * half + (k0 ^ (z & 1)), y, x), place(half, z, y, x))
+        (place(k1 ^ (z >> 1), 2 * half + 1 - (k0 ^ (z & 1)), y, x), place(half, z, y, x))
         for half in range(2)
         for z in range(4)
         for y in range(2)
@@ -93,7 +93,7 @@
 
 
 X, Y = 1, 2
-NEAR, FAR = lane_pairs(X, Y), lane_pairs(Y, X)
+NEAR, FAR, ACROSS = lane_pairs(X, Y), lane_pairs(Y, X), lane_pairs(X + Y, X + Y)
 SLACK = 4
 SMALL = pl.CostEstimate(flops=1, bytes_accessed=1, transcendentals=0)
 
@@ -111,7 +111,7 @@
     row, z, y, x = q
     dy = dnear * row + dfar * (1 - row)
     dx = dnear * (1 - row) + dfar * row
-    return flip(k0, z % 2) * 4 + flip(dy, y) * 2 + flip(dx, x), flip(k1, z // 2)
+    return flip(1 - k0, z % 2) * 4 + flip(dy, y) * 2 + flip(dx, x), flip(k1, z // 2)
 
 
 def in_vmem(array):
@@ -207,14 +207,37 @@
     )(listed, in_hbm(gate_w), in_hbm(up_w), *([in_vmem(earlier)] if turning else []), later_than)
 
 
-def forward_kernel(turn, listed, packed_a, packed_b, own, near, far, both, part, turned, tokens):
+def start_clearing(first, count, listed, zeros, gate_out, up_out, sem):
+    zeros[...] = jnp.zeros_like(zeros)
+    kept = kept_of(listed)
+
+    def column(j, _):
+        cols = spanning(first + j)
+        for k in range(kept):
+            rows = spanning(listed[first + j, kept + SLACK + k])
+            pltpu.make_async_copy(zeros, gate_out.at[rows, cols], sem).start()
+            pltpu.make_async_copy(zeros, up_out.at[rows, cols], sem).start()
+        return 0
+
+    lax.fori_loop(0, count, column, 0)
+
+
+def finish_clearing(count, gate_out, sem):
+    written = gate_out.at[:, pl.ds(0, count * BLOCK)]
+    pltpu.make_async_copy(written, written, sem).wait()
+
+
+CLEARING = [VMEM((BLOCK, BLOCK), F32), pltpu.SemaphoreType.DMA]
+
+
+def forward_kernel(turn, listed, packed_a, packed_b, here, there, _, part, turned, tokens):
     q = coords()
-    width = own.shape[1] // BLOCK
-    for ref, dnear, dfar in ((own, 0, 0), (near, 1, 0), (far, 0, 1), (both, 1, 1)):
-        for k0 in range(2):
-            chip, _ = block_of(q, dnear, dfar, turn, k0)
+    width = here.shape[1] // BLOCK
+    for dfar, ref in enumerate((here, there)):
+        for slot in range(4):
+            chip, _ = block_of(q, slot // 2, dfar, turn, slot % 2)
             for s in range(width):
-                tokens[chip * width + s] = ref[k0 * BLOCK : (k0 + 1) * BLOCK, s * BLOCK : (s + 1) * BLOCK]
+                tokens[chip * width + s] = ref[slot * BLOCK : (slot + 1) * BLOCK, s * BLOCK : (s + 1) * BLOCK]
     cut = packed_a.shape[0]
     for j in range(part.shape[0]):
         picked = jnp.concatenate([tokens[listed[j, k]] for k in range(kept_of(listed))], axis=1)
@@ -224,36 +247,33 @@
         turned[i] = tokens[i].T
 
 
-def forward(turn, listed, packed, parts):
+def forward(turn, listed, packed, parts, later_than):
     columns = packed[0].shape[0] + packed[1].shape[0]
     seg = parts[0].shape[1] // BLOCK * 8
     return pl.pallas_call(
         functools.partial(forward_kernel, turn),
         out_shape=[VMEM((columns, BLOCK, 2 * BLOCK), F32), VMEM((seg, BLOCK, BLOCK), BF16)],
-        in_specs=[spec(SMEM)] + [spec(VMEM)] * 6,
+        in_specs=[spec(SMEM)] + [spec(VMEM)] * 4 + [spec(pl.ANY)],
         out_specs=[spec(VMEM)] * 2,
         scratch_shapes=[VMEM((seg, BLOCK, BLOCK), BF16)],
         compiler_params=pltpu.CompilerParams(vmem_limit_bytes=8 * MIB),
         cost_estimate=SMALL,
         name="forward",
-    )(listed, *map(in_vmem, packed), *parts)
-
-
-def backward_kernel(
-    turn, listed, turned_a, packed_b, part, other, cot, other_cot, *rest
-):
+    )(listed, *map(in_vmem, packed), *parts, later_than)
+
+
+def backward_kernel(turn, listed, turned_a, turned_b, part, other, cot, other_cot, *refs):
     if turn:
-        before, gate_in, up_in, hidden, grads, s00, s01, s10, s11, gate_out, up_out, acc, zeros, sem = rest
+        before, hidden, grads, far, near, acc = refs
     else:
-        hidden, grads, s00, s01, s10, s11, gate_out, up_out, acc, zeros, sem = rest
+        hidden, grads, far, near, acc = refs
     q = coords()
     columns, kept = part.shape[0], kept_of(listed)
     mine = flip(turn, q[1] // 2) == q[0]
     acc[...] = jnp.zeros_like(acc)
-    zeros[...] = jnp.zeros_like(zeros)
     cut = turned_a.shape[0]
 
-    def column(j, packed, at):
+    def column(j, turned, at):
         cols = spanning(j)
         total = part[j] + other[j]
         gate, up = total[:, :BLOCK], total[:, BLOCK:]
@@ -264,64 +284,49 @@
         hidden[:, cols] = jnp.where(mine, shown, before[:, cols]) if turn else shown
         grads[j, :, :BLOCK] = (cotf * up * sig * (1.0 + gate * (1.0 - sig))).astype(BF16)
         grads[j, :, BLOCK:] = (cotf * silu).astype(BF16)
-        facing = (((1,), (0 if packed is turned_a else 1,)), ((), ()))
-        spread = lax.dot_general(grads[j], packed[at], facing, preferred_element_type=F32)
+        spread = jnp.dot(grads[j], turned[at], preferred_element_type=F32)
         for k in range(kept):
             acc[listed[j, k]] += spread[:, k * BLOCK : (k + 1) * BLOCK]
 
-    def clear(j):
-        for k in range(kept):
-            rows = spanning(listed[j, kept + SLACK + k])
-            pltpu.make_async_copy(zeros, gate_out.at[rows, spanning(j)], sem).start()
-            pltpu.make_async_copy(zeros, up_out.at[rows, spanning(j)], sem).start()
-
-    cleared = columns // 2
-    lax.fori_loop(0, cleared, lambda j, _: (clear(turn * cleared + j), 0)[1], 0)
     step = 3
-    for packed, first, number in ((turned_a, 0, cut), (packed_b, cut, columns - cut)):
-
-        def steps(g, _, packed=packed, first=first):
+    for turned, first, number in ((turned_a, 0, cut), (turned_b, cut, columns - cut)):
+
+        def steps(g, _, turned=turned, first=first):
             for u in range(step):
-                column(first + g * step + u, packed, g * step + u)
+                column(first + g * step + u, turned, g * step + u)
             return 0
 
         lax.fori_loop(0, number // step, steps, 0)
-    width = s00.shape[1] // BLOCK
-    for ref, dnear, dfar in ((s11, 1, 1), (s01, 0, 1), (s10, 1, 0), (s00, 0, 0)):
-        for k0 in range(2):
-            chip, _ = block_of(q, dnear, dfar, turn, k0)
+    width = far.shape[1] // BLOCK
+    for dfar, ref in enumerate((near, far)):
+        for slot in range(4):
+            chip, _ = block_of(q, 1 - slot // 2, dfar, turn, slot % 2)
             for s in range(width):
-                ref[k0 * BLOCK : (k0 + 1) * BLOCK, s * BLOCK : (s + 1) * BLOCK] = acc[chip * width + s].astype(BF16)
-    part_written = gate_out.at[:, pl.ds(0, cleared * BLOCK)]
-    pltpu.make_async_copy(part_written, part_written, sem).wait()
-
-
-def backward(turn, listed, packed, part, other, cot, other_cot, width, grad_shape, before=None):
+                ref[slot * BLOCK : (slot + 1) * BLOCK, s * BLOCK : (s + 1) * BLOCK] = acc[chip * width + s].astype(BF16)
+
+
+def backward(turn, listed, packed, part, other, cot, other_cot, width, before=None):
     columns = part.shape[0]
-    extra = [] if before is None else [before[0], in_hbm(before[1]), in_hbm(before[2])]
+    extra = [] if before is None else [before]
     return pl.pallas_call(
         functools.partial(backward_kernel, turn),
         out_shape=[VMEM(cot.shape, BF16), VMEM((columns, BLOCK, 2 * BLOCK), BF16)]
-        + [VMEM((2 * BLOCK, width), BF16)] * 4
-        + [pltpu.HBM(grad_shape, F32)] * 2,
-        in_specs=[spec(SMEM)] + [spec(VMEM)] * 6 + ([spec(VMEM)] + [spec(pltpu.HBM)] * 2 if extra else []),
-        out_specs=[spec(VMEM)] * 6 + [spec(pltpu.HBM)] * 2,
-        scratch_shapes=[
-            VMEM((8 * width // BLOCK, BLOCK, BLOCK), F32),
-            VMEM((BLOCK, BLOCK), F32),
-            pltpu.SemaphoreType.DMA,
-        ],
-        input_output_aliases={8: 6, 9: 7} if extra else {},
+        + [VMEM((4 * BLOCK, width), BF16)] * 2,
+        in_specs=[spec(SMEM)] + [spec(VMEM)] * (6 + len(extra)),
+        out_specs=[spec(VMEM)] * 4,
+        scratch_shapes=[VMEM((8 * width // BLOCK, BLOCK, BLOCK), F32)],
         compiler_params=pltpu.CompilerParams(vmem_limit_bytes=8 * MIB),
         cost_estimate=SMALL,
         name="backward",
     )(listed, *map(in_vmem, packed), in_vmem(part), in_vmem(other), cot, other_cot, *extra)
 
 
-def weight_kernel(first, listed, toks0, toks1, grads0, grads1, gate_in, up_in, _, gate_out, up_out, token, stage, sem):
-    kept = kept_of(listed)
-    for slot in range(stage.shape[0]):
-        j = first + slot
+def weight_kernel(first, count, listed, toks0, toks1, grads0, grads1, gate_in, up_in, _, gate_out, up_out, stage, sems):
+    kept, slots = kept_of(listed), stage.shape[0]
+    for j in range(first, first + count):
+        slot = (j - first) % slots
+        if j - first >= slots:
+            pltpu.make_async_copy(stage.at[slot], stage.at[slot], sems.at[slot]).wait()
         picked = jnp.concatenate(
             [jnp.concatenate([toks0[listed[j, k]], toks1[listed[j, k]]], axis=1) for k in range(kept)], axis=0
         )
@@ -330,46 +335,110 @@
         for k in range(kept):
             rows = spanning(listed[j, k])
             here = stage.at[slot, k * BLOCK : (k + 1) * BLOCK]
-            pltpu.make_async_copy(here.at[:, :BLOCK], gate_out.at[rows, spanning(j)], sem).start()
-            pltpu.make_async_copy(here.at[:, BLOCK:], up_out.at[rows, spanning(j)], sem).start()
-    token[...] = jnp.zeros_like(token)
-    pltpu.make_async_copy(stage, stage, sem).wait()
+            pltpu.make_async_copy(here.at[:, :BLOCK], gate_out.at[rows, spanning(j)], sems.at[slot]).start()
+            pltpu.make_async_copy(here.at[:, BLOCK:], up_out.at[rows, spanning(j)], sems.at[slot]).start()
+    for slot in range(slots):
+        pltpu.make_async_copy(stage.at[slot], stage.at[slot], sems.at[slot]).wait()
 
 
 def weight_grads(first, count, listed, tokens, grads, written, later_than):
-    kept = kept_of(listed)
-    grad = pltpu.HBM(written[0].shape, F32)
-    return pl.pallas_call(
-        functools.partial(weight_kernel, first),
-        out_shape=[grad, grad, VMEM((8, BLOCK), F32)],
+    slots = min(6, count)
+    return pl.pallas_call(
+        functools.partial(weight_kernel, first, count),
+        out_shape=[pltpu.HBM(grad.shape, F32) for grad in written],
         in_specs=[spec(SMEM)] + [spec(VMEM)] * 4 + [spec(pltpu.HBM)] * 2 + [spec(pl.ANY)],
-        out_specs=[spec(pltpu.HBM)] * 2 + [spec(VMEM)],
-        scratch_shapes=[VMEM((count, kept * BLOCK, 2 * BLOCK), F32), pltpu.SemaphoreType.DMA],
+        out_specs=[spec(pltpu.HBM)] * 2,
+        scratch_shapes=[VMEM((slots, kept_of(listed) * BLOCK, 2 * BLOCK), F32), pltpu.SemaphoreType.DMA((slots,))],
         input_output_aliases={5: 0, 6: 1},
-        compiler_params=pltpu.CompilerParams(vmem_limit_bytes=12 * MIB),
+        compiler_params=pltpu.CompilerParams(vmem_limit_bytes=16 * MIB),
         cost_estimate=SMALL,
         name="weight_grads",
-    )(listed, *map(in_vmem, tokens), *map(in_vmem, grads), in_hbm(written[0]), in_hbm(written[1]), later_than)
-
-
-def add_kernel(*refs):
+    )(listed, *map(in_vmem, tokens), *map(in_vmem, grads), *map(in_hbm, written), later_than)
+
+
+def add_kernel(firsts, *refs):
     out = refs[-1]
-    total = refs[0][...].astype(F32)
-    for ref in refs[1:-2]:
-        total += ref[...].astype(F32)
+    total = 0.0
+    for first, ref in zip(firsts, refs):
+        total += ref[first : first + out.shape[0]].astype(F32)
     out[...] = total.astype(BF16)
 
 
 def add(*terms, later_than):
-    return pl.pallas_call(
-        add_kernel,
-        out_shape=VMEM(terms[0].shape, BF16),
-        in_specs=[spec(VMEM)] * len(terms) + [spec(pl.ANY)],
+    firsts, arrays = zip(*terms)
+    return pl.pallas_call(
+        functools.partial(add_kernel, firsts),
+        out_shape=VMEM((2 * BLOCK, arrays[0].shape[1]), BF16),
+        in_specs=[spec(VMEM)] * len(arrays) + [spec(pl.ANY)],
         out_specs=spec(VMEM),
         compiler_params=pltpu.CompilerParams(vmem_limit_bytes=4 * MIB),
         cost_estimate=SMALL,
         name="add",
-    )(*terms, later_than)
+    )(*arrays, later_than)
+
+
+def join_kernel(_, *refs):
+    ins, out = refs[:-1], refs[-1]
+    size = ins[0].shape[0]
+    for i, ref in enumerate(ins):
+        out[i * size : (i + 1) * size] = ref[...]
+
+
+def join(*parts, later_than):
+    rows, width = parts[0].shape
+    return pl.pallas_call(
+        join_kernel,
+        out_shape=VMEM((len(parts) * rows, width), BF16),
+        in_specs=[spec(pl.ANY)] + [spec(VMEM)] * len(parts),
+        out_specs=spec(VMEM),
+        compiler_params=pltpu.CompilerParams(vmem_limit_bytes=4 * MIB),
+        cost_estimate=SMALL,
+        name="join",
+    )(later_than, *parts)
+
+
+def mix_kernel(_, own, near, *outs):
+    half = own.shape[0] // 2
+    for i, out in enumerate(outs):
+        out[:half] = own[i * half : (i + 1) * half]
+        out[half:] = near[i * half : (i + 1) * half]
+
+
+def mix(own, near, later_than):
+    return pl.pallas_call(
+        mix_kernel,
+        out_shape=[VMEM(own.shape, BF16)] * 2,
+        in_specs=[spec(pl.ANY)] + [spec(VMEM)] * 2,
+        out_specs=[spec(VMEM)] * 2,
+        compiler_params=pltpu.CompilerParams(vmem_limit_bytes=4 * MIB),
+        cost_estimate=SMALL,
+        name="mix",
+    )(later_than, own, near)
+
+
+def turn_kernel(listed, packed, _, turned, gate_out, up_out, zeros, sem):
+    start_clearing(0, listed.shape[0], listed, zeros, gate_out, up_out, sem)
+
+    def turn(j, _):
+        turned[j] = packed[j].T
+        return 0
+
+    lax.fori_loop(0, packed.shape[0], turn, 0)
+    finish_clearing(listed.shape[0], gate_out, sem)
+
+
+def transposed(listed, packed, grad_shape, later_than):
+    columns, rows, wide = packed.shape
+    return pl.pallas_call(
+        turn_kernel,
+        out_shape=[VMEM((columns, wide, rows), BF16)] + [pltpu.HBM(grad_shape, F32)] * 2,
+        in_specs=[spec(SMEM), spec(VMEM), spec(pl.ANY)],
+        out_specs=[spec(VMEM)] + [spec(pltpu.HBM)] * 2,
+        scratch_shapes=CLEARING,
+        compiler_params=pltpu.CompilerParams(vmem_limit_bytes=4 * MIB),
+        cost_estimate=SMALL,
+        name="turn",
+    )(listed, in_vmem(packed), later_than)
 
 
 def chip_body(tokens, gate_weight, up_weight, block_mask, cotangent):
@@ -377,56 +446,52 @@
     width = tokens.shape[1]
     columns, segs = gate_weight.shape[1] // BLOCK, gate_weight.shape[0] // BLOCK
     cut = columns // 2
+    listed = places(block_mask.T, segs)
     other_cot = lax.ppermute(cotangent, "row", swap)
-    listed = places(block_mask.T, segs)
-
-    def gathered(turn):
-        return jnp.concatenate([lax.ppermute(tokens, AXES, z_pairs(turn, k0)) for k0 in range(2)], axis=0)
-
-    owns = [gathered(0), gathered(1)]
-    nears = [lax.ppermute(own, AXES, NEAR) for own in owns]
-    fars = [lax.ppermute(own, AXES, FAR) for own in owns]
-    (pack_a,) = pack(0, cut, listed, gate_weight, up_weight, owns[1])
-    pack_b, turned_a = pack(cut, columns - cut, listed, gate_weight, up_weight, nears[1], pack_a)
-    boths = [lax.ppermute(near, AXES, FAR) for near in nears]
-    held = list(zip(owns, nears, fars, boths))
-
-    parts, toks = zip(*[forward(turn, listed, (pack_a, pack_b), held[turn]) for turn in range(2)])
-    others = [lax.ppermute(part, "row", swap) for part in parts]
-    done = []
-    for turn in range(2):
-        before = (done[0][0], done[0][6], done[0][7]) if turn else None
-        weights = (turned_a, pack_b)
-        done.append(
-            backward(
-                turn, listed, weights, parts[turn], others[turn], cotangent, other_cot, width, gate_weight.shape, before
-            )
-        )
-    grads = [out[1] for out in done]
-    hidden = done[1][0]
-
-    (a00, a01, a10, a11), (b00, b01, b10, b11) = done[0][2:6], done[1][2:6]
-    first_a, direct_a = lax.ppermute(a11, AXES, FAR), lax.ppermute(a01, AXES, FAR)
-    first_b, direct_b = lax.ppermute(b11, AXES, FAR), lax.ppermute(b01, AXES, FAR)
-    sum_a = add(a10, first_a, later_than=b10)
+
+    again = join(tokens, later_than=other_cot)
+    blocks = [
+        lax.ppermute(block, AXES, z_pairs(turn, k0)) for turn in range(2) for k0, block in enumerate((tokens, again))
+    ]
+    (pack_a,) = pack(0, cut, listed, gate_weight, up_weight, other_cot)
+    own = join(*blocks, later_than=pack_a)
+    near = lax.ppermute(own, AXES, NEAR)
+    pack_b, turned_a = pack(cut, columns - cut, listed, gate_weight, up_weight, own, pack_a)
+    heres = mix(own, near, later_than=pack_b)
+    theres = [lax.ppermute(here, AXES, FAR) for here in heres]
+    turned_b, *written = transposed(listed, pack_b, gate_weight.shape, heres[1])
+    turned, packed = (turned_a, turned_b), (pack_a, pack_b)
+
+    part_a, toks_a = forward(0, listed, packed, (heres[0], theres[0]), turned_b)
+    part_b, toks_b = forward(1, listed, packed, (heres[1], theres[1]), turned_b)
+    toks = (toks_a, toks_b)
+    other_a, other_b = (lax.ppermute(part, "row", swap) for part in (part_a, part_b))
+    shown, grads_a, far_a, near_a = backward(0, listed, turned, part_a, other_a, cotangent, other_cot, width)
+    hidden, grads_b, far_b, near_b = backward(1, listed, turned, part_b, other_b, cotangent, other_cot, width, shown)
+    grads = (grads_a, grads_b)
+
+    pair = 2 * BLOCK
+    got_a = lax.ppermute(far_a, AXES, FAR)
+    first_b, direct_b = lax.ppermute(far_b[:pair], AXES, FAR), lax.ppermute(far_b[pair:], AXES, FAR)
+    sum_a = add((0, near_a), (0, got_a), later_than=far_b)
     carried_a = lax.ppermute(sum_a, AXES, NEAR)
-    lead, middle = columns // 3, columns // 4
-    written = done[1][6:8]
-    *written, token = weight_grads(0, lead, listed, toks, grads, written, sum_a)
-    sum_b = add(b10, first_b, later_than=token)
+    sum_b = add((0, near_b), (0, first_b), later_than=sum_a)
     carried_b = lax.ppermute(sum_b, AXES, NEAR)
-    here_a = add(a00, direct_a, carried_a, later_than=sum_b)
-    *written, token = weight_grads(lead, middle, listed, toks, grads, written, here_a)
-    here_b = add(b00, direct_b, carried_b, later_than=token)
-    total = jnp.zeros(tokens.shape, F32)
-    for turn, here in enumerate((here_a, here_b)):
+    here_a = add((pair, near_a), (pair, got_a), (0, carried_a), later_than=sum_b)
+    here_b = add((pair, near_b), (0, direct_b), (0, carried_b), later_than=here_a)
+
+    def homeward(turn, here):
         for k0 in range(2):
             back = [(b, a) for a, b in z_pairs(turn, k0)]
-            total += lax.ppermute(here[k0 * BLOCK : (k0 + 1) * BLOCK], AXES, back).astype(F32)
-    input_grad = total.astype(BF16)
-    last = lead + middle
-    *written, token = weight_grads(last, columns - last, listed, toks, grads, written, here_b)
-    return hidden, input_grad, *written
+            yield lax.ppermute(here[k0 * BLOCK : (k0 + 1) * BLOCK], AXES, back)
+
+    home_a, home_b = list(homeward(0, here_a)), list(homeward(1, here_b))
+    joined_a = join(*home_a, later_than=here_b)
+    lead = columns * 5 // 6
+    written = weight_grads(0, lead, listed, toks, grads, written, here_b)
+    written = weight_grads(lead, columns - lead, listed, toks, grads, written, joined_a)
+    total = sum(piece.astype(F32) for piece in (joined_a[:BLOCK], joined_a[BLOCK:], *home_b))
+    return hidden, total.astype(BF16), *written
 
 
 def solution(mesh):

time: 83.9 us -> 75.2 us (0.90)
  the two profiles are of different devices: /device:TPU:0 before, /device:TPU:1 now
where the time goes in v2:
time: 75.2 us; the launch traced here: 74.8 us
  Pallas kernels  35.4 us (47%)
  starting transfers between devices  27.5 us (37%)
  waiting for transfers between devices  7.84 us (10%)
  local copies, waits for them, and re-layouts  2.48 us (3%)
  between operations  0.9 us (1%)
    ppermute x4, starting transfers between devices, homeward(): yield lax.ppermute(here[k0 * BLOCK:(k0 + 1) * BLOCK], AXES, back)  10.9 us
    pallas_call x2, Pallas kernels, weight_grads(): pl.pallas_call(functools.partial(weight_kernel, first, count), out_shape=...  9.55 us
    ppermute x4, starting transfers between devices, chip_body(): lax.ppermute(block, AXES, z_pairs(turn, k0))  7.6 us
    pallas_call x1, Pallas kernels, transposed(): pl.pallas_call(turn_kernel, out_shape=[VMEM((columns, wide, rows), BF16)]...  7.01 us
    pallas_call x2, Pallas kernels, backward(): pl.pallas_call(functools.partial(backward_kernel, turn), out_shape=[VMEM(...  6.88 us
    pallas_call x2, Pallas kernels, pack(): pl.pallas_call(functools.partial(pack_kernel, first, turning), out_shape=...  6.23 us
    pallas_call x2, Pallas kernels, forward(): pl.pallas_call(functools.partial(forward_kernel, turn), out_shape=[VMEM((...  4.99 us
    unnamed x7, local copies, waits for them, and re-layouts  2.4 us
  transfers between devices with their start and end apart: 19, of which 6 were waited for; matrix products, arithmetic and copies ran while one was open for 1% of the time, Pallas kernels for 47%

profile of v2, /device:TPU:1, one launch (start us, length us, event | category | flops | bytes accessed | tf_op | source)
XLA Modules:
  0.0 74.8 jit_solution(8442348884865883628)
XLA Ops:
  0.6 0.1 collective-permute-start
  0.8 4.7 %collective-permute-start.1 = (bf16[128,384]{1,0:T(8,128)(2,1)}, bf16[128,384]{1,0:T(8,128)(2,1)S(1)}, u32[]{:S(2)}, u32[]{:S(2)}) collective-permute-start(bf16[128,384]{1,0:T(8,128)(2,1)} %refs_0_.1), channel_id=1, source_target_pairs={{4,0},{5,1},{6,2},{7,3},{0,4},{1,5},{2,6},{3,7},{20,8},{21,9},{22,... | collective-permute-start | bytes 294920 | tf_op jit(solution)/shard_map/ppermute | solution.py:454
  5.5 0.0 collective-permute-start.3
  5.5 0.0 collective-permute-done.refs_0_._.other_cot
  5.5 1.0 %copy-done.1 = bf16[128,384]{1,0:T(8,128)(2,1)S(1)} copy-done((bf16[128,384]{1,0:T(8,128)(2,1)S(1)}, bf16[128,384]{1,0:T(8,128)(2,1)}, u32[]{:S(2)}) %copy-start.1) | copy-done | bytes 98328
  6.5 0.5 collective-permute-start.4
  7.0 2.4 %collective-permute-start.2 = (bf16[128,384]{1,0:T(8,128)(2,1)S(1)}, bf16[128,384]{1,0:T(8,128)(2,1)S(1)}, u32[]{:S(2)}, u32[]{:S(2)}) collective-permute-start(bf16[128,384]{1,0:T(8,128)(2,1)S(1)} %join.3), channel_id=1, source_target_pairs={{0,0},{1,1},{2,2},{3,3},{4,4},{5,5},{6,6},{7,7},{16,8},{17,9},{18,... | collective-permute-start | bytes 294920 | tf_op jit(solution)/shard_map/ppermute | solution.py:454
  9.3 0.0 copy-start.2
  9.3 0.7 copy-done.2
  10.0 0.4 places.1.listed
  10.4 3.1 %pack.2._.refs_0_.packed_a = bf16[6,1536,256]{2,1,0:T(8,128)(2,1)S(1)} custom-call(s32[12,32]{1,0:T(8,128)S(1)} %places.1.listed, bf16[3072,1536]{1,0:T(8,128)(2,1)} %gate_w.3, bf16[3072,1536]{1,0:T(8,128)(2,1)} %up_w.3, bf16[128,1536]{1,0:T(8,128)(2,1)S(1)} %collective-permute-done.refs_0_._.other_cot), custom_call_target="tpu_custom_call" | custom-call | flops 1 | bytes 1 | tf_op jit(solution)/shard_map/pack/pallas_call | solution.py:198
  13.5 0.0 collective-permute-done.1.refs_0_
  13.6 1.5 %collective-permute-done.2.refs_1_ = bf16[128,384]{1,0:T(8,128)(2,1)S(1)} collective-permute-done((bf16[128,384]{1,0:T(8,128)(2,1)S(1)}, bf16[128,384]{1,0:T(8,128)(2,1)S(1)}, u32[]{:S(2)}, u32[]{:S(2)}) %collective-permute-start.2) | collective-permute-done | bytes 98336 | tf_op jit(solution)/shard_map/ppermute | solution.py:454
  15.1 1.3 %collective-permute-start.5 = (bf16[512,384]{1,0:T(8,128)(2,1)S(1)}, bf16[512,384]{1,0:T(8,128)(2,1)S(1)}, u32[]{:S(2)}, u32[]{:S(2)}) collective-permute-start(bf16[512,384]{1,0:T(8,128)(2,1)S(1)} %join.4.refs_1_.own), channel_id=1, source_target_pairs={{0,1},{1,0},{2,3},{3,2},{4,5},{5,4},{6,7},{7,6},{8,9},{9,8},{10,11... | collective-permute-start | bytes 1179656 | tf_op jit(solution)/shard_map/ppermute | solution.py:458
  16.4 3.1 %pack.3 = (bf16[6,1536,256]{2,1,0:T(8,128)(2,1)S(1)}, bf16[6,256,1536]{2,1,0:T(8,128)(2,1)S(1)}) custom-call(s32[12,32]{1,0:T(8,128)S(1)} %places.1.listed, bf16[3072,1536]{1,0:T(8,128)(2,1)} %gate_w.3, bf16[3072,1536]{1,0:T(8,128)(2,1)} %up_w.3, bf16[6,1536,256]{2,1,0:T(8,128)(2,1)S(1)} %pack.2._.refs_0_.packed_a, bf16[512,384]{1,0:T(8,128)(2,1)S(1)} %join.4.refs_1_.own), custom_call_target="tpu_custom_call" | custom-call | flops 1 | bytes 1 | tf_op jit(solution)/shard_map/pack/pallas_call | solution.py:198
  19.6 2.3 %collective-permute-done.5.near = bf16[512,384]{1,0:T(8,128)(2,1)S(1)} collective-permute-done((bf16[512,384]{1,0:T(8,128)(2,1)S(1)}, bf16[512,384]{1,0:T(8,128)(2,1)S(1)}, u32[]{:S(2)}, u32[]{:S(2)}) %collective-permute-start.5) | collective-permute-done | bytes 393248 | tf_op jit(solution)/shard_map/ppermute | solution.py:458
  21.8 0.1 mix.1
  21.9 1.3 %collective-permute-start.8 = (bf16[512,384]{1,0:T(8,128)(2,1)S(1)}, bf16[512,384]{1,0:T(8,128)(2,1)S(1)}, u32[]{:S(2)}, u32[]{:S(2)}) collective-permute-start(bf16[512,384]{1,0:T(8,128)(2,1)S(1)} %get-tuple-element.32.here), channel_id=1, source_target_pairs={{0,2},{1,3},{2,0},{3,1},{4,6},{5,7},{6,4},{7,5},{8,10},{9,11},{10,... | collective-permute-start | bytes 1179656 | tf_op jit(solution)/shard_map/ppermute | solution.py:461
  23.2 0.3 collective-permute-start.6
  23.4 7.0 %turn.1 = (bf16[6,256,1536]{2,1,0:T(8,128)(2,1)S(1)}, f32[3072,1536]{1,0:T(8,128)}, f32[3072,1536]{1,0:T(8,128)}) custom-call(s32[12,32]{1,0:T(8,128)S(1)} %places.1.listed, bf16[6,1536,256]{2,1,0:T(8,128)(2,1)S(1)} %get-tuple-element.28._.packed.packed_b, bf16[512,384]{1,0:T(8,128)(2,1)S(1)} %get-tuple-element.29._.here), custom_call_target="tpu_custom_call" | custom-call | flops 1 | bytes 1 | tf_op jit(solution)/shard_map/turn/pallas_call | solution.py:432
  30.5 2.5 %forward.3 = (f32[12,128,256]{2,1,0:T(8,128)S(1)}, bf16[24,128,128]{2,1,0:T(8,128)(2,1)S(1)}) custom-call(s32[12,32]{1,0:T(8,128)S(1)} %places.1.listed, bf16[6,1536,256]{2,1,0:T(8,128)(2,1)S(1)} %pack.2._.refs_0_.packed_a, bf16[6,1536,256]{2,1,0:T(8,128)(2,1)S(1)} %get-tuple-element.28._.packed.packed_b, bf16[512,384]{1,0:T(8,128)(2,1)S(1)} %get-tuple-element.32.here, ...), custom_call_target="tpu_custom_call" | custom-call | flops 1 | bytes 1 | tf_op jit(solution)/shard_map/forward/pallas_call | solution.py:253
  33.0 0.0 copy-start
  33.0 0.1 collective-permute-start.9
  33.1 2.5 %forward.2 = (f32[12,128,256]{2,1,0:T(8,128)S(1)}, bf16[24,128,128]{2,1,0:T(8,128)(2,1)S(1)}) custom-call(s32[12,32]{1,0:T(8,128)S(1)} %places.1.listed, bf16[6,1536,256]{2,1,0:T(8,128)(2,1)S(1)} %pack.2._.refs_0_.packed_a, bf16[6,1536,256]{2,1,0:T(8,128)(2,1)S(1)} %get-tuple-element.28._.packed.packed_b, bf16[512,384]{1,0:T(8,128)(2,1)S(1)} %get-tuple-element.29._.here, ...), custom_call_target="tpu_custom_call" | custom-call | flops 1 | bytes 1 | tf_op jit(solution)/shard_map/forward/pallas_call | solution.py:253
  35.6 0.5 collective-permute-start.7
  36.1 0.3 collective-permute-done.9.other
  36.5 3.4 %backward.2 = (bf16[128,1536]{1,0:T(8,128)(2,1)S(1)}, bf16[12,128,256]{2,1,0:T(8,128)(2,1)S(1)}, bf16[512,384]{1,0:T(8,128)(2,1)S(1)}, bf16[512,384]{1,0:T(8,128)(2,1)S(1)}) custom-call(s32[12,32]{1,0:T(8,128)S(1)} %places.1.listed, bf16[6,256,1536]{2,1,0:T(8,128)(2,1)S(1)} %get-tuple-element.27.turned_a, ...), custom_call_target="tpu_custom_call" | custom-call | flops 1 | bytes 1 | tf_op jit(solution)/shard_map/backward/pallas_call | solution.py:311
  39.8 1.3 %collective-permute-start.12 = (bf16[512,384]{1,0:T(8,128)(2,1)S(1)}, bf16[512,384]{1,0:T(8,128)(2,1)S(1)}, u32[]{:S(2)}, u32[]{:S(2)}) collective-permute-start(bf16[512,384]{1,0:T(8,128)(2,1)S(1)} %get-tuple-element.39), channel_id=1, source_target_pairs={{0,2},{1,3},{2,0},{3,1},{4,6},{5,7},{6,4},{7,5},{8,10},{9,11},{10,... | collective-permute-start | bytes 1179656 | tf_op jit(solution)/shard_map/ppermute | solution.py:474
  41.1 3.5 %backward.3 = (bf16[128,1536]{1,0:T(8,128)(2,1)S(1)}, bf16[12,128,256]{2,1,0:T(8,128)(2,1)S(1)}, bf16[512,384]{1,0:T(8,128)(2,1)S(1)}, bf16[512,384]{1,0:T(8,128)(2,1)S(1)}) custom-call(s32[12,32]{1,0:T(8,128)S(1)} %places.1.listed, bf16[6,256,1536]{2,1,0:T(8,128)(2,1)S(1)} %get-tuple-element.27.turned_a, ...), custom_call_target="tpu_custom_call" | custom-call | flops 1 | bytes 1 | tf_op jit(solution)/shard_map/backward/pallas_call | solution.py:311
  44.7 0.3 collective-permute-start.11
  45.0 1.8 %collective-permute-done.12.refs_1_ = bf16[512,384]{1,0:T(8,128)(2,1)S(1)} collective-permute-done((bf16[512,384]{1,0:T(8,128)(2,1)S(1)}, bf16[512,384]{1,0:T(8,128)(2,1)S(1)}, u32[]{:S(2)}, u32[]{:S(2)}) %collective-permute-start.12) | collective-permute-done | bytes 393248 | tf_op jit(solution)/shard_map/ppermute | solution.py:474
  46.8 0.1 add.19.refs_2_
  46.9 1.3 %collective-permute-start.14 = (bf16[256,384]{1,0:T(8,128)(2,1)S(1)}, bf16[256,384]{1,0:T(8,128)(2,1)S(1)}, u32[]{:S(2)}, u32[]{:S(2)}) collective-permute-start(bf16[256,384]{1,0:T(8,128)(2,1)S(1)} %add.19.refs_2_), channel_id=1, source_target_pairs={{0,1},{1,0},{2,3},{3,2},{4,5},{5,4},{6,7},{7,6},{8,9},{9,8},{10,11... | collective-permute-start | bytes 589832 | tf_op jit(solution)/shard_map/ppermute | solution.py:477
  48.2 1.2 %collective-permute-start.10 = (bf16[256,384]{1,0:T(8,128)(2,1)S(1)}, bf16[256,384]{1,0:T(8,128)(2,1)S(1)}, u32[]{:S(2)}, u32[]{:S(2)}) collective-permute-start(bf16[256,384]{1,0:T(8,128)(2,1)S(1)} %get-tuple-element.51), channel_id=1, source_target_pairs={{0,2},{1,3},{2,0},{3,1},{4,6},{5,7},{6,4},{7,5},{8,10},{9,11},{10,... | collective-permute-start | bytes 589832 | tf_op jit(solution)/shard_map/ppermute | solution.py:475
  49.4 0.2 collective-permute-done.11.refs_1_
  49.5 0.1 add.20.refs_3_
  49.6 1.3 %collective-permute-start.13 = (bf16[256,384]{1,0:T(8,128)(2,1)S(1)}, bf16[256,384]{1,0:T(8,128)(2,1)S(1)}, u32[]{:S(2)}, u32[]{:S(2)}) collective-permute-start(bf16[256,384]{1,0:T(8,128)(2,1)S(1)} %add.20.refs_3_), channel_id=1, source_target_pairs={{0,1},{1,0},{2,3},{3,2},{4,5},{5,4},{6,7},{7,6},{8,9},{9,8},{10,11... | collective-permute-start | bytes 589832 | tf_op jit(solution)/shard_map/ppermute | solution.py:479
  50.9 1.7 %collective-permute-done.14.refs_2_ = bf16[256,384]{1,0:T(8,128)(2,1)S(1)} collective-permute-done((bf16[256,384]{1,0:T(8,128)(2,1)S(1)}, bf16[256,384]{1,0:T(8,128)(2,1)S(1)}, u32[]{:S(2)}, u32[]{:S(2)}) %collective-permute-start.14) | collective-permute-done | bytes 196640 | tf_op jit(solution)/shard_map/ppermute | solution.py:477
  52.6 0.1 add.21.refs_3_
  52.7 7.0 %collective-permute-start.16 = (bf16[128,384]{1,0:T(8,128)(2,1)S(1)}, bf16[128,384]{1,0:T(8,128)(2,1)S(1)}, u32[]{:S(2)}, u32[]{:S(2)}) collective-permute-start(bf16[128,384]{1,0:T(8,128)(2,1)S(1)} %get-tuple-element.52), channel_id=1, source_target_pairs={{0,0},{1,1},{2,2},{3,3},{4,4},{5,5},{6,6},{7,7},{8,16},{9,17},{10,... | collective-permute-start | bytes 294920 | tf_op jit(solution)/shard_map/ppermute | solution.py:486
  59.7 1.8 %collective-permute-start.15 = (bf16[128,384]{1,0:T(8,128)(2,1)S(1)}, bf16[128,384]{1,0:T(8,128)(2,1)S(1)}, u32[]{:S(2)}, u32[]{:S(2)}) collective-permute-start(bf16[128,384]{1,0:T(8,128)(2,1)S(1)} %get-tuple-element.53), channel_id=1, source_target_pairs={{0,4},{1,5},{2,6},{3,7},{4,0},{5,1},{6,2},{7,3},{8,20},{9,21},{10,... | collective-permute-start | bytes 294920 | tf_op jit(solution)/shard_map/ppermute | solution.py:486
  61.4 0.1 add.22._
  61.6 0.1 collective-permute-start.17
  61.6 2.1 %collective-permute-start.18 = (bf16[128,384]{1,0:T(8,128)(2,1)S(1)}, bf16[128,384]{1,0:T(8,128)(2,1)S(1)}, u32[]{:S(2)}, u32[]{:S(2)}) collective-permute-start(bf16[128,384]{1,0:T(8,128)(2,1)S(1)} %get-tuple-element.55), channel_id=1, source_target_pairs={{0,16},{1,17},{2,18},{3,19},{4,20},{5,21},{6,22},{7,23},{8,0},{9,1... | collective-permute-start | bytes 294920 | tf_op jit(solution)/shard_map/ppermute | solution.py:486
  63.8 0.7 copy.17
  64.5 6.7 %weight_grads.2 = (f32[3072,1536]{1,0:T(8,128)}, f32[3072,1536]{1,0:T(8,128)}) custom-call(s32[12,32]{1,0:T(8,128)S(1)} %places.1.listed, bf16[24,128,128]{2,1,0:T(8,128)(2,1)S(1)} %get-tuple-element.40.toks0, bf16[24,128,128]{2,1,0:T(8,128)(2,1)S(1)} %get-tuple-element.41.toks1, ...), custom_call_target="tpu_custom_call", output_to_operand_aliasing={{0}: (5, {}), {1}: (6, {})} | custom-call | flops 1 | bytes 1 | tf_op jit(solution)/shard_map/weight_grads/pallas_call | solution.py:346
  71.2 2.9 %weight_grads.3 = (f32[3072,1536]{1,0:T(8,128)}, f32[3072,1536]{1,0:T(8,128)}) custom-call(s32[12,32]{1,0:T(8,128)S(1)} %places.1.listed, bf16[24,128,128]{2,1,0:T(8,128)(2,1)S(1)} %get-tuple-element.40.toks0, bf16[24,128,128]{2,1,0:T(8,128)(2,1)S(1)} %get-tuple-element.41.toks1, ...), custom_call_target="tpu_custom_call", output_to_operand_aliasing={{0}: (5, {}), {1}: (6, {})} | custom-call | flops 1 | bytes 1 | tf_op jit(solution)/shard_map/weight_grads/pallas_call | solution.py:346
  74.1 0.7 add_convert_fusion
  (19 shorter events, 0.2 us)
Async XLA Ops:
  0.6 4.9 %collective-permute-start = (bf16[128,1536]{1,0:T(8,128)(2,1)}, bf16[128,1536]{1,0:T(8,128)(2,1)S(1)}, u32[]{:S(2)}, u32[]{:S(2)}) collective-permute-start(bf16[128,1536]{1,0:T(8,128)(2,1)} %cot.3), channel_id=1, source_target_pairs={{0,16},{16,0},{1,17},{17,1},{2,18},{18,2},{3,19},{19,3},{4,20},{20... | collective-permute-start | bytes 1179656 | tf_op jit(solution)/shard_map/ppermute | solution.py:450
  0.8 12.8 %collective-permute-start.1 = (bf16[128,384]{1,0:T(8,128)(2,1)}, bf16[128,384]{1,0:T(8,128)(2,1)S(1)}, u32[]{:S(2)}, u32[]{:S(2)}) collective-permute-start(bf16[128,384]{1,0:T(8,128)(2,1)} %refs_0_.1), channel_id=1, source_target_pairs={{4,0},{5,1},{6,2},{7,3},{0,4},{1,5},{2,6},{3,7},{20,8},{21,9},{22,... | collective-permute-start | bytes 294920 | tf_op jit(solution)/shard_map/ppermute | solution.py:454
  5.5 8.1 %collective-permute-start.3 = (bf16[128,384]{1,0:T(8,128)(2,1)}, bf16[128,384]{1,0:T(8,128)(2,1)S(1)}, u32[]{:S(2)}, u32[]{:S(2)}) collective-permute-start(bf16[128,384]{1,0:T(8,128)(2,1)} %refs_0_.1), channel_id=1, source_target_pairs={{20,0},{21,1},{22,2},{23,3},{16,4},{17,5},{18,6},{19,7},{4,8},{5,9... | collective-permute-start | bytes 294920 | tf_op jit(solution)/shard_map/ppermute | solution.py:454
  5.5 1.0 %copy-start.1 = (bf16[128,384]{1,0:T(8,128)(2,1)S(1)}, bf16[128,384]{1,0:T(8,128)(2,1)}, u32[]{:S(2)}) copy-start(bf16[128,384]{1,0:T(8,128)(2,1)} %refs_0_.1) | copy-start | bytes 294916
  6.5 7.1 %collective-permute-start.4 = (bf16[128,384]{1,0:T(8,128)(2,1)S(1)}, bf16[128,384]{1,0:T(8,128)(2,1)S(1)}, u32[]{:S(2)}, u32[]{:S(2)}) collective-permute-start(bf16[128,384]{1,0:T(8,128)(2,1)S(1)} %join.3), channel_id=1, source_target_pairs={{16,0},{17,1},{18,2},{19,3},{20,4},{21,5},{22,6},{23,7},{0,8},{1,9... | collective-permute-start | bytes 294920 | tf_op jit(solution)/shard_map/ppermute | solution.py:454
  7.0 8.1 %collective-permute-start.2 = (bf16[128,384]{1,0:T(8,128)(2,1)S(1)}, bf16[128,384]{1,0:T(8,128)(2,1)S(1)}, u32[]{:S(2)}, u32[]{:S(2)}) collective-permute-start(bf16[128,384]{1,0:T(8,128)(2,1)S(1)} %join.3), channel_id=1, source_target_pairs={{0,0},{1,1},{2,2},{3,3},{4,4},{5,5},{6,6},{7,7},{16,8},{17,9},{18,... | collective-permute-start | bytes 294920 | tf_op jit(solution)/shard_map/ppermute | solution.py:454
  9.3 0.7 copy-start.2
  15.1 6.7 %collective-permute-start.5 = (bf16[512,384]{1,0:T(8,128)(2,1)S(1)}, bf16[512,384]{1,0:T(8,128)(2,1)S(1)}, u32[]{:S(2)}, u32[]{:S(2)}) collective-permute-start(bf16[512,384]{1,0:T(8,128)(2,1)S(1)} %join.4.refs_1_.own), channel_id=1, source_target_pairs={{0,1},{1,0},{2,3},{3,2},{4,5},{5,4},{6,7},{7,6},{8,9},{9,8},{10,11... | collective-permute-start | bytes 1179656 | tf_op jit(solution)/shard_map/ppermute | solution.py:458
  21.9 8.5 %collective-permute-start.8 = (bf16[512,384]{1,0:T(8,128)(2,1)S(1)}, bf16[512,384]{1,0:T(8,128)(2,1)S(1)}, u32[]{:S(2)}, u32[]{:S(2)}) collective-permute-start(bf16[512,384]{1,0:T(8,128)(2,1)S(1)} %get-tuple-element.32.here), channel_id=1, source_target_pairs={{0,2},{1,3},{2,0},{3,1},{4,6},{5,7},{6,4},{7,5},{8,10},{9,11},{10,... | collective-permute-start | bytes 1179656 | tf_op jit(solution)/shard_map/ppermute | solution.py:461
  23.2 9.9 %collective-permute-start.6 = (bf16[512,384]{1,0:T(8,128)(2,1)S(1)}, bf16[512,384]{1,0:T(8,128)(2,1)S(1)}, u32[]{:S(2)}, u32[]{:S(2)}) collective-permute-start(bf16[512,384]{1,0:T(8,128)(2,1)S(1)} %get-tuple-element.29._.here), channel_id=1, source_target_pairs={{0,2},{1,3},{2,0},{3,1},{4,6},{5,7},{6,4},{7,5},{8,10},{9,11},{10,... | collective-permute-start | bytes 1179656 | tf_op jit(solution)/shard_map/ppermute | solution.py:461
  33.0 3.5 %copy-start = (bf16[128,1536]{1,0:T(8,128)(2,1)S(1)}, bf16[128,1536]{1,0:T(8,128)(2,1)}, u32[]{:S(2)}) copy-start(bf16[128,1536]{1,0:T(8,128)(2,1)} %cot.3) | copy-start | bytes 1179652
  33.0 3.5 %collective-permute-start.9 = (f32[12,128,256]{2,1,0:T(8,128)S(1)}, f32[12,128,256]{2,1,0:T(8,128)S(1)}, u32[]{:S(2)}, u32[]{:S(2)}) collective-permute-start(f32[12,128,256]{2,1,0:T(8,128)S(1)} %get-tuple-element.33.part), channel_id=1, source_target_pairs={{0,16},{16,0},{1,17},{17,1},{2,18},{18,2},{3,19},{19,3},{4,20},{20... | collective-permute-start | bytes 4718600 | tf_op jit(solution)/shard_map/ppermute | solution.py:468
  35.6 5.5 %collective-permute-start.7 = (f32[12,128,256]{2,1,0:T(8,128)S(1)}, f32[12,128,256]{2,1,0:T(8,128)S(1)}, u32[]{:S(2)}, u32[]{:S(2)}) collective-permute-start(f32[12,128,256]{2,1,0:T(8,128)S(1)} %get-tuple-element.31.part), channel_id=1, source_target_pairs={{0,16},{16,0},{1,17},{17,1},{2,18},{18,2},{3,19},{19,3},{4,20},{20... | collective-permute-start | bytes 4718600 | tf_op jit(solution)/shard_map/ppermute | solution.py:468
  39.8 7.0 %collective-permute-start.12 = (bf16[512,384]{1,0:T(8,128)(2,1)S(1)}, bf16[512,384]{1,0:T(8,128)(2,1)S(1)}, u32[]{:S(2)}, u32[]{:S(2)}) collective-permute-start(bf16[512,384]{1,0:T(8,128)(2,1)S(1)} %get-tuple-element.39), channel_id=1, source_target_pairs={{0,2},{1,3},{2,0},{3,1},{4,6},{5,7},{6,4},{7,5},{8,10},{9,11},{10,... | collective-permute-start | bytes 1179656 | tf_op jit(solution)/shard_map/ppermute | solution.py:474
  44.7 4.9 %collective-permute-start.11 = (bf16[256,384]{1,0:T(8,128)(2,1)S(1)}, bf16[256,384]{1,0:T(8,128)(2,1)S(1)}, u32[]{:S(2)}, u32[]{:S(2)}) collective-permute-start(bf16[256,384]{1,0:T(8,128)(2,1)S(1)} %get-tuple-element.50), channel_id=1, source_target_pairs={{0,2},{1,3},{2,0},{3,1},{4,6},{5,7},{6,4},{7,5},{8,10},{9,11},{10,... | collective-permute-start | bytes 589832 | tf_op jit(solution)/shard_map/ppermute | solution.py:475
  46.9 5.7 %collective-permute-start.14 = (bf16[256,384]{1,0:T(8,128)(2,1)S(1)}, bf16[256,384]{1,0:T(8,128)(2,1)S(1)}, u32[]{:S(2)}, u32[]{:S(2)}) collective-permute-start(bf16[256,384]{1,0:T(8,128)(2,1)S(1)} %add.19.refs_2_), channel_id=1, source_target_pairs={{0,1},{1,0},{2,3},{3,2},{4,5},{5,4},{6,7},{7,6},{8,9},{9,8},{10,11... | collective-permute-start | bytes 589832 | tf_op jit(solution)/shard_map/ppermute | solution.py:477
  48.2 13.3 %collective-permute-start.10 = (bf16[256,384]{1,0:T(8,128)(2,1)S(1)}, bf16[256,384]{1,0:T(8,128)(2,1)S(1)}, u32[]{:S(2)}, u32[]{:S(2)}) collective-permute-start(bf16[256,384]{1,0:T(8,128)(2,1)S(1)} %get-tuple-element.51), channel_id=1, source_target_pairs={{0,2},{1,3},{2,0},{3,1},{4,6},{5,7},{6,4},{7,5},{8,10},{9,11},{10,... | collective-permute-start | bytes 589832 | tf_op jit(solution)/shard_map/ppermute | solution.py:475
  49.6 11.8 %collective-permute-start.13 = (bf16[256,384]{1,0:T(8,128)(2,1)S(1)}, bf16[256,384]{1,0:T(8,128)(2,1)S(1)}, u32[]{:S(2)}, u32[]{:S(2)}) collective-permute-start(bf16[256,384]{1,0:T(8,128)(2,1)S(1)} %add.20.refs_3_), channel_id=1, source_target_pairs={{0,1},{1,0},{2,3},{3,2},{4,5},{5,4},{6,7},{7,6},{8,9},{9,8},{10,11... | collective-permute-start | bytes 589832 | tf_op jit(solution)/shard_map/ppermute | solution.py:479
  52.7 18.5 %collective-permute-start.16 = (bf16[128,384]{1,0:T(8,128)(2,1)S(1)}, bf16[128,384]{1,0:T(8,128)(2,1)S(1)}, u32[]{:S(2)}, u32[]{:S(2)}) collective-permute-start(bf16[128,384]{1,0:T(8,128)(2,1)S(1)} %get-tuple-element.52), channel_id=1, source_target_pairs={{0,0},{1,1},{2,2},{3,3},{4,4},{5,5},{6,6},{7,7},{8,16},{9,17},{10,... | collective-permute-start | bytes 294920 | tf_op jit(solution)/shard_map/ppermute | solution.py:486
  59.7 11.5 %collective-permute-start.15 = (bf16[128,384]{1,0:T(8,128)(2,1)S(1)}, bf16[128,384]{1,0:T(8,128)(2,1)S(1)}, u32[]{:S(2)}, u32[]{:S(2)}) collective-permute-start(bf16[128,384]{1,0:T(8,128)(2,1)S(1)} %get-tuple-element.53), channel_id=1, source_target_pairs={{0,4},{1,5},{2,6},{3,7},{4,0},{5,1},{6,2},{7,3},{8,20},{9,21},{10,... | collective-permute-start | bytes 294920 | tf_op jit(solution)/shard_map/ppermute | solution.py:486
  61.6 12.6 %collective-permute-start.17 = (bf16[128,384]{1,0:T(8,128)(2,1)S(1)}, bf16[128,384]{1,0:T(8,128)(2,1)S(1)}, u32[]{:S(2)}, u32[]{:S(2)}) collective-permute-start(bf16[128,384]{1,0:T(8,128)(2,1)S(1)} %get-tuple-element.54), channel_id=1, source_target_pairs={{0,20},{1,21},{2,22},{3,23},{4,16},{5,17},{6,18},{7,19},{8,4},{9,5... | collective-permute-start | bytes 294920 | tf_op jit(solution)/shard_map/ppermute | solution.py:486
  61.6 12.5 %collective-permute-start.18 = (bf16[128,384]{1,0:T(8,128)(2,1)S(1)}, bf16[128,384]{1,0:T(8,128)(2,1)S(1)}, u32[]{:S(2)}, u32[]{:S(2)}) collective-permute-start(bf16[128,384]{1,0:T(8,128)(2,1)S(1)} %get-tuple-element.55), channel_id=1, source_target_pairs={{0,16},{1,17},{2,18},{3,19},{4,20},{5,21},{6,22},{7,23},{8,0},{9,1... | collective-permute-start | bytes 294920 | tf_op jit(solution)/shard_map/ppermute | solution.py:486

commit v3 on v2

--- a/solution.py
+++ b/solution.py
@@ -288,7 +288,7 @@
         for k in range(kept):
             acc[listed[j, k]] += spread[:, k * BLOCK : (k + 1) * BLOCK]
 
-    step = 3
+    step = 4
     for turned, first, number in ((turned_a, 0, cut), (turned_b, cut, columns - cut)):
 
         def steps(g, _, turned=turned, first=first):
@@ -321,7 +321,8 @@
     )(listed, *map(in_vmem, packed), in_vmem(part), in_vmem(other), cot, other_cot, *extra)
 
 
-def weight_kernel(first, count, listed, toks0, toks1, grads0, grads1, gate_in, up_in, _, gate_out, up_out, stage, sems):
+def weight_kernel(first, count, listed, toks0, toks1, grads0, grads1, gate_in, up_in, _, gate_out, up_out, token, stage, sems):
+    token[...] = jnp.zeros_like(token)
     kept, slots = kept_of(listed), stage.shape[0]
     for j in range(first, first + count):
         slot = (j - first) % slots
@@ -345,15 +346,32 @@
     slots = min(6, count)
     return pl.pallas_call(
         functools.partial(weight_kernel, first, count),
-        out_shape=[pltpu.HBM(grad.shape, F32) for grad in written],
+        out_shape=[pltpu.HBM(grad.shape, F32) for grad in written] + [VMEM((8, BLOCK), F32)],
         in_specs=[spec(SMEM)] + [spec(VMEM)] * 4 + [spec(pltpu.HBM)] * 2 + [spec(pl.ANY)],
-        out_specs=[spec(pltpu.HBM)] * 2,
+        out_specs=[spec(pltpu.HBM)] * 2 + [spec(VMEM)],
         scratch_shapes=[VMEM((slots, kept_of(listed) * BLOCK, 2 * BLOCK), F32), pltpu.SemaphoreType.DMA((slots,))],
         input_output_aliases={5: 0, 6: 1},
         compiler_params=pltpu.CompilerParams(vmem_limit_bytes=16 * MIB),
         cost_estimate=SMALL,
         name="weight_grads",
     )(listed, *map(in_vmem, tokens), *map(in_vmem, grads), *map(in_hbm, written), later_than)
+
+
+def seal_kernel(written, _, same):
+    pass
+
+
+def seal(written, later_than):
+    return pl.pallas_call(
+        seal_kernel,
+        out_shape=pltpu.HBM(written.shape, F32),
+        in_specs=[spec(pltpu.HBM), spec(pl.ANY)],
+        out_specs=spec(pltpu.HBM),
+        input_output_aliases={0: 0},
+        compiler_params=pltpu.CompilerParams(vmem_limit_bytes=4 * MIB),
+        cost_estimate=SMALL,
+        name="seal",
+    )(in_hbm(written), later_than)
 
 
 def add_kernel(firsts, *refs):
@@ -445,7 +463,7 @@
     swap = [(0, 1), (1, 0)]
     width = tokens.shape[1]
     columns, segs = gate_weight.shape[1] // BLOCK, gate_weight.shape[0] // BLOCK
-    cut = columns // 2
+    cut = columns // 3
     listed = places(block_mask.T, segs)
     other_cot = lax.ppermute(cotangent, "row", swap)
 
@@ -473,11 +491,15 @@
     pair = 2 * BLOCK
     got_a = lax.ppermute(far_a, AXES, FAR)
     first_b, direct_b = lax.ppermute(far_b[:pair], AXES, FAR), lax.ppermute(far_b[pair:], AXES, FAR)
-    sum_a = add((0, near_a), (0, got_a), later_than=far_b)
+    lead = columns // 6
+    *written, token = weight_grads(0, lead, listed, toks, grads, written, far_b)
+    sum_a = add((0, near_a), (0, got_a), later_than=token)
     carried_a = lax.ppermute(sum_a, AXES, NEAR)
     sum_b = add((0, near_b), (0, first_b), later_than=sum_a)
     carried_b = lax.ppermute(sum_b, AXES, NEAR)
-    here_a = add((pair, near_a), (pair, got_a), (0, carried_a), later_than=sum_b)
+    middle = columns // 4
+    *written, token = weight_grads(lead, middle, listed, toks, grads, written, sum_b)
+    here_a = add((pair, near_a), (pair, got_a), (0, carried_a), later_than=token)
     here_b = add((pair, near_b), (0, direct_b), (0, carried_b), later_than=here_a)
 
     def homeward(turn, here):
@@ -487,9 +509,9 @@
 
     home_a, home_b = list(homeward(0, here_a)), list(homeward(1, here_b))
     joined_a = join(*home_a, later_than=here_b)
-    lead = columns * 5 // 6
-    written = weight_grads(0, lead, listed, toks, grads, written, here_b)
-    written = weight_grads(lead, columns - lead, listed, toks, grads, written, joined_a)
+    last = lead + middle
+    *written, _ = weight_grads(last, columns - last, listed, toks, grads, written, here_b)
+    written[0] = seal(written[0], joined_a)
     total = sum(piece.astype(F32) for piece in (joined_a[:BLOCK], joined_a[BLOCK:], *home_b))
     return hidden, total.astype(BF16), *written
 

time: 75.2 us -> 72.9 us (0.969)
  the two profiles are of different devices: /device:TPU:1 before, /device:TPU:0 now
where the time goes in v3:
time: 72.9 us; the launch traced here: 72.5 us
  Pallas kernels  37.3 us (51%)
  starting transfers between devices  25.3 us (35%)
  waiting for transfers between devices  5.83 us (8%)
  local copies, waits for them, and re-layouts  2.45 us (3%)
  between operations  0.9 us (1%)
    pallas_call x3, Pallas kernels, weight_grads(): pl.pallas_call(functools.partial(weight_kernel, first, count), out_shape=...  11.7 us
    ppermute x4, starting transfers between devices, homeward(): yield lax.ppermute(here[k0 * BLOCK:(k0 + 1) * BLOCK], AXES, back)  7.07 us
    pallas_call x1, Pallas kernels, transposed(): pl.pallas_call(turn_kernel, out_shape=[VMEM((columns, wide, rows), BF16)]...  7.01 us
    pallas_call x2, Pallas kernels, backward(): pl.pallas_call(functools.partial(backward_kernel, turn), out_shape=[VMEM(...  6.58 us
    pallas_call x2, Pallas kernels, pack(): pl.pallas_call(functools.partial(pack_kernel, first, turning), out_shape=...  6.23 us
    ppermute x4, starting transfers between devices, chip_body(): lax.ppermute(block, AXES, z_pairs(turn, k0))  6.2 us
    pallas_call x2, Pallas kernels, forward(): pl.pallas_call(functools.partial(forward_kernel, turn), out_shape=[VMEM((...  4.98 us
    ppermute x1, waiting for transfers between devices, chip_body(): near = lax.ppermute(own, AXES, NEAR)  2.63 us
  transfers between devices with their start and end apart: 19, of which 5 were waited for; matrix products, arithmetic and copies ran while one was open for 1% of the time, Pallas kernels for 51%

profile of v3, /device:TPU:0, one launch (start us, length us, event | category | flops | bytes accessed | tf_op | source)
XLA Modules:
  0.0 72.5 jit_solution(3854476117432331516)
XLA Ops:
  0.6 0.5 collective-permute-start
  1.1 2.7 %collective-permute-start.1 = (bf16[128,384]{1,0:T(8,128)(2,1)}, bf16[128,384]{1,0:T(8,128)(2,1)S(1)}, u32[]{:S(2)}, u32[]{:S(2)}) collective-permute-start(bf16[128,384]{1,0:T(8,128)(2,1)} %refs_0_.1), channel_id=1, source_target_pairs={{4,0},{5,1},{6,2},{7,3},{0,4},{1,5},{2,6},{3,7},{20,8},{21,9},{22,... | collective-permute-start | bytes 294920 | tf_op jit(solution)/shard_map/ppermute | solution.py:472
  3.8 2.1 %collective-permute-start.3 = (bf16[128,384]{1,0:T(8,128)(2,1)}, bf16[128,384]{1,0:T(8,128)(2,1)S(1)}, u32[]{:S(2)}, u32[]{:S(2)}) collective-permute-start(bf16[128,384]{1,0:T(8,128)(2,1)} %refs_0_.1), channel_id=1, source_target_pairs={{20,0},{21,1},{22,2},{23,3},{16,4},{17,5},{18,6},{19,7},{4,8},{5,9... | collective-permute-start | bytes 294920 | tf_op jit(solution)/shard_map/ppermute | solution.py:472
  5.9 0.0 collective-permute-done.refs_0_._.other_cot
  5.9 0.9 %copy-done.1 = bf16[128,384]{1,0:T(8,128)(2,1)S(1)} copy-done((bf16[128,384]{1,0:T(8,128)(2,1)S(1)}, bf16[128,384]{1,0:T(8,128)(2,1)}, u32[]{:S(2)}) %copy-start.1) | copy-done | bytes 98328
  6.8 0.8 %collective-permute-start.4 = (bf16[128,384]{1,0:T(8,128)(2,1)S(1)}, bf16[128,384]{1,0:T(8,128)(2,1)S(1)}, u32[]{:S(2)}, u32[]{:S(2)}) collective-permute-start(bf16[128,384]{1,0:T(8,128)(2,1)S(1)} %join.3), channel_id=1, source_target_pairs={{16,0},{17,1},{18,2},{19,3},{20,4},{21,5},{22,6},{23,7},{0,8},{1,9... | collective-permute-start | bytes 294920 | tf_op jit(solution)/shard_map/ppermute | solution.py:472
  7.6 0.7 collective-permute-start.2
  8.3 0.0 copy-start.2
  8.3 0.7 copy-done.2
  9.0 0.4 places.1.listed
  9.4 2.6 %pack.2._.refs_0_.packed_a = bf16[4,1536,256]{2,1,0:T(8,128)(2,1)S(1)} custom-call(s32[12,32]{1,0:T(8,128)S(1)} %places.1.listed, bf16[3072,1536]{1,0:T(8,128)(2,1)} %gate_w.3, bf16[3072,1536]{1,0:T(8,128)(2,1)} %up_w.3, bf16[128,1536]{1,0:T(8,128)(2,1)S(1)} %collective-permute-done.refs_0_._.other_cot), custom_call_target="tpu_custom_call" | custom-call | flops 1 | bytes 1 | tf_op jit(solution)/shard_map/pack/pallas_call | solution.py:198
  12.0 0.0 collective-permute-done.1.refs_0_
  12.0 0.0 collective-permute-done.3.refs_2_
  12.1 1.6 %collective-permute-start.5 = (bf16[512,384]{1,0:T(8,128)(2,1)S(1)}, bf16[512,384]{1,0:T(8,128)(2,1)S(1)}, u32[]{:S(2)}, u32[]{:S(2)}) collective-permute-start(bf16[512,384]{1,0:T(8,128)(2,1)S(1)} %join.4.refs_1_.own), channel_id=1, source_target_pairs={{0,1},{1,0},{2,3},{3,2},{4,5},{5,4},{6,7},{7,6},{8,9},{9,8},{10,11... | collective-permute-start | bytes 1179656 | tf_op jit(solution)/shard_map/ppermute | solution.py:476
  13.6 3.6 %pack.3 = (bf16[8,1536,256]{2,1,0:T(8,128)(2,1)S(1)}, bf16[4,256,1536]{2,1,0:T(8,128)(2,1)S(1)}) custom-call(s32[12,32]{1,0:T(8,128)S(1)} %places.1.listed, bf16[3072,1536]{1,0:T(8,128)(2,1)} %gate_w.3, bf16[3072,1536]{1,0:T(8,128)(2,1)} %up_w.3, bf16[4,1536,256]{2,1,0:T(8,128)(2,1)S(1)} %pack.2._.refs_0_.packed_a, bf16[512,384]{1,0:T(8,128)(2,1)S(1)} %join.4.refs_1_.own), custom_call_target="tpu_custom_call" | custom-call | flops 1 | bytes 1 | tf_op jit(solution)/shard_map/pack/pallas_call | solution.py:198
  17.3 2.6 %collective-permute-done.5.near = bf16[512,384]{1,0:T(8,128)(2,1)S(1)} collective-permute-done((bf16[512,384]{1,0:T(8,128)(2,1)S(1)}, bf16[512,384]{1,0:T(8,128)(2,1)S(1)}, u32[]{:S(2)}, u32[]{:S(2)}) %collective-permute-start.5) | collective-permute-done | bytes 393248 | tf_op jit(solution)/shard_map/ppermute | solution.py:476
  19.9 0.1 mix.1
  20.0 1.6 %collective-permute-start.8 = (bf16[512,384]{1,0:T(8,128)(2,1)S(1)}, bf16[512,384]{1,0:T(8,128)(2,1)S(1)}, u32[]{:S(2)}, u32[]{:S(2)}) collective-permute-start(bf16[512,384]{1,0:T(8,128)(2,1)S(1)} %get-tuple-element.36.here), channel_id=1, source_target_pairs={{0,2},{1,3},{2,0},{3,1},{4,6},{5,7},{6,4},{7,5},{8,10},{9,11},{10,... | collective-permute-start | bytes 1179656 | tf_op jit(solution)/shard_map/ppermute | solution.py:479
  21.6 0.5 collective-permute-start.6
  22.1 7.0 %turn.1 = (bf16[8,256,1536]{2,1,0:T(8,128)(2,1)S(1)}, f32[3072,1536]{1,0:T(8,128)}, f32[3072,1536]{1,0:T(8,128)}) custom-call(s32[12,32]{1,0:T(8,128)S(1)} %places.1.listed, bf16[8,1536,256]{2,1,0:T(8,128)(2,1)S(1)} %get-tuple-element.32._.packed.packed_b, bf16[512,384]{1,0:T(8,128)(2,1)S(1)} %get-tuple-element.33._.here), custom_call_target="tpu_custom_call" | custom-call | flops 1 | bytes 1 | tf_op jit(solution)/shard_map/turn/pallas_call | solution.py:450
  29.1 2.5 %forward.3 = (f32[12,128,256]{2,1,0:T(8,128)S(1)}, bf16[24,128,128]{2,1,0:T(8,128)(2,1)S(1)}) custom-call(s32[12,32]{1,0:T(8,128)S(1)} %places.1.listed, bf16[4,1536,256]{2,1,0:T(8,128)(2,1)S(1)} %pack.2._.refs_0_.packed_a, bf16[8,1536,256]{2,1,0:T(8,128)(2,1)S(1)} %get-tuple-element.32._.packed.packed_b, bf16[512,384]{1,0:T(8,128)(2,1)S(1)} %get-tuple-element.36.here, ...), custom_call_target="tpu_custom_call" | custom-call | flops 1 | bytes 1 | tf_op jit(solution)/shard_map/forward/pallas_call | solution.py:253
  31.6 0.0 copy-start
  31.6 1.9 %collective-permute-start.9 = (f32[12,128,256]{2,1,0:T(8,128)S(1)}, f32[12,128,256]{2,1,0:T(8,128)S(1)}, u32[]{:S(2)}, u32[]{:S(2)}) collective-permute-start(f32[12,128,256]{2,1,0:T(8,128)S(1)} %get-tuple-element.37.part), channel_id=1, source_target_pairs={{0,16},{16,0},{1,17},{17,1},{2,18},{18,2},{3,19},{19,3},{4,20},{20... | collective-permute-start | bytes 4718600 | tf_op jit(solution)/shard_map/ppermute | solution.py:486
  33.5 2.5 %forward.2 = (f32[12,128,256]{2,1,0:T(8,128)S(1)}, bf16[24,128,128]{2,1,0:T(8,128)(2,1)S(1)}) custom-call(s32[12,32]{1,0:T(8,128)S(1)} %places.1.listed, bf16[4,1536,256]{2,1,0:T(8,128)(2,1)S(1)} %pack.2._.refs_0_.packed_a, bf16[8,1536,256]{2,1,0:T(8,128)(2,1)S(1)} %get-tuple-element.32._.packed.packed_b, bf16[512,384]{1,0:T(8,128)(2,1)S(1)} %get-tuple-element.33._.here, ...), custom_call_target="tpu_custom_call" | custom-call | flops 1 | bytes 1 | tf_op jit(solution)/shard_map/forward/pallas_call | solution.py:253
  36.0 0.1 collective-permute-start.7
  36.1 0.4 collective-permute-done.9.other
  36.5 3.3 %backward.2 = (bf16[128,1536]{1,0:T(8,128)(2,1)S(1)}, bf16[12,128,256]{2,1,0:T(8,128)(2,1)S(1)}, bf16[512,384]{1,0:T(8,128)(2,1)S(1)}, bf16[512,384]{1,0:T(8,128)(2,1)S(1)}) custom-call(s32[12,32]{1,0:T(8,128)S(1)} %places.1.listed, bf16[4,256,1536]{2,1,0:T(8,128)(2,1)S(1)} %get-tuple-element.31.turned_a, ...), custom_call_target="tpu_custom_call" | custom-call | flops 1 | bytes 1 | tf_op jit(solution)/shard_map/backward/pallas_call | solution.py:311
  39.8 1.6 %collective-permute-start.12 = (bf16[512,384]{1,0:T(8,128)(2,1)S(1)}, bf16[512,384]{1,0:T(8,128)(2,1)S(1)}, u32[]{:S(2)}, u32[]{:S(2)}) collective-permute-start(bf16[512,384]{1,0:T(8,128)(2,1)S(1)} %get-tuple-element.43), channel_id=1, source_target_pairs={{0,2},{1,3},{2,0},{3,1},{4,6},{5,7},{6,4},{7,5},{8,10},{9,11},{10,... | collective-permute-start | bytes 1179656 | tf_op jit(solution)/shard_map/ppermute | solution.py:492
  41.4 3.3 %backward.3 = (bf16[128,1536]{1,0:T(8,128)(2,1)S(1)}, bf16[12,128,256]{2,1,0:T(8,128)(2,1)S(1)}, bf16[512,384]{1,0:T(8,128)(2,1)S(1)}, bf16[512,384]{1,0:T(8,128)(2,1)S(1)}) custom-call(s32[12,32]{1,0:T(8,128)S(1)} %places.1.listed, bf16[4,256,1536]{2,1,0:T(8,128)(2,1)S(1)} %get-tuple-element.31.turned_a, ...), custom_call_target="tpu_custom_call" | custom-call | flops 1 | bytes 1 | tf_op jit(solution)/shard_map/backward/pallas_call | solution.py:311
  44.8 0.6 collective-permute-start.11
  45.3 2.9 %weight_grads.3 = (f32[3072,1536]{1,0:T(8,128)}, f32[3072,1536]{1,0:T(8,128)}, f32[8,128]{1,0:T(8,128)S(1)}) custom-call(s32[12,32]{1,0:T(8,128)S(1)} %places.1.listed, bf16[24,128,128]{2,1,0:T(8,128)(2,1)S(1)} %get-tuple-element.44.toks0, bf16[24,128,128]{2,1,0:T(8,128)(2,1)S(1)} %get-tuple-element.45.toks1, ...), custom_call_target="tpu_custom_call", output_to_operand_aliasing={{0}: (5, {}), {1}: (6, {})} | custom-call | flops 1 | bytes 1 | tf_op jit(solution)/shard_map/weight_grads/pallas_call | solution.py:347
  48.2 0.1 add.19.refs_2_
  48.3 1.6 %collective-permute-start.14 = (bf16[256,384]{1,0:T(8,128)(2,1)S(1)}, bf16[256,384]{1,0:T(8,128)(2,1)S(1)}, u32[]{:S(2)}, u32[]{:S(2)}) collective-permute-start(bf16[256,384]{1,0:T(8,128)(2,1)S(1)} %add.19.refs_2_), channel_id=1, source_target_pairs={{0,1},{1,0},{2,3},{3,2},{4,5},{5,4},{6,7},{7,6},{8,9},{9,8},{10,11... | collective-permute-start | bytes 589832 | tf_op jit(solution)/shard_map/ppermute | solution.py:497
  49.9 1.5 %collective-permute-start.10 = (bf16[256,384]{1,0:T(8,128)(2,1)S(1)}, bf16[256,384]{1,0:T(8,128)(2,1)S(1)}, u32[]{:S(2)}, u32[]{:S(2)}) collective-permute-start(bf16[256,384]{1,0:T(8,128)(2,1)S(1)} %get-tuple-element.59), channel_id=1, source_target_pairs={{0,2},{1,3},{2,0},{3,1},{4,6},{5,7},{6,4},{7,5},{8,10},{9,11},{10,... | collective-permute-start | bytes 589832 | tf_op jit(solution)/shard_map/ppermute | solution.py:493
  51.4 0.1 add.20._
  51.4 0.7 collective-permute-start.13
  52.1 3.2 %weight_grads.4 = (f32[3072,1536]{1,0:T(8,128)}, f32[3072,1536]{1,0:T(8,128)}, f32[8,128]{1,0:T(8,128)S(1)}) custom-call(s32[12,32]{1,0:T(8,128)S(1)} %places.1.listed, bf16[24,128,128]{2,1,0:T(8,128)(2,1)S(1)} %get-tuple-element.44.toks0, bf16[24,128,128]{2,1,0:T(8,128)(2,1)S(1)} %get-tuple-element.45.toks1, ...), custom_call_target="tpu_custom_call", output_to_operand_aliasing={{0}: (5, {}), {1}: (6, {})} | custom-call | flops 1 | bytes 1 | tf_op jit(solution)/shard_map/weight_grads/pallas_call | solution.py:347
  55.3 0.7 %collective-permute-done.14.refs_2_ = bf16[256,384]{1,0:T(8,128)(2,1)S(1)} collective-permute-done((bf16[256,384]{1,0:T(8,128)(2,1)S(1)}, bf16[256,384]{1,0:T(8,128)(2,1)S(1)}, u32[]{:S(2)}, u32[]{:S(2)}) %collective-permute-start.14) | collective-permute-done | bytes 196640 | tf_op jit(solution)/shard_map/ppermute | solution.py:497
  56.0 0.1 add.21.refs_3_
  56.2 0.7 collective-permute-start.16
  56.8 1.3 %collective-permute-start.15 = (bf16[128,384]{1,0:T(8,128)(2,1)S(1)}, bf16[128,384]{1,0:T(8,128)(2,1)S(1)}, u32[]{:S(2)}, u32[]{:S(2)}) collective-permute-start(bf16[128,384]{1,0:T(8,128)(2,1)S(1)} %get-tuple-element.61), channel_id=1, source_target_pairs={{0,4},{1,5},{2,6},{3,7},{4,0},{5,1},{6,2},{7,3},{8,20},{9,21},{10,... | collective-permute-start | bytes 294920 | tf_op jit(solution)/shard_map/ppermute | solution.py:508
  58.1 0.1 collective-permute-done.13.refs_2_
  58.2 0.1 add.22._
  58.4 5.1 %collective-permute-start.17 = (bf16[128,384]{1,0:T(8,128)(2,1)S(1)}, bf16[128,384]{1,0:T(8,128)(2,1)S(1)}, u32[]{:S(2)}, u32[]{:S(2)}) collective-permute-start(bf16[128,384]{1,0:T(8,128)(2,1)S(1)} %get-tuple-element.62), channel_id=1, source_target_pairs={{0,20},{1,21},{2,22},{3,23},{4,16},{5,17},{6,18},{7,19},{8,4},{9,5... | collective-permute-start | bytes 294920 | tf_op jit(solution)/shard_map/ppermute | solution.py:508
  63.5 0.7 %copy.23 = bf16[128,1536]{1,0:T(8,128)(2,1)} copy(bf16[128,1536]{1,0:T(8,128)(2,1)S(1)} %get-tuple-element.64) | data formatting | bytes 786432
  64.2 5.7 %weight_grads.5 = (f32[3072,1536]{1,0:T(8,128)}, f32[3072,1536]{1,0:T(8,128)}, f32[8,128]{1,0:T(8,128)}) custom-call(s32[12,32]{1,0:T(8,128)S(1)} %places.1.listed, bf16[24,128,128]{2,1,0:T(8,128)(2,1)S(1)} %get-tuple-element.44.toks0, bf16[24,128,128]{2,1,0:T(8,128)(2,1)S(1)} %get-tuple-element.45.toks1, ...), custom_call_target="tpu_custom_call", output_to_operand_aliasing={{0}: (5, {}), {1}: (6, {})} | custom-call | flops 1 | bytes 1 | tf_op jit(solution)/shard_map/weight_grads/pallas_call | solution.py:347
  70.0 1.8 %collective-permute-done.18 = bf16[128,384]{1,0:T(8,128)(2,1)S(1)} collective-permute-done((bf16[128,384]{1,0:T(8,128)(2,1)S(1)}, bf16[128,384]{1,0:T(8,128)(2,1)S(1)}, u32[]{:S(2)}, u32[]{:S(2)}) %collective-permute-start.18) | collective-permute-done | bytes 98336 | tf_op jit(solution)/shard_map/ppermute | solution.py:508
  71.8 0.7 add_convert_fusion
  (21 shorter events, 0.2 us)
Async XLA Ops:
  0.6 5.3 %collective-permute-start = (bf16[128,1536]{1,0:T(8,128)(2,1)}, bf16[128,1536]{1,0:T(8,128)(2,1)S(1)}, u32[]{:S(2)}, u32[]{:S(2)}) collective-permute-start(bf16[128,1536]{1,0:T(8,128)(2,1)} %cot.3), channel_id=1, source_target_pairs={{0,16},{16,0},{1,17},{17,1},{2,18},{18,2},{3,19},{19,3},{4,20},{20... | collective-permute-start | bytes 1179656 | tf_op jit(solution)/shard_map/ppermute | solution.py:468
  1.1 10.8 %collective-permute-start.1 = (bf16[128,384]{1,0:T(8,128)(2,1)}, bf16[128,384]{1,0:T(8,128)(2,1)S(1)}, u32[]{:S(2)}, u32[]{:S(2)}) collective-permute-start(bf16[128,384]{1,0:T(8,128)(2,1)} %refs_0_.1), channel_id=1, source_target_pairs={{4,0},{5,1},{6,2},{7,3},{0,4},{1,5},{2,6},{3,7},{20,8},{21,9},{22,... | collective-permute-start | bytes 294920 | tf_op jit(solution)/shard_map/ppermute | solution.py:472
  3.8 8.2 %collective-permute-start.3 = (bf16[128,384]{1,0:T(8,128)(2,1)}, bf16[128,384]{1,0:T(8,128)(2,1)S(1)}, u32[]{:S(2)}, u32[]{:S(2)}) collective-permute-start(bf16[128,384]{1,0:T(8,128)(2,1)} %refs_0_.1), channel_id=1, source_target_pairs={{20,0},{21,1},{22,2},{23,3},{16,4},{17,5},{18,6},{19,7},{4,8},{5,9... | collective-permute-start | bytes 294920 | tf_op jit(solution)/shard_map/ppermute | solution.py:472
  5.9 0.9 %copy-start.1 = (bf16[128,384]{1,0:T(8,128)(2,1)S(1)}, bf16[128,384]{1,0:T(8,128)(2,1)}, u32[]{:S(2)}) copy-start(bf16[128,384]{1,0:T(8,128)(2,1)} %refs_0_.1) | copy-start | bytes 294916
  6.8 5.2 %collective-permute-start.4 = (bf16[128,384]{1,0:T(8,128)(2,1)S(1)}, bf16[128,384]{1,0:T(8,128)(2,1)S(1)}, u32[]{:S(2)}, u32[]{:S(2)}) collective-permute-start(bf16[128,384]{1,0:T(8,128)(2,1)S(1)} %join.3), channel_id=1, source_target_pairs={{16,0},{17,1},{18,2},{19,3},{20,4},{21,5},{22,6},{23,7},{0,8},{1,9... | collective-permute-start | bytes 294920 | tf_op jit(solution)/shard_map/ppermute | solution.py:472
  7.6 4.4 %collective-permute-start.2 = (bf16[128,384]{1,0:T(8,128)(2,1)S(1)}, bf16[128,384]{1,0:T(8,128)(2,1)S(1)}, u32[]{:S(2)}, u32[]{:S(2)}) collective-permute-start(bf16[128,384]{1,0:T(8,128)(2,1)S(1)} %join.3), channel_id=1, source_target_pairs={{0,0},{1,1},{2,2},{3,3},{4,4},{5,5},{6,6},{7,7},{16,8},{17,9},{18,... | collective-permute-start | bytes 294920 | tf_op jit(solution)/shard_map/ppermute | solution.py:472
  8.3 0.7 copy-start.2
  12.1 7.8 %collective-permute-start.5 = (bf16[512,384]{1,0:T(8,128)(2,1)S(1)}, bf16[512,384]{1,0:T(8,128)(2,1)S(1)}, u32[]{:S(2)}, u32[]{:S(2)}) collective-permute-start(bf16[512,384]{1,0:T(8,128)(2,1)S(1)} %join.4.refs_1_.own), channel_id=1, source_target_pairs={{0,1},{1,0},{2,3},{3,2},{4,5},{5,4},{6,7},{7,6},{8,9},{9,8},{10,11... | collective-permute-start | bytes 1179656 | tf_op jit(solution)/shard_map/ppermute | solution.py:476
  20.0 9.1 %collective-permute-start.8 = (bf16[512,384]{1,0:T(8,128)(2,1)S(1)}, bf16[512,384]{1,0:T(8,128)(2,1)S(1)}, u32[]{:S(2)}, u32[]{:S(2)}) collective-permute-start(bf16[512,384]{1,0:T(8,128)(2,1)S(1)} %get-tuple-element.36.here), channel_id=1, source_target_pairs={{0,2},{1,3},{2,0},{3,1},{4,6},{5,7},{6,4},{7,5},{8,10},{9,11},{10,... | collective-permute-start | bytes 1179656 | tf_op jit(solution)/shard_map/ppermute | solution.py:479
  21.6 11.9 %collective-permute-start.6 = (bf16[512,384]{1,0:T(8,128)(2,1)S(1)}, bf16[512,384]{1,0:T(8,128)(2,1)S(1)}, u32[]{:S(2)}, u32[]{:S(2)}) collective-permute-start(bf16[512,384]{1,0:T(8,128)(2,1)S(1)} %get-tuple-element.33._.here), channel_id=1, source_target_pairs={{0,2},{1,3},{2,0},{3,1},{4,6},{5,7},{6,4},{7,5},{8,10},{9,11},{10,... | collective-permute-start | bytes 1179656 | tf_op jit(solution)/shard_map/ppermute | solution.py:479
  31.6 5.0 %copy-start = (bf16[128,1536]{1,0:T(8,128)(2,1)S(1)}, bf16[128,1536]{1,0:T(8,128)(2,1)}, u32[]{:S(2)}) copy-start(bf16[128,1536]{1,0:T(8,128)(2,1)} %cot.3) | copy-start | bytes 1179652
  31.6 4.9 %collective-permute-start.9 = (f32[12,128,256]{2,1,0:T(8,128)S(1)}, f32[12,128,256]{2,1,0:T(8,128)S(1)}, u32[]{:S(2)}, u32[]{:S(2)}) collective-permute-start(f32[12,128,256]{2,1,0:T(8,128)S(1)} %get-tuple-element.37.part), channel_id=1, source_target_pairs={{0,16},{16,0},{1,17},{17,1},{2,18},{18,2},{3,19},{19,3},{4,20},{20... | collective-permute-start | bytes 4718600 | tf_op jit(solution)/shard_map/ppermute | solution.py:486
  36.0 5.4 %collective-permute-start.7 = (f32[12,128,256]{2,1,0:T(8,128)S(1)}, f32[12,128,256]{2,1,0:T(8,128)S(1)}, u32[]{:S(2)}, u32[]{:S(2)}) collective-permute-start(f32[12,128,256]{2,1,0:T(8,128)S(1)} %get-tuple-element.35.part), channel_id=1, source_target_pairs={{0,16},{16,0},{1,17},{17,1},{2,18},{18,2},{3,19},{19,3},{4,20},{20... | collective-permute-start | bytes 4718600 | tf_op jit(solution)/shard_map/ppermute | solution.py:486
  39.8 8.4 %collective-permute-start.12 = (bf16[512,384]{1,0:T(8,128)(2,1)S(1)}, bf16[512,384]{1,0:T(8,128)(2,1)S(1)}, u32[]{:S(2)}, u32[]{:S(2)}) collective-permute-start(bf16[512,384]{1,0:T(8,128)(2,1)S(1)} %get-tuple-element.43), channel_id=1, source_target_pairs={{0,2},{1,3},{2,0},{3,1},{4,6},{5,7},{6,4},{7,5},{8,10},{9,11},{10,... | collective-permute-start | bytes 1179656 | tf_op jit(solution)/shard_map/ppermute | solution.py:492
  44.8 6.6 %collective-permute-start.11 = (bf16[256,384]{1,0:T(8,128)(2,1)S(1)}, bf16[256,384]{1,0:T(8,128)(2,1)S(1)}, u32[]{:S(2)}, u32[]{:S(2)}) collective-permute-start(bf16[256,384]{1,0:T(8,128)(2,1)S(1)} %get-tuple-element.58), channel_id=1, source_target_pairs={{0,2},{1,3},{2,0},{3,1},{4,6},{5,7},{6,4},{7,5},{8,10},{9,11},{10,... | collective-permute-start | bytes 589832 | tf_op jit(solution)/shard_map/ppermute | solution.py:493
  48.3 7.7 %collective-permute-start.14 = (bf16[256,384]{1,0:T(8,128)(2,1)S(1)}, bf16[256,384]{1,0:T(8,128)(2,1)S(1)}, u32[]{:S(2)}, u32[]{:S(2)}) collective-permute-start(bf16[256,384]{1,0:T(8,128)(2,1)S(1)} %add.19.refs_2_), channel_id=1, source_target_pairs={{0,1},{1,0},{2,3},{3,2},{4,5},{5,4},{6,7},{7,6},{8,9},{9,8},{10,11... | collective-permute-start | bytes 589832 | tf_op jit(solution)/shard_map/ppermute | solution.py:497
  49.9 8.3 %collective-permute-start.10 = (bf16[256,384]{1,0:T(8,128)(2,1)S(1)}, bf16[256,384]{1,0:T(8,128)(2,1)S(1)}, u32[]{:S(2)}, u32[]{:S(2)}) collective-permute-start(bf16[256,384]{1,0:T(8,128)(2,1)S(1)} %get-tuple-element.59), channel_id=1, source_target_pairs={{0,2},{1,3},{2,0},{3,1},{4,6},{5,7},{6,4},{7,5},{8,10},{9,11},{10,... | collective-permute-start | bytes 589832 | tf_op jit(solution)/shard_map/ppermute | solution.py:493
  51.4 6.8 %collective-permute-start.13 = (bf16[256,384]{1,0:T(8,128)(2,1)S(1)}, bf16[256,384]{1,0:T(8,128)(2,1)S(1)}, u32[]{:S(2)}, u32[]{:S(2)}) collective-permute-start(bf16[256,384]{1,0:T(8,128)(2,1)S(1)} %add.20._), channel_id=1, source_target_pairs={{0,1},{1,0},{2,3},{3,2},{4,5},{5,4},{6,7},{7,6},{8,9},{9,8},{10,11... | collective-permute-start | bytes 589832 | tf_op jit(solution)/shard_map/ppermute | solution.py:499
  56.2 13.8 %collective-permute-start.16 = (bf16[128,384]{1,0:T(8,128)(2,1)S(1)}, bf16[128,384]{1,0:T(8,128)(2,1)S(1)}, u32[]{:S(2)}, u32[]{:S(2)}) collective-permute-start(bf16[128,384]{1,0:T(8,128)(2,1)S(1)} %get-tuple-element.60), channel_id=1, source_target_pairs={{0,0},{1,1},{2,2},{3,3},{4,4},{5,5},{6,6},{7,7},{8,16},{9,17},{10,... | collective-permute-start | bytes 294920 | tf_op jit(solution)/shard_map/ppermute | solution.py:508
  56.8 13.1 %collective-permute-start.15 = (bf16[128,384]{1,0:T(8,128)(2,1)S(1)}, bf16[128,384]{1,0:T(8,128)(2,1)S(1)}, u32[]{:S(2)}, u32[]{:S(2)}) collective-permute-start(bf16[128,384]{1,0:T(8,128)(2,1)S(1)} %get-tuple-element.61), channel_id=1, source_target_pairs={{0,4},{1,5},{2,6},{3,7},{4,0},{5,1},{6,2},{7,3},{8,20},{9,21},{10,... | collective-permute-start | bytes 294920 | tf_op jit(solution)/shard_map/ppermute | solution.py:508
  58.4 11.6 %collective-permute-start.17 = (bf16[128,384]{1,0:T(8,128)(2,1)S(1)}, bf16[128,384]{1,0:T(8,128)(2,1)S(1)}, u32[]{:S(2)}, u32[]{:S(2)}) collective-permute-start(bf16[128,384]{1,0:T(8,128)(2,1)S(1)} %get-tuple-element.62), channel_id=1, source_target_pairs={{0,20},{1,21},{2,22},{3,23},{4,16},{5,17},{6,18},{7,19},{8,4},{9,5... | collective-permute-start | bytes 294920 | tf_op jit(solution)/shard_map/ppermute | solution.py:508
  63.5 8.3 %collective-permute-start.18 = (bf16[128,384]{1,0:T(8,128)(2,1)S(1)}, bf16[128,384]{1,0:T(8,128)(2,1)S(1)}, u32[]{:S(2)}, u32[]{:S(2)}) collective-permute-start(bf16[128,384]{1,0:T(8,128)(2,1)S(1)} %get-tuple-element.63), channel_id=1, source_target_pairs={{0,16},{1,17},{2,18},{3,19},{4,20},{5,21},{6,22},{7,23},{8,0},{9,1... | collective-permute-start | bytes 294920 | tf_op jit(solution)/shard_map/ppermute | solution.py:508

commit v4 on v3

--- a/solution.py
+++ b/solution.py
@@ -321,8 +321,13 @@
     )(listed, *map(in_vmem, packed), in_vmem(part), in_vmem(other), cot, other_cot, *extra)
 
 
-def weight_kernel(first, count, listed, toks0, toks1, grads0, grads1, gate_in, up_in, _, gate_out, up_out, token, stage, sems):
+def weight_kernel(first, count, listed, toks0, toks1, grads0, grads1, gate_in, up_in, _, gate_out, up_out, token, stage, sems, zeros, sem):
     token[...] = jnp.zeros_like(token)
+    columns = listed.shape[0]
+    early = columns * 3 // 4
+    final = first + count == columns
+    if final:
+        start_clearing(early, columns - early, listed, zeros, gate_out, up_out, sem)
     kept, slots = kept_of(listed), stage.shape[0]
     for j in range(first, first + count):
         slot = (j - first) % slots
@@ -340,6 +345,8 @@
             pltpu.make_async_copy(here.at[:, BLOCK:], up_out.at[rows, spanning(j)], sems.at[slot]).start()
     for slot in range(slots):
         pltpu.make_async_copy(stage.at[slot], stage.at[slot], sems.at[slot]).wait()
+    if final:
+        finish_clearing(columns - early, gate_out, sem)
 
 
 def weight_grads(first, count, listed, tokens, grads, written, later_than):
@@ -349,7 +356,7 @@
         out_shape=[pltpu.HBM(grad.shape, F32) for grad in written] + [VMEM((8, BLOCK), F32)],
         in_specs=[spec(SMEM)] + [spec(VMEM)] * 4 + [spec(pltpu.HBM)] * 2 + [spec(pl.ANY)],
         out_specs=[spec(pltpu.HBM)] * 2 + [spec(VMEM)],
-        scratch_shapes=[VMEM((slots, kept_of(listed) * BLOCK, 2 * BLOCK), F32), pltpu.SemaphoreType.DMA((slots,))],
+        scratch_shapes=[VMEM((slots, kept_of(listed) * BLOCK, 2 * BLOCK), F32), pltpu.SemaphoreType.DMA((slots,)), *CLEARING],
         input_output_aliases={5: 0, 6: 1},
         compiler_params=pltpu.CompilerParams(vmem_limit_bytes=16 * MIB),
         cost_estimate=SMALL,
@@ -435,14 +442,15 @@
 
 
 def turn_kernel(listed, packed, _, turned, gate_out, up_out, zeros, sem):
-    start_clearing(0, listed.shape[0], listed, zeros, gate_out, up_out, sem)
+    early = listed.shape[0] * 3 // 4
+    start_clearing(0, early, listed, zeros, gate_out, up_out, sem)
 
     def turn(j, _):
         turned[j] = packed[j].T
         return 0
 
     lax.fori_loop(0, packed.shape[0], turn, 0)
-    finish_clearing(listed.shape[0], gate_out, sem)
+    finish_clearing(early, gate_out, sem)
 
 
 def transposed(listed, packed, grad_shape, later_than):

time: 72.9 us -> 72.2 us (level)
  waiting for transfers between devices: 5.83 us -> 4.17 us
  starting transfers between devices: 25.3 us -> 26.7 us
    pallas_call x1, Pallas kernels: 7.01 us -> 5.6 us  [transposed(): pl.pallas_call(turn_kernel, out_shape=[VMEM((columns, wide, rows), BF16)]...]
    pallas_call x3, Pallas kernels: 11.7 us -> 12.8 us  [weight_grads(): pl.pallas_call(functools.partial(weight_kernel, first, count), out_shape=...]
    ppermute x4, waiting for transfers between devices: 1.85 us -> 0.79 us  [homeward(): yield lax.ppermute(here[k0 * BLOCK:(k0 + 1) * BLOCK], AXES, back)]
    ppermute x2, starting transfers between devices: 1.99 us -> 3.02 us  [chip_body(): lax.ppermute(part, 'row', swap)]
  transfers between devices with their start and end apart: 19 -> 19, of which waited for: 5 -> 4; matrix products, arithmetic and copies ran while one was open for 1% -> 1% of each run, Pallas kernels for 51% -> 51%
where the time goes in v4:
time: 72.2 us; the launch traced here: 71.8 us
  Pallas kernels  37 us (51%)
  starting transfers between devices  26.7 us (37%)
  waiting for transfers between devices  4.17 us (6%)
  local copies, waits for them, and re-layouts  2.45 us (3%)
  between operations  0.9 us (1%)
    pallas_call x3, Pallas kernels, weight_grads(): pl.pallas_call(functools.partial(weight_kernel, first, count), out_shape=...  12.8 us
    ppermute x4, starting transfers between devices, homeward(): yield lax.ppermute(here[k0 * BLOCK:(k0 + 1) * BLOCK], AXES, back)  7.35 us
    pallas_call x2, Pallas kernels, backward(): pl.pallas_call(functools.partial(backward_kernel, turn), out_shape=[VMEM(...  6.58 us
    pallas_call x2, Pallas kernels, pack(): pl.pallas_call(functools.partial(pack_kernel, first, turning), out_shape=...  6.23 us
    ppermute x4, starting transfers between devices, chip_body(): lax.ppermute(block, AXES, z_pairs(turn, k0))  6.2 us
    pallas_call x1, Pallas kernels, transposed(): pl.pallas_call(turn_kernel, out_shape=[VMEM((columns, wide, rows), BF16)]...  5.6 us
    pallas_call x2, Pallas kernels, forward(): pl.pallas_call(functools.partial(forward_kernel, turn), out_shape=[VMEM((...  4.97 us
    ppermute x2, starting transfers between devices, chip_body(): lax.ppermute(part, 'row', swap)  3.02 us
  transfers between devices with their start and end apart: 19, of which 4 were waited for; matrix products, arithmetic and copies ran while one was open for 1% of the time, Pallas kernels for 51%

profile of v4, /device:TPU:0, one launch (start us, length us, event | category | flops | bytes accessed | tf_op | source)
XLA Modules:
  0.0 71.8 jit_solution(2592024115141853858)
XLA Ops:
  0.6 0.5 collective-permute-start
  1.1 2.7 %collective-permute-start.1 = (bf16[128,384]{1,0:T(8,128)(2,1)}, bf16[128,384]{1,0:T(8,128)(2,1)S(1)}, u32[]{:S(2)}, u32[]{:S(2)}) collective-permute-start(bf16[128,384]{1,0:T(8,128)(2,1)} %refs_0_.1), channel_id=1, source_target_pairs={{4,0},{5,1},{6,2},{7,3},{0,4},{1,5},{2,6},{3,7},{20,8},{21,9},{22,... | collective-permute-start | bytes 294920 | tf_op jit(solution)/shard_map/ppermute | solution.py:480
  3.8 2.1 %collective-permute-start.3 = (bf16[128,384]{1,0:T(8,128)(2,1)}, bf16[128,384]{1,0:T(8,128)(2,1)S(1)}, u32[]{:S(2)}, u32[]{:S(2)}) collective-permute-start(bf16[128,384]{1,0:T(8,128)(2,1)} %refs_0_.1), channel_id=1, source_target_pairs={{20,0},{21,1},{22,2},{23,3},{16,4},{17,5},{18,6},{19,7},{4,8},{5,9... | collective-permute-start | bytes 294920 | tf_op jit(solution)/shard_map/ppermute | solution.py:480
  5.9 0.0 collective-permute-done.refs_0_._.other_cot
  5.9 0.9 %copy-done.1 = bf16[128,384]{1,0:T(8,128)(2,1)S(1)} copy-done((bf16[128,384]{1,0:T(8,128)(2,1)S(1)}, bf16[128,384]{1,0:T(8,128)(2,1)}, u32[]{:S(2)}) %copy-start.1) | copy-done | bytes 98328
  6.8 0.8 %collective-permute-start.4 = (bf16[128,384]{1,0:T(8,128)(2,1)S(1)}, bf16[128,384]{1,0:T(8,128)(2,1)S(1)}, u32[]{:S(2)}, u32[]{:S(2)}) collective-permute-start(bf16[128,384]{1,0:T(8,128)(2,1)S(1)} %join.3), channel_id=1, source_target_pairs={{16,0},{17,1},{18,2},{19,3},{20,4},{21,5},{22,6},{23,7},{0,8},{1,9... | collective-permute-start | bytes 294920 | tf_op jit(solution)/shard_map/ppermute | solution.py:480
  7.6 0.7 collective-permute-start.2
  8.3 0.0 copy-start.2
  8.3 0.7 copy-done.2
  9.0 0.4 places.1.listed
  9.4 2.6 %pack.2._.refs_0_.packed_a = bf16[4,1536,256]{2,1,0:T(8,128)(2,1)S(1)} custom-call(s32[12,32]{1,0:T(8,128)S(1)} %places.1.listed, bf16[3072,1536]{1,0:T(8,128)(2,1)} %gate_w.3, bf16[3072,1536]{1,0:T(8,128)(2,1)} %up_w.3, bf16[128,1536]{1,0:T(8,128)(2,1)S(1)} %collective-permute-done.refs_0_._.other_cot), custom_call_target="tpu_custom_call" | custom-call | flops 1 | bytes 1 | tf_op jit(solution)/shard_map/pack/pallas_call | solution.py:198
  12.0 0.0 collective-permute-done.1.refs_0_
  12.0 0.0 collective-permute-done.2.refs_1_
  12.1 1.6 %collective-permute-start.5 = (bf16[512,384]{1,0:T(8,128)(2,1)S(1)}, bf16[512,384]{1,0:T(8,128)(2,1)S(1)}, u32[]{:S(2)}, u32[]{:S(2)}) collective-permute-start(bf16[512,384]{1,0:T(8,128)(2,1)S(1)} %join.4.refs_1_.own), channel_id=1, source_target_pairs={{0,1},{1,0},{2,3},{3,2},{4,5},{5,4},{6,7},{7,6},{8,9},{9,8},{10,11... | collective-permute-start | bytes 1179656 | tf_op jit(solution)/shard_map/ppermute | solution.py:484
  13.6 3.6 %pack.3 = (bf16[8,1536,256]{2,1,0:T(8,128)(2,1)S(1)}, bf16[4,256,1536]{2,1,0:T(8,128)(2,1)S(1)}) custom-call(s32[12,32]{1,0:T(8,128)S(1)} %places.1.listed, bf16[3072,1536]{1,0:T(8,128)(2,1)} %gate_w.3, bf16[3072,1536]{1,0:T(8,128)(2,1)} %up_w.3, bf16[4,1536,256]{2,1,0:T(8,128)(2,1)S(1)} %pack.2._.refs_0_.packed_a, bf16[512,384]{1,0:T(8,128)(2,1)S(1)} %join.4.refs_1_.own), custom_call_target="tpu_custom_call" | custom-call | flops 1 | bytes 1 | tf_op jit(solution)/shard_map/pack/pallas_call | solution.py:198
  17.3 2.6 %collective-permute-done.5.near = bf16[512,384]{1,0:T(8,128)(2,1)S(1)} collective-permute-done((bf16[512,384]{1,0:T(8,128)(2,1)S(1)}, bf16[512,384]{1,0:T(8,128)(2,1)S(1)}, u32[]{:S(2)}, u32[]{:S(2)}) %collective-permute-start.5) | collective-permute-done | bytes 393248 | tf_op jit(solution)/shard_map/ppermute | solution.py:484
  19.9 0.1 mix.1
  20.0 1.6 %collective-permute-start.8 = (bf16[512,384]{1,0:T(8,128)(2,1)S(1)}, bf16[512,384]{1,0:T(8,128)(2,1)S(1)}, u32[]{:S(2)}, u32[]{:S(2)}) collective-permute-start(bf16[512,384]{1,0:T(8,128)(2,1)S(1)} %get-tuple-element.36.here), channel_id=1, source_target_pairs={{0,2},{1,3},{2,0},{3,1},{4,6},{5,7},{6,4},{7,5},{8,10},{9,11},{10,... | collective-permute-start | bytes 1179656 | tf_op jit(solution)/shard_map/ppermute | solution.py:487
  21.6 0.5 collective-permute-start.6
  22.1 5.6 %turn.1 = (bf16[8,256,1536]{2,1,0:T(8,128)(2,1)S(1)}, f32[3072,1536]{1,0:T(8,128)}, f32[3072,1536]{1,0:T(8,128)}) custom-call(s32[12,32]{1,0:T(8,128)S(1)} %places.1.listed, bf16[8,1536,256]{2,1,0:T(8,128)(2,1)S(1)} %get-tuple-element.32._.packed.packed_b, bf16[512,384]{1,0:T(8,128)(2,1)S(1)} %get-tuple-element.33._.here), custom_call_target="tpu_custom_call" | custom-call | flops 1 | bytes 1 | tf_op jit(solution)/shard_map/turn/pallas_call | solution.py:458
  27.7 0.1 collective-permute-done.8.there
  27.8 2.5 %forward.3 = (f32[12,128,256]{2,1,0:T(8,128)S(1)}, bf16[24,128,128]{2,1,0:T(8,128)(2,1)S(1)}) custom-call(s32[12,32]{1,0:T(8,128)S(1)} %places.1.listed, bf16[4,1536,256]{2,1,0:T(8,128)(2,1)S(1)} %pack.2._.refs_0_.packed_a, bf16[8,1536,256]{2,1,0:T(8,128)(2,1)S(1)} %get-tuple-element.32._.packed.packed_b, bf16[512,384]{1,0:T(8,128)(2,1)S(1)} %get-tuple-element.36.here, ...), custom_call_target="tpu_custom_call" | custom-call | flops 1 | bytes 1 | tf_op jit(solution)/shard_map/forward/pallas_call | solution.py:253
  30.3 0.0 copy-start
  30.3 1.8 %collective-permute-start.9 = (f32[12,128,256]{2,1,0:T(8,128)S(1)}, f32[12,128,256]{2,1,0:T(8,128)S(1)}, u32[]{:S(2)}, u32[]{:S(2)}) collective-permute-start(f32[12,128,256]{2,1,0:T(8,128)S(1)} %get-tuple-element.37.part), channel_id=1, source_target_pairs={{0,16},{16,0},{1,17},{17,1},{2,18},{18,2},{3,19},{19,3},{4,20},{20... | collective-permute-start | bytes 4718600 | tf_op jit(solution)/shard_map/ppermute | solution.py:494
  32.1 2.5 %forward.2 = (f32[12,128,256]{2,1,0:T(8,128)S(1)}, bf16[24,128,128]{2,1,0:T(8,128)(2,1)S(1)}) custom-call(s32[12,32]{1,0:T(8,128)S(1)} %places.1.listed, bf16[4,1536,256]{2,1,0:T(8,128)(2,1)S(1)} %pack.2._.refs_0_.packed_a, bf16[8,1536,256]{2,1,0:T(8,128)(2,1)S(1)} %get-tuple-element.32._.packed.packed_b, bf16[512,384]{1,0:T(8,128)(2,1)S(1)} %get-tuple-element.33._.here, ...), custom_call_target="tpu_custom_call" | custom-call | flops 1 | bytes 1 | tf_op jit(solution)/shard_map/forward/pallas_call | solution.py:253
  34.6 1.2 %collective-permute-start.7 = (f32[12,128,256]{2,1,0:T(8,128)S(1)}, f32[12,128,256]{2,1,0:T(8,128)S(1)}, u32[]{:S(2)}, u32[]{:S(2)}) collective-permute-start(f32[12,128,256]{2,1,0:T(8,128)S(1)} %get-tuple-element.35.part), channel_id=1, source_target_pairs={{0,16},{16,0},{1,17},{17,1},{2,18},{18,2},{3,19},{19,3},{4,20},{20... | collective-permute-start | bytes 4718600 | tf_op jit(solution)/shard_map/ppermute | solution.py:494
  35.8 3.3 %backward.2 = (bf16[128,1536]{1,0:T(8,128)(2,1)S(1)}, bf16[12,128,256]{2,1,0:T(8,128)(2,1)S(1)}, bf16[512,384]{1,0:T(8,128)(2,1)S(1)}, bf16[512,384]{1,0:T(8,128)(2,1)S(1)}) custom-call(s32[12,32]{1,0:T(8,128)S(1)} %places.1.listed, bf16[4,256,1536]{2,1,0:T(8,128)(2,1)S(1)} %get-tuple-element.31.turned_a, ...), custom_call_target="tpu_custom_call" | custom-call | flops 1 | bytes 1 | tf_op jit(solution)/shard_map/backward/pallas_call | solution.py:311
  39.1 1.6 %collective-permute-start.12 = (bf16[512,384]{1,0:T(8,128)(2,1)S(1)}, bf16[512,384]{1,0:T(8,128)(2,1)S(1)}, u32[]{:S(2)}, u32[]{:S(2)}) collective-permute-start(bf16[512,384]{1,0:T(8,128)(2,1)S(1)} %get-tuple-element.43), channel_id=1, source_target_pairs={{0,2},{1,3},{2,0},{3,1},{4,6},{5,7},{6,4},{7,5},{8,10},{9,11},{10,... | collective-permute-start | bytes 1179656 | tf_op jit(solution)/shard_map/ppermute | solution.py:500
  40.7 3.3 %backward.3 = (bf16[128,1536]{1,0:T(8,128)(2,1)S(1)}, bf16[12,128,256]{2,1,0:T(8,128)(2,1)S(1)}, bf16[512,384]{1,0:T(8,128)(2,1)S(1)}, bf16[512,384]{1,0:T(8,128)(2,1)S(1)}) custom-call(s32[12,32]{1,0:T(8,128)S(1)} %places.1.listed, bf16[4,256,1536]{2,1,0:T(8,128)(2,1)S(1)} %get-tuple-element.31.turned_a, ...), custom_call_target="tpu_custom_call" | custom-call | flops 1 | bytes 1 | tf_op jit(solution)/shard_map/backward/pallas_call | solution.py:311
  44.1 0.6 collective-permute-start.11
  44.6 2.9 %weight_grads.3 = (f32[3072,1536]{1,0:T(8,128)}, f32[3072,1536]{1,0:T(8,128)}, f32[8,128]{1,0:T(8,128)S(1)}) custom-call(s32[12,32]{1,0:T(8,128)S(1)} %places.1.listed, bf16[24,128,128]{2,1,0:T(8,128)(2,1)S(1)} %get-tuple-element.44.toks0, bf16[24,128,128]{2,1,0:T(8,128)(2,1)S(1)} %get-tuple-element.45.toks1, ...), custom_call_target="tpu_custom_call", output_to_operand_aliasing={{0}: (5, {}), {1}: (6, {})} | custom-call | flops 1 | bytes 1 | tf_op jit(solution)/shard_map/weight_grads/pallas_call | solution.py:354
  47.5 0.1 add.19.refs_2_
  47.6 1.6 %collective-permute-start.14 = (bf16[256,384]{1,0:T(8,128)(2,1)S(1)}, bf16[256,384]{1,0:T(8,128)(2,1)S(1)}, u32[]{:S(2)}, u32[]{:S(2)}) collective-permute-start(bf16[256,384]{1,0:T(8,128)(2,1)S(1)} %add.19.refs_2_), channel_id=1, source_target_pairs={{0,1},{1,0},{2,3},{3,2},{4,5},{5,4},{6,7},{7,6},{8,9},{9,8},{10,11... | collective-permute-start | bytes 589832 | tf_op jit(solution)/shard_map/ppermute | solution.py:505
  49.2 1.5 %collective-permute-start.10 = (bf16[256,384]{1,0:T(8,128)(2,1)S(1)}, bf16[256,384]{1,0:T(8,128)(2,1)S(1)}, u32[]{:S(2)}, u32[]{:S(2)}) collective-permute-start(bf16[256,384]{1,0:T(8,128)(2,1)S(1)} %get-tuple-element.59), channel_id=1, source_target_pairs={{0,2},{1,3},{2,0},{3,1},{4,6},{5,7},{6,4},{7,5},{8,10},{9,11},{10,... | collective-permute-start | bytes 589832 | tf_op jit(solution)/shard_map/ppermute | solution.py:501
  50.7 0.1 add.20._
  50.7 0.7 collective-permute-start.13
  51.4 3.2 %weight_grads.4 = (f32[3072,1536]{1,0:T(8,128)}, f32[3072,1536]{1,0:T(8,128)}, f32[8,128]{1,0:T(8,128)S(1)}) custom-call(s32[12,32]{1,0:T(8,128)S(1)} %places.1.listed, bf16[24,128,128]{2,1,0:T(8,128)(2,1)S(1)} %get-tuple-element.44.toks0, bf16[24,128,128]{2,1,0:T(8,128)(2,1)S(1)} %get-tuple-element.45.toks1, ...), custom_call_target="tpu_custom_call", output_to_operand_aliasing={{0}: (5, {}), {1}: (6, {})} | custom-call | flops 1 | bytes 1 | tf_op jit(solution)/shard_map/weight_grads/pallas_call | solution.py:354
  54.6 0.6 collective-permute-done.14.refs_2_
  55.2 0.1 add.21.refs_3_
  55.3 0.7 collective-permute-start.16
  56.0 1.3 %collective-permute-start.15 = (bf16[128,384]{1,0:T(8,128)(2,1)S(1)}, bf16[128,384]{1,0:T(8,128)(2,1)S(1)}, u32[]{:S(2)}, u32[]{:S(2)}) collective-permute-start(bf16[128,384]{1,0:T(8,128)(2,1)S(1)} %get-tuple-element.61), channel_id=1, source_target_pairs={{0,4},{1,5},{2,6},{3,7},{4,0},{5,1},{6,2},{7,3},{8,20},{9,21},{10,... | collective-permute-start | bytes 294920 | tf_op jit(solution)/shard_map/ppermute | solution.py:516
  57.3 0.0 collective-permute-done.13.refs_2_
  57.3 0.1 add.22._
  57.4 5.4 %collective-permute-start.17 = (bf16[128,384]{1,0:T(8,128)(2,1)S(1)}, bf16[128,384]{1,0:T(8,128)(2,1)S(1)}, u32[]{:S(2)}, u32[]{:S(2)}) collective-permute-start(bf16[128,384]{1,0:T(8,128)(2,1)S(1)} %get-tuple-element.62), channel_id=1, source_target_pairs={{0,20},{1,21},{2,22},{3,23},{4,16},{5,17},{6,18},{7,19},{8,4},{9,5... | collective-permute-start | bytes 294920 | tf_op jit(solution)/shard_map/ppermute | solution.py:516
  62.8 0.7 %copy.23 = bf16[128,1536]{1,0:T(8,128)(2,1)} copy(bf16[128,1536]{1,0:T(8,128)(2,1)S(1)} %get-tuple-element.64) | data formatting | bytes 786432
  63.6 6.7 %weight_grads.5 = (f32[3072,1536]{1,0:T(8,128)}, f32[3072,1536]{1,0:T(8,128)}, f32[8,128]{1,0:T(8,128)}) custom-call(s32[12,32]{1,0:T(8,128)S(1)} %places.1.listed, bf16[24,128,128]{2,1,0:T(8,128)(2,1)S(1)} %get-tuple-element.44.toks0, bf16[24,128,128]{2,1,0:T(8,128)(2,1)S(1)} %get-tuple-element.45.toks1, ...), custom_call_target="tpu_custom_call", output_to_operand_aliasing={{0}: (5, {}), {1}: (6, {})} | custom-call | flops 1 | bytes 1 | tf_op jit(solution)/shard_map/weight_grads/pallas_call | solution.py:354
  70.4 0.8 %collective-permute-done.18 = bf16[128,384]{1,0:T(8,128)(2,1)S(1)} collective-permute-done((bf16[128,384]{1,0:T(8,128)(2,1)S(1)}, bf16[128,384]{1,0:T(8,128)(2,1)S(1)}, u32[]{:S(2)}, u32[]{:S(2)}) %collective-permute-start.18) | collective-permute-done | bytes 98336 | tf_op jit(solution)/shard_map/ppermute | solution.py:516
  71.1 0.7 add_convert_fusion
  (21 shorter events, 0.2 us)
Async XLA Ops:
  0.6 5.3 %collective-permute-start = (bf16[128,1536]{1,0:T(8,128)(2,1)}, bf16[128,1536]{1,0:T(8,128)(2,1)S(1)}, u32[]{:S(2)}, u32[]{:S(2)}) collective-permute-start(bf16[128,1536]{1,0:T(8,128)(2,1)} %cot.3), channel_id=1, source_target_pairs={{0,16},{16,0},{1,17},{17,1},{2,18},{18,2},{3,19},{19,3},{4,20},{20... | collective-permute-start | bytes 1179656 | tf_op jit(solution)/shard_map/ppermute | solution.py:476
  1.1 10.8 %collective-permute-start.1 = (bf16[128,384]{1,0:T(8,128)(2,1)}, bf16[128,384]{1,0:T(8,128)(2,1)S(1)}, u32[]{:S(2)}, u32[]{:S(2)}) collective-permute-start(bf16[128,384]{1,0:T(8,128)(2,1)} %refs_0_.1), channel_id=1, source_target_pairs={{4,0},{5,1},{6,2},{7,3},{0,4},{1,5},{2,6},{3,7},{20,8},{21,9},{22,... | collective-permute-start | bytes 294920 | tf_op jit(solution)/shard_map/ppermute | solution.py:480
  3.8 8.2 %collective-permute-start.3 = (bf16[128,384]{1,0:T(8,128)(2,1)}, bf16[128,384]{1,0:T(8,128)(2,1)S(1)}, u32[]{:S(2)}, u32[]{:S(2)}) collective-permute-start(bf16[128,384]{1,0:T(8,128)(2,1)} %refs_0_.1), channel_id=1, source_target_pairs={{20,0},{21,1},{22,2},{23,3},{16,4},{17,5},{18,6},{19,7},{4,8},{5,9... | collective-permute-start | bytes 294920 | tf_op jit(solution)/shard_map/ppermute | solution.py:480
  5.9 0.9 %copy-start.1 = (bf16[128,384]{1,0:T(8,128)(2,1)S(1)}, bf16[128,384]{1,0:T(8,128)(2,1)}, u32[]{:S(2)}) copy-start(bf16[128,384]{1,0:T(8,128)(2,1)} %refs_0_.1) | copy-start | bytes 294916
  6.8 5.2 %collective-permute-start.4 = (bf16[128,384]{1,0:T(8,128)(2,1)S(1)}, bf16[128,384]{1,0:T(8,128)(2,1)S(1)}, u32[]{:S(2)}, u32[]{:S(2)}) collective-permute-start(bf16[128,384]{1,0:T(8,128)(2,1)S(1)} %join.3), channel_id=1, source_target_pairs={{16,0},{17,1},{18,2},{19,3},{20,4},{21,5},{22,6},{23,7},{0,8},{1,9... | collective-permute-start | bytes 294920 | tf_op jit(solution)/shard_map/ppermute | solution.py:480
  7.6 4.4 %collective-permute-start.2 = (bf16[128,384]{1,0:T(8,128)(2,1)S(1)}, bf16[128,384]{1,0:T(8,128)(2,1)S(1)}, u32[]{:S(2)}, u32[]{:S(2)}) collective-permute-start(bf16[128,384]{1,0:T(8,128)(2,1)S(1)} %join.3), channel_id=1, source_target_pairs={{0,0},{1,1},{2,2},{3,3},{4,4},{5,5},{6,6},{7,7},{16,8},{17,9},{18,... | collective-permute-start | bytes 294920 | tf_op jit(solution)/shard_map/ppermute | solution.py:480
  8.3 0.7 copy-start.2
  12.1 7.8 %collective-permute-start.5 = (bf16[512,384]{1,0:T(8,128)(2,1)S(1)}, bf16[512,384]{1,0:T(8,128)(2,1)S(1)}, u32[]{:S(2)}, u32[]{:S(2)}) collective-permute-start(bf16[512,384]{1,0:T(8,128)(2,1)S(1)} %join.4.refs_1_.own), channel_id=1, source_target_pairs={{0,1},{1,0},{2,3},{3,2},{4,5},{5,4},{6,7},{7,6},{8,9},{9,8},{10,11... | collective-permute-start | bytes 1179656 | tf_op jit(solution)/shard_map/ppermute | solution.py:484
  20.0 7.8 %collective-permute-start.8 = (bf16[512,384]{1,0:T(8,128)(2,1)S(1)}, bf16[512,384]{1,0:T(8,128)(2,1)S(1)}, u32[]{:S(2)}, u32[]{:S(2)}) collective-permute-start(bf16[512,384]{1,0:T(8,128)(2,1)S(1)} %get-tuple-element.36.here), channel_id=1, source_target_pairs={{0,2},{1,3},{2,0},{3,1},{4,6},{5,7},{6,4},{7,5},{8,10},{9,11},{10,... | collective-permute-start | bytes 1179656 | tf_op jit(solution)/shard_map/ppermute | solution.py:487
  21.6 10.5 %collective-permute-start.6 = (bf16[512,384]{1,0:T(8,128)(2,1)S(1)}, bf16[512,384]{1,0:T(8,128)(2,1)S(1)}, u32[]{:S(2)}, u32[]{:S(2)}) collective-permute-start(bf16[512,384]{1,0:T(8,128)(2,1)S(1)} %get-tuple-element.33._.here), channel_id=1, source_target_pairs={{0,2},{1,3},{2,0},{3,1},{4,6},{5,7},{6,4},{7,5},{8,10},{9,11},{10,... | collective-permute-start | bytes 1179656 | tf_op jit(solution)/shard_map/ppermute | solution.py:487
  30.3 5.5 %copy-start = (bf16[128,1536]{1,0:T(8,128)(2,1)S(1)}, bf16[128,1536]{1,0:T(8,128)(2,1)}, u32[]{:S(2)}) copy-start(bf16[128,1536]{1,0:T(8,128)(2,1)} %cot.3) | copy-start | bytes 1179652
  30.3 5.5 %collective-permute-start.9 = (f32[12,128,256]{2,1,0:T(8,128)S(1)}, f32[12,128,256]{2,1,0:T(8,128)S(1)}, u32[]{:S(2)}, u32[]{:S(2)}) collective-permute-start(f32[12,128,256]{2,1,0:T(8,128)S(1)} %get-tuple-element.37.part), channel_id=1, source_target_pairs={{0,16},{16,0},{1,17},{17,1},{2,18},{18,2},{3,19},{19,3},{4,20},{20... | collective-permute-start | bytes 4718600 | tf_op jit(solution)/shard_map/ppermute | solution.py:494
  34.6 6.1 %collective-permute-start.7 = (f32[12,128,256]{2,1,0:T(8,128)S(1)}, f32[12,128,256]{2,1,0:T(8,128)S(1)}, u32[]{:S(2)}, u32[]{:S(2)}) collective-permute-start(f32[12,128,256]{2,1,0:T(8,128)S(1)} %get-tuple-element.35.part), channel_id=1, source_target_pairs={{0,16},{16,0},{1,17},{17,1},{2,18},{18,2},{3,19},{19,3},{4,20},{20... | collective-permute-start | bytes 4718600 | tf_op jit(solution)/shard_map/ppermute | solution.py:494
  39.1 8.4 %collective-permute-start.12 = (bf16[512,384]{1,0:T(8,128)(2,1)S(1)}, bf16[512,384]{1,0:T(8,128)(2,1)S(1)}, u32[]{:S(2)}, u32[]{:S(2)}) collective-permute-start(bf16[512,384]{1,0:T(8,128)(2,1)S(1)} %get-tuple-element.43), channel_id=1, source_target_pairs={{0,2},{1,3},{2,0},{3,1},{4,6},{5,7},{6,4},{7,5},{8,10},{9,11},{10,... | collective-permute-start | bytes 1179656 | tf_op jit(solution)/shard_map/ppermute | solution.py:500
  44.1 6.6 %collective-permute-start.11 = (bf16[256,384]{1,0:T(8,128)(2,1)S(1)}, bf16[256,384]{1,0:T(8,128)(2,1)S(1)}, u32[]{:S(2)}, u32[]{:S(2)}) collective-permute-start(bf16[256,384]{1,0:T(8,128)(2,1)S(1)} %get-tuple-element.58), channel_id=1, source_target_pairs={{0,2},{1,3},{2,0},{3,1},{4,6},{5,7},{6,4},{7,5},{8,10},{9,11},{10,... | collective-permute-start | bytes 589832 | tf_op jit(solution)/shard_map/ppermute | solution.py:501
  47.6 7.6 %collective-permute-start.14 = (bf16[256,384]{1,0:T(8,128)(2,1)S(1)}, bf16[256,384]{1,0:T(8,128)(2,1)S(1)}, u32[]{:S(2)}, u32[]{:S(2)}) collective-permute-start(bf16[256,384]{1,0:T(8,128)(2,1)S(1)} %add.19.refs_2_), channel_id=1, source_target_pairs={{0,1},{1,0},{2,3},{3,2},{4,5},{5,4},{6,7},{7,6},{8,9},{9,8},{10,11... | collective-permute-start | bytes 589832 | tf_op jit(solution)/shard_map/ppermute | solution.py:505
  49.2 8.1 %collective-permute-start.10 = (bf16[256,384]{1,0:T(8,128)(2,1)S(1)}, bf16[256,384]{1,0:T(8,128)(2,1)S(1)}, u32[]{:S(2)}, u32[]{:S(2)}) collective-permute-start(bf16[256,384]{1,0:T(8,128)(2,1)S(1)} %get-tuple-element.59), channel_id=1, source_target_pairs={{0,2},{1,3},{2,0},{3,1},{4,6},{5,7},{6,4},{7,5},{8,10},{9,11},{10,... | collective-permute-start | bytes 589832 | tf_op jit(solution)/shard_map/ppermute | solution.py:501
  50.7 6.6 %collective-permute-start.13 = (bf16[256,384]{1,0:T(8,128)(2,1)S(1)}, bf16[256,384]{1,0:T(8,128)(2,1)S(1)}, u32[]{:S(2)}, u32[]{:S(2)}) collective-permute-start(bf16[256,384]{1,0:T(8,128)(2,1)S(1)} %add.20._), channel_id=1, source_target_pairs={{0,1},{1,0},{2,3},{3,2},{4,5},{5,4},{6,7},{7,6},{8,9},{9,8},{10,11... | collective-permute-start | bytes 589832 | tf_op jit(solution)/shard_map/ppermute | solution.py:507
  55.3 15.0 %collective-permute-start.16 = (bf16[128,384]{1,0:T(8,128)(2,1)S(1)}, bf16[128,384]{1,0:T(8,128)(2,1)S(1)}, u32[]{:S(2)}, u32[]{:S(2)}) collective-permute-start(bf16[128,384]{1,0:T(8,128)(2,1)S(1)} %get-tuple-element.60), channel_id=1, source_target_pairs={{0,0},{1,1},{2,2},{3,3},{4,4},{5,5},{6,6},{7,7},{8,16},{9,17},{10,... | collective-permute-start | bytes 294920 | tf_op jit(solution)/shard_map/ppermute | solution.py:516
  56.0 14.3 %collective-permute-start.15 = (bf16[128,384]{1,0:T(8,128)(2,1)S(1)}, bf16[128,384]{1,0:T(8,128)(2,1)S(1)}, u32[]{:S(2)}, u32[]{:S(2)}) collective-permute-start(bf16[128,384]{1,0:T(8,128)(2,1)S(1)} %get-tuple-element.61), channel_id=1, source_target_pairs={{0,4},{1,5},{2,6},{3,7},{4,0},{5,1},{6,2},{7,3},{8,20},{9,21},{10,... | collective-permute-start | bytes 294920 | tf_op jit(solution)/shard_map/ppermute | solution.py:516
  57.4 12.9 %collective-permute-start.17 = (bf16[128,384]{1,0:T(8,128)(2,1)S(1)}, bf16[128,384]{1,0:T(8,128)(2,1)S(1)}, u32[]{:S(2)}, u32[]{:S(2)}) collective-permute-start(bf16[128,384]{1,0:T(8,128)(2,1)S(1)} %get-tuple-element.62), channel_id=1, source_target_pairs={{0,20},{1,21},{2,22},{3,23},{4,16},{5,17},{6,18},{7,19},{8,4},{9,5... | collective-permute-start | bytes 294920 | tf_op jit(solution)/shard_map/ppermute | solution.py:516
  62.8 8.3 %collective-permute-start.18 = (bf16[128,384]{1,0:T(8,128)(2,1)S(1)}, bf16[128,384]{1,0:T(8,128)(2,1)S(1)}, u32[]{:S(2)}, u32[]{:S(2)}) collective-permute-start(bf16[128,384]{1,0:T(8,128)(2,1)S(1)} %get-tuple-element.63), channel_id=1, source_target_pairs={{0,16},{1,17},{2,18},{3,19},{4,20},{5,21},{6,22},{7,23},{8,0},{9,1... | collective-permute-start | bytes 294920 | tf_op jit(solution)/shard_map/ppermute | solution.py:516
